TPU v7x, 32 devices: a whole 2x2x4 slice. The times are simulated.
32 devices in a mesh: row: 4 (over y, x), col: 8 (over z, core).
Axes of the slice: x: 2, y: 2, z: 4, core: 2. Of those that a mesh axis runs over, the one named last changes fastest.
Arguments:
- matrix: float32 [20480, 20480], P('row', 'col'), as said below
Outputs:
- factored: float32 [20480, 20480], P('row', 'col')
Inputs may be any that keep to these rules, and one draw needn't show every extreme that they name: `matrix`: symmetric positive definite in global order, stored in the tile storage of the statement.
All inputs are finite; a program needn't handle non-finite values.
Results may differ from a plain program's by a relative error of at most 0.000053.
Values sent between devices are 32-bit elements; how exact they have to be, the bound alone decides.
No kernel may reach another device: no remote copies, remote signals or barrier semaphores. Data moves between devices by JAX's collectives and lax.ppermute only.
A program may use at most 256 MiB of HBM per device.

v0:
```python
import jax
import jax.numpy as jnp
from jax import lax
from jax.sharding import PartitionSpec as P

TILE = 128


def spread(block, axis, source):
    block = jnp.where(lax.axis_index(axis) == source, block, jnp.zeros_like(block))
    return lax.psum(block, axis)


def product_t(left, right):
    return lax.dot_general(
        left,
        right,
        (((1,), (1,)), ((), ())),
        precision=lax.Precision.HIGHEST,
        preferred_element_type=jnp.float32,
    )


def column_of(work, panel, tile, col_count):
    start = panel // col_count * tile
    return work[:, start : start + tile]


def gathered_columns(rows_panel, tile, row_count, row_tiles, col_global):
    whole = lax.all_gather(rows_panel, "row", axis=0, tiled=True)
    blocks = whole.reshape(row_count * row_tiles, tile, tile)
    tile_index = col_global % row_count * row_tiles + col_global // row_count
    return jnp.take(blocks, tile_index, axis=0).reshape(-1, tile)


def factor_panel(
    strip, panel, tile, row_count, col_count, row_tiles, row_global, col_global, col_here
):
    owner_row = panel % row_count
    local_row = panel // row_count
    corner = strip[local_row * tile : (local_row + 1) * tile]
    corner = spread(corner, "row", owner_row)
    lower = jnp.linalg.cholesky(corner)
    identity = jnp.eye(tile, dtype=lower.dtype)
    inverse = lax.linalg.triangular_solve(lower, identity, left_side=True, lower=True)
    solved = product_t(strip, inverse).reshape(row_tiles, tile, tile)
    below = (row_global > panel)[:, None, None]
    at_panel = (row_global == panel)[:, None, None]
    trail = jnp.where(below, solved, 0.0)
    written = jnp.where(at_panel, lower[None], trail).reshape(-1, tile)
    trail = trail.reshape(-1, tile)
    rows_panel = spread(trail, "col", panel % col_count)
    cols_panel = gathered_columns(rows_panel, tile, row_count, row_tiles, col_global)
    return (written, rows_panel, cols_panel)


def finish_panel(
    work, panel, written, tile, row_count, col_count, col_tiles, row_here, col_here, col_global
):
    start = panel // col_count * tile
    block = work[:, start : start + tile]
    work = work.at[:, start : start + tile].set(
        jnp.where(col_here == panel % col_count, written, block)
    )
    row_start = panel // row_count * tile
    band = work[row_start : row_start + tile].reshape(tile, col_tiles, tile)
    keep = jnp.logical_or(row_here != panel % row_count, col_global <= panel)[None, :, None]
    band = jnp.where(keep, band, 0.0).reshape(tile, -1)
    return work.at[row_start : row_start + tile].set(band)


def per_device(matrix):
    tile = TILE
    row_count = lax.axis_size("row")
    col_count = lax.axis_size("col")
    row_here = lax.axis_index("row")
    col_here = lax.axis_index("col")
    row_tiles = matrix.shape[0] // tile
    col_tiles = matrix.shape[1] // tile
    row_global = jnp.arange(row_tiles, dtype=jnp.int32) * row_count + row_here
    col_global = jnp.arange(col_tiles, dtype=jnp.int32) * col_count + col_here
    shared = (tile, row_count, col_count, row_tiles, row_global, col_global, col_here)
    work = matrix
    written_one, rows_one, cols_one = factor_panel(column_of(work, 0, tile, col_count), 0, *shared)
    work = work - product_t(rows_one, cols_one)
    work = finish_panel(
        work, 0, written_one, tile, row_count, col_count, col_tiles, row_here, col_here, col_global
    )
    written_two, rows_two, cols_two = factor_panel(column_of(work, 1, tile, col_count), 1, *shared)
    work = work - product_t(rows_two, cols_two)
    work = finish_panel(
        work, 1, written_two, tile, row_count, col_count, col_tiles, row_here, col_here, col_global
    )
    return work


def solution(mesh):
    in_specs = (P("row", "col"),)
    out_specs = P("row", "col")
    return jax.shard_map(
        per_device, mesh=mesh, in_specs=in_specs, out_specs=out_specs, check_vma=False
    )
```

profile of v0, /device:TPU:25, one launch (start us, length us, event | category | flops | bytes accessed | tf_op | source)
XLA Modules:
  0.0 772.2 jit_solution(7698082486698921255)
XLA Ops:
  6.5 52.0 %copy.15 = f32[5120,2560]{0,1:T(8,128)} copy(f32[5120,2560]{1,0:T(8,128)} %param.14) | data formatting | bytes 104857600 | tf_op args[0]
  58.6 1.5 slice_select_fusion.3
  60.2 42.1 %all-reduce.5.cloned.1.call-done = f32[128,128]{0,1:T(8,128)} async-done(((f32[128,128]{0,1:T(8,128)}), f32[128,128]{0,1:T(8,128)}) %all-reduce.5.cloned.1.call-update) | async-done | bytes 65552 | tf_op jit(solution)/shard_map/psum | solution.py:11
  102.3 0.9 copy.13
  104.1 11.7 %cholesky.44 = f32[128,128]{1,0:T(8,128)S(1)} custom-call(f32[128,128]{1,0:T(8,128)S(1)} %fusion.13), custom_call_target="Cholesky" | custom-call | tf_op jit(solution)/shard_map/jit(cholesky)/cholesky | solution.py:43
  117.0 9.8 %custom-call.6 = f32[1,128,128]{1,2,0:T(8,128)S(1)} custom-call(f32[1,128,128]{2,1,0:T(8,128)S(1)} %get-tuple-element.60), custom_call_target="InvertDiagBlocksLowerTriangular" | custom-call | tf_op jit(solution)/shard_map/triangular_solve/custom-call.0 | solution.py:45
  127.1 6.5 broadcast_select_fusion.1
  133.7 67.5 %all-reduce.7.cloned.1.call-done = f32[5120,128]{0,1:T(8,128)} async-done(((f32[5120,128]{0,1:T(8,128)}), f32[5120,128]{0,1:T(8,128)}) %all-reduce.7.cloned.1.call-update) | async-done | bytes 2621456 | tf_op jit(solution)/shard_map/psum | solution.py:11
  202.5 107.0 %all-gather.3.cloned.1.call-done = f32[20480,128]{0,1:T(8,128)} async-done(((f32[5120,128]{0,1:T(8,128)}), f32[20480,128]{0,1:T(8,128)}) %all-gather.3.cloned.1.call-update) | async-done | bytes 10485776 | tf_op jit(solution)/shard_map/all_gather | solution.py:30
  309.5 11.7 %copy.27 = f32[20480,128]{1,0:T(8,128)} copy(f32[20480,128]{0,1:T(8,128)} %all-gather.3.cloned.1.call-done) | data formatting | bytes 20971520 | tf_op jit(solution)/shard_map/reshape | solution.py:31
  321.2 5.8 gather_fusion
  327.1 1.5 broadcast_select_fusion.3
  328.6 48.5 %convolution_subtract_fusion.1 = f32[5120,2560]{0,1:T(8,128)} fusion(f32[5120,2560]{0,1:T(8,128)} %copy.15, f32[5120,128]{0,1:T(8,128)S(1)} %copy-done, f32[2560,128]{1,0:T(8,128)S(1)} %bitcast.61), kind=kOutput, calls=%fused_computation.3 | convolution fusion | flops 20145766400 | bytes 108789760 | tf_op jit(solution)/shard_map/dot_general | solution.py:15
  377.3 1.6 copy-done.2
  378.8 4.8 fusion.1
  383.6 3.2 constant_dynamic-update-slice_fusion
  387.9 41.0 %all-reduce.9.cloned.1.call-done = f32[128,128]{0,1:T(8,128)} async-done(((f32[128,128]{0,1:T(8,128)}), f32[128,128]{0,1:T(8,128)}) %all-reduce.9.cloned.1.call-update) | async-done | bytes 65552 | tf_op jit(solution)/shard_map/psum | solution.py:11
  428.8 0.9 copy.18
  429.8 0.9 fusion.11
  430.6 11.7 %cholesky.55 = f32[128,128]{1,0:T(8,128)S(1)} custom-call(f32[128,128]{1,0:T(8,128)S(1)} %fusion.11), custom_call_target="Cholesky" | custom-call | tf_op jit(solution)/shard_map/jit(cholesky)/cholesky | solution.py:43
  443.6 9.8 %custom-call.7 = f32[1,128,128]{1,2,0:T(8,128)S(1)} custom-call(f32[1,128,128]{2,1,0:T(8,128)S(1)} %get-tuple-element.56), custom_call_target="InvertDiagBlocksLowerTriangular" | custom-call | tf_op jit(solution)/shard_map/triangular_solve/custom-call.0 | solution.py:45
  453.7 6.6 broadcast_select_fusion
  460.6 67.2 %all-reduce.11.cloned.1.call-done = f32[5120,128]{0,1:T(8,128)} async-done(((f32[5120,128]{0,1:T(8,128)}), f32[5120,128]{0,1:T(8,128)}) %all-reduce.11.cloned.1.call-update) | async-done | bytes 2621456 | tf_op jit(solution)/shard_map/psum | solution.py:11
  528.2 107.7 %all-gather.5.cloned.1.call-done = f32[20480,128]{0,1:T(8,128)} async-done(((f32[5120,128]{0,1:T(8,128)}), f32[20480,128]{0,1:T(8,128)}) %all-gather.5.cloned.1.call-update) | async-done | bytes 10485776 | tf_op jit(solution)/shard_map/all_gather | solution.py:30
  635.9 11.8 %copy.28 = f32[20480,128]{1,0:T(8,128)} copy(f32[20480,128]{0,1:T(8,128)} %all-gather.5.cloned.1.call-done) | data formatting | bytes 20971520 | tf_op jit(solution)/shard_map/reshape | solution.py:31
  647.6 5.8 gather_fusion.1
  653.5 1.5 broadcast_select_fusion.2
  654.9 48.6 %convolution_subtract_fusion = f32[5120,2560]{0,1:T(8,128)} fusion(f32[5120,2560]{0,1:T(8,128)} %get-tuple-element.58, f32[5120,128]{0,1:T(8,128)S(1)} %copy-done.1, f32[2560,128]{1,0:T(8,128)S(1)} %bitcast.60), kind=kOutput, calls=%fused_computation.2 | convolution fusion | flops 20145766400 | bytes 108789760 | tf_op jit(solution)/shard_map/dot_general | solution.py:15
  703.7 1.6 copy-done.3
  705.3 4.8 fusion.2
  710.1 3.3 fusion.5
  713.4 52.0 %copy.23 = f32[5120,2560]{1,0:T(8,128)} copy(f32[5120,2560]{0,1:T(8,128)} %fusion.5) | data formatting | bytes 104857600 | tf_op jit(solution)/shard_map/scatter | solution.py:69
  (48 shorter events, 7.2 us)
Async XLA Ops:
  6.5 95.7 %all-reduce.5.cloned.1.call-start = ((), (), s32[]{:S(2)}) async-start(), calls=%async_computation | async-start | bytes 131072 | tf_op jit(solution)/shard_map/psum | solution.py:11
  60.1 141.2 %all-reduce.7.cloned.1.call-start = ((), (), s32[]{:S(2)}) async-start(), calls=%async_computation.1 | async-start | bytes 5242880 | tf_op jit(solution)/shard_map/psum | solution.py:11
  133.7 175.8 %all-gather.3.cloned.1.call-start = ((), (), s32[]{:S(2)}) async-start(), calls=%async_computation.2 | async-start | bytes 13107200 | tf_op jit(solution)/shard_map/all_gather | solution.py:30
  201.2 227.6 %all-reduce.9.cloned.1.call-start = ((), (), s32[]{:S(2)}) async-start(), calls=%async_computation.3 | async-start | bytes 131072 | tf_op jit(solution)/shard_map/psum | solution.py:11
  321.2 7.3 copy-start
  377.1 1.7 copy-start.2
  387.5 140.3 %all-reduce.11.cloned.1.call-start = ((), (), s32[]{:S(2)}) async-start(), calls=%async_computation.4 | async-start | bytes 5242880 | tf_op jit(solution)/shard_map/psum | solution.py:11
  460.3 175.5 %all-gather.5.cloned.1.call-start = ((), (), s32[]{:S(2)}) async-start(), calls=%async_computation.5 | async-start | bytes 13107200 | tf_op jit(solution)/shard_map/all_gather | solution.py:30
  647.6 7.3 copy-start.1
  703.5 1.7 copy-start.3
Sparse Core Ops, SparseCore 0:
  60.2 42.0 all-reduce.4
  133.8 67.3 all-reduce.6
  203.2 106.2 all-gather.2
  387.6 41.1 all-reduce.8
  460.5 67.3 all-reduce.10
  529.6 106.2 all-gather.4
where the time goes:
time: 777 us; the launch traced here: 772 us
  waiting for transfers between devices  433 us (56%)
  local copies, waits for them, and re-layouts  145 us (19%)
  matrix products  111 us (14%)
  other arithmetic  69.1 us (9%)
  between operations  13.7 us (2%)
    psum x4, waiting for transfers between devices, spread(): return lax.psum(block, axis)  218 us
    all_gather x2, waiting for transfers between devices, gathered_columns(): whole = lax.all_gather(rows_panel, 'row', axis=0, tiled=True)  215 us
    dot_general x4, matrix products, product_t(): lax.dot_general(left, right, (((1,), (1,)), ((), ())), precision=lax.Prec...  110 us
    unnamed x9, local copies, waits for them, and re-layouts  55.2 us
    scatter x1, local copies, waits for them, and re-layouts, finish_panel(): return work.at[row_start:row_start + tile].set(band)  52 us
    another operation x6, other arithmetic, factor_panel(): lower = jnp.linalg.cholesky(corner)  24.8 us
    reshape x2, local copies, waits for them, and re-layouts, gathered_columns(): blocks = whole.reshape(row_count * row_tiles, tile, tile)  23.5 us
    another operation x4, other arithmetic, factor_panel(): lax.linalg.triangular_solve(lower, identity, left_side=True, lower=True)  20.8 us
  transfers between devices with their start and end apart: 6, of which 6 were waited for; matrix products, arithmetic and copies ran while one was open for 0% of the time, Pallas kernels for 0%

commit v1 on v0

v1 whole, which is shorter than its diff:
```python
import functools

import jax
import jax.numpy as jnp
from jax import lax
from jax.experimental import pallas as pl
from jax.experimental.pallas import tpu as pltpu
from jax.sharding import PartitionSpec as P

TILE = 128
PANELS = 2
WIDE = PANELS * TILE
CORES = 2
VMEM_LIMIT = 40 * 1024 * 1024
GROUP = 8


def dot_full(left, right, dims=((1,), (0,))):
    return lax.dot_general(
        left,
        right,
        (dims, ((), ())),
        precision=lax.Precision.HIGHEST,
        preferred_element_type=jnp.float32,
    )


def dot_half(left, right):
    return lax.dot_general(
        left, right, (((1,), (0,)), ((), ())), preferred_element_type=jnp.float32
    )


def split_half(value):
    high = value.astype(jnp.bfloat16)
    low = (value - high.astype(jnp.float32)).astype(jnp.bfloat16)
    return high, low


def factor_tile(square):
    groups = TILE // GROUP
    lane = lax.broadcasted_iota(jnp.int32, (GROUP, TILE), 1)
    sub = lax.broadcasted_iota(jnp.int32, (GROUP, TILE), 0)
    sub_col = lax.broadcasted_iota(jnp.int32, (GROUP, 1), 0)
    left = [square[g * GROUP : (g + 1) * GROUP] for g in range(groups)]
    right = [jnp.where(lane == sub + g * GROUP, 1.0, 0.0) for g in range(groups)]
    for step in range(TILE):
        group, place = divmod(step, GROUP)
        row_left = left[group][place : place + 1]
        row_right = right[group][place : place + 1]
        inverse = 1.0 / row_left[:, step : step + 1]
        row_left = row_left * inverse
        row_right = row_right * inverse
        for other in range(group, groups):
            column = left[other][:, step : step + 1]
            if other == group:
                column = jnp.where(sub_col > place, column, 0.0)
            left[other] = left[other] - column * row_left
            right[other] = right[other] - column * row_right
    upper, inverse = [], []
    for g in range(groups):
        row = sub + g * GROUP
        pivot = jnp.sum(jnp.where(lane == row, left[g], 0.0), axis=1, keepdims=True)
        scale = 1.0 / jnp.sqrt(pivot)
        upper.append(jnp.where(lane >= row, left[g] * scale, 0.0))
        inverse.append(right[g] * scale)
    return jnp.concatenate(upper, axis=0), jnp.concatenate(inverse, axis=0)


def corner_kernel(corner_ref, low_ref, inv_ref, inv_t_ref):
    zero = jnp.zeros((TILE, TILE), jnp.float32)
    upper_0, inv_0 = factor_tile(corner_ref[:TILE, :TILE])
    low_10 = dot_full(corner_ref[TILE:, :TILE], inv_0, ((1,), (1,)))
    square = corner_ref[TILE:, TILE:] - dot_full(low_10, low_10, ((1,), (1,)))
    upper_1, inv_1 = factor_tile(square)
    inv_10 = -dot_full(inv_1, dot_full(low_10, inv_0))
    low_ref[:TILE, :TILE] = upper_0.T
    low_ref[:TILE, TILE:] = zero
    low_ref[TILE:, :TILE] = low_10
    low_ref[TILE:, TILE:] = upper_1.T
    inv_ref[:TILE, :TILE] = inv_0
    inv_ref[:TILE, TILE:] = zero
    inv_ref[TILE:, :TILE] = inv_10
    inv_ref[TILE:, TILE:] = inv_1
    inv_t_ref[:TILE, :TILE] = inv_0.T
    inv_t_ref[:TILE, TILE:] = inv_10.T
    inv_t_ref[TILE:, :TILE] = zero
    inv_t_ref[TILE:, TILE:] = inv_1.T


def factor_corner(corner):
    shape = jax.ShapeDtypeStruct((WIDE, WIDE), jnp.float32)
    return pl.pallas_call(
        corner_kernel,
        out_shape=(shape, shape, shape),
        compiler_params=pltpu.CompilerParams(vmem_limit_bytes=VMEM_LIMIT),
        cost_estimate=pl.CostEstimate(flops=40_000_000, bytes_accessed=1 << 20, transcendentals=0),
    )(corner)


def columns_kernel(info_ref, inv_ref, *refs):
    parts = len(refs) // 2 - 1
    high_ref, low_ref = refs[-2:]
    odd = info_ref[0] % 2 == 1
    start = 0
    for part in range(parts):
        mine, other = refs[2 * part][...], refs[2 * part + 1][...]
        first = jnp.where(odd, other, mine)
        second = jnp.where(odd, mine, other)
        raw = jnp.concatenate([first, second], axis=0)
        size = raw.shape[1]
        high, low = split_half(dot_full(inv_ref[...], raw))
        high_ref[:, start : start + size] = high
        low_ref[:, start : start + size] = low
        start += size


def solve_columns(info, inverse, pairs):
    flat = [array for pair in pairs for array in pair]
    total = sum(pair[0].shape[1] for pair in pairs)
    shape = jax.ShapeDtypeStruct((WIDE, total), jnp.bfloat16)
    vmem = pl.BlockSpec(memory_space=pltpu.VMEM)
    return pl.pallas_call(
        columns_kernel,
        in_specs=[pl.BlockSpec(memory_space=pltpu.SMEM)] + [vmem] * (1 + len(flat)),
        out_specs=(vmem, vmem),
        out_shape=(shape, shape),
        compiler_params=pltpu.CompilerParams(vmem_limit_bytes=VMEM_LIMIT),
        cost_estimate=pl.CostEstimate(
            flops=12 * WIDE * WIDE * total, bytes_accessed=WIDE * total * 8, transcendentals=0
        ),
    )(info, inverse, *flat)


def update_kernel(chunk, depth, info_ref, mat_ref, high_ref, low_ref, lower_ref, inv_t_ref, *refs):
    mine_refs, other_refs = refs[:depth], refs[depth : 2 * depth]
    out_ref, raw, panel_high, panel_low, panel, sems = refs[-6:]
    row, place, core, col = info_ref[0], info_ref[1], info_ref[2], info_ref[3]
    step = pl.program_id(0)

    @pl.when(step == 0)
    def _():
        for source in range(depth):

            @pl.when(place == source)
            def _():
                mine_at = pl.ds(pl.multiple_of(core * TILE, TILE), TILE)
                other_at = pl.ds(pl.multiple_of((1 - core) * TILE, TILE), TILE)
                first = pltpu.make_async_copy(mine_refs[source], raw.at[:, mine_at], sems.at[0])
                second = pltpu.make_async_copy(other_refs[source], raw.at[:, other_at], sems.at[1])
                first.start()
                second.start()
                first.wait()
                second.wait()

        solved = dot_full(raw[...], inv_t_ref[...])
        if chunk == 0:
            head = jnp.where(row == 1, lower_ref[TILE:], solved[:TILE])
            head = jnp.where(row == 0, lower_ref[:TILE], head)
            solved = jnp.concatenate([head, solved[TILE:]], axis=0)
        high, low = split_half(solved)
        panel_high[...] = high
        panel_low[...] = low
        panel[...] = jnp.where(col == 1, solved[:, TILE:], solved[:, :TILE])

    high, low = panel_high[...], panel_low[...]
    right = high_ref[...]
    product = dot_half(high, right) + dot_half(low, right) + dot_half(high, low_ref[...])
    out_ref[...] = mat_ref[...] - product
    if chunk == 0:

        @pl.when(row < PANELS)
        def _():
            out_ref[:TILE, :] = jnp.zeros((TILE, out_ref.shape[1]), jnp.float32)

    @pl.when(jnp.logical_and(step == 0, col < PANELS))
    def _():
        out_ref[:, :TILE] = panel[...]


def update_chunk(chunk, rows, info, matrix, high, low, lower, inv_t, mine, other, out):
    depth = len(mine)
    columns = matrix.shape[1]
    block = next(b for b in (512, 640, 256, TILE) if columns % b == 0)
    any_spec = pl.BlockSpec(memory_space=pl.ANY)
    vmem = pl.BlockSpec(memory_space=pltpu.VMEM)
    window = pl.BlockSpec((rows, block), lambda j: (chunk, j))
    across = pl.BlockSpec((WIDE, block), lambda j: (0, j))
    in_specs = [pl.BlockSpec(memory_space=pltpu.SMEM), window, across, across, vmem, vmem]
    in_specs += [any_spec] * (2 * depth)
    operands = [info, matrix, high, low, lower, inv_t, *mine, *other]
    aliases = {}
    if out is not None:
        aliases = {len(operands): 0}
        in_specs.append(any_spec)
        operands.append(out)
    return pl.pallas_call(
        functools.partial(update_kernel, chunk, depth),
        grid=(columns // block,),
        in_specs=in_specs,
        out_specs=window,
        out_shape=jax.ShapeDtypeStruct(matrix.shape, jnp.float32),
        scratch_shapes=[
            pltpu.VMEM((rows, WIDE), jnp.float32),
            pltpu.VMEM((rows, WIDE), jnp.bfloat16),
            pltpu.VMEM((rows, WIDE), jnp.bfloat16),
            pltpu.VMEM((rows, TILE), jnp.float32),
            pltpu.SemaphoreType.DMA((2,)),
        ],
        input_output_aliases=aliases,
        compiler_params=pltpu.CompilerParams(vmem_limit_bytes=VMEM_LIMIT),
        cost_estimate=pl.CostEstimate(
            flops=6 * rows * columns * WIDE,
            bytes_accessed=8 * rows * columns,
            transcendentals=0,
        ),
    )(*operands)


def swap_pairs(count):
    return [(i, i ^ 1) for i in range(count)]


def share_corner(matrix, row, place, core, row_count, col_count):
    depth = col_count // CORES
    tile = matrix[:TILE, :TILE]
    beside = lax.ppermute(tile, "col", [(0, 1), (1, 0)])
    strip = jnp.concatenate(
        [jnp.where(core == 0, tile, beside), jnp.where(core == 0, beside, tile)], axis=1
    )
    got = [strip]
    for shift in range(1, row_count):
        pairs = [(p, (p + shift) % row_count) for p in range(PANELS)]
        got.append(lax.ppermute(strip, "row", pairs))
    strips = []
    for panel in range(PANELS):
        chosen = got[0]
        for shift in range(1, row_count):
            chosen = jnp.where((row - panel) % row_count == shift, got[shift], chosen)
        strips.append(chosen)
    square = jnp.concatenate(strips, axis=0)
    corner = square
    for shift in range(1, depth):
        pairs = [(c, c + CORES * shift) for c in range(CORES)]
        corner = jnp.where(place == shift, lax.ppermute(square, "col", pairs), corner)
    return corner


def share_rows(block, row, row_count):
    stride = PANELS
    while stride < row_count:
        pairs = [(i, i + stride) for i in range(min(stride, row_count - stride))]
        got = lax.ppermute(block, "row", pairs)
        block = jnp.where(jnp.logical_and(row >= stride, row < 2 * stride), got, block)
        stride *= 2
    return block, lax.ppermute(block, "row", swap_pairs(row_count))


def per_device(matrix):
    row_count = lax.axis_size("row")
    col_count = lax.axis_size("col")
    row = lax.axis_index("row")
    col = lax.axis_index("col")
    depth = col_count // CORES
    place, core = col // CORES, col % CORES
    info = jnp.stack([row, place, core, col]).astype(jnp.int32)
    row_tiles = matrix.shape[0] // TILE
    chunk_tiles = next(t for t in (5, 4, 2, 1) if row_tiles % t == 0 and row_tiles // t >= 5)
    rows = chunk_tiles * TILE
    chunks = row_tiles // chunk_tiles

    corner = share_corner(matrix, row, place, core, row_count, col_count)
    lower, inverse, inv_t = factor_corner(corner)

    half = matrix.shape[1] // 2
    pairs = [
        share_rows(matrix[:TILE, :half], row, row_count),
        share_rows(matrix[:TILE, half:], row, row_count),
    ]
    high, low = solve_columns(info, inverse, pairs)

    slots = chunks + depth - 1
    mine, other = [], []
    got = None
    for slot in range(slots):
        if slot < chunks:
            own = matrix[slot * rows : (slot + 1) * rows, :TILE]
            block = own if got is None else jnp.where(place == 0, own, got)
        else:
            block = got
        busy = [c for c in range(col_count) if 0 <= slot - c // CORES < chunks]
        mine.append(block)
        other.append(lax.ppermute(block, "col", [(c, c ^ 1) for c in busy]))
        hops = [(c, c + CORES) for c in busy if c + CORES < col_count]
        if hops:
            got = lax.ppermute(block, "col", hops)

    out = None
    for chunk in range(chunks):
        out = update_chunk(
            chunk,
            rows,
            info,
            matrix,
            high,
            low,
            lower,
            inv_t,
            mine[chunk : chunk + depth],
            other[chunk : chunk + depth],
            out,
        )
    return out


def solution(mesh):
    return jax.shard_map(
        per_device,
        mesh=mesh,
        in_specs=(P("row", "col"),),
        out_specs=P("row", "col"),
        check_vma=False,
    )
```

time: 777 us -> 206 us (0.27)
  the two profiles are of different devices: /device:TPU:25 before, /device:TPU:0 now
where the time goes in v1:
time: 206 us; the launch traced here: 204 us
  Pallas kernels  101 us (49%)
  starting transfers between devices  61.2 us (30%)
  waiting for transfers between devices  27.1 us (13%)
  other arithmetic  10.7 us (5%)
  local copies, waits for them, and re-layouts  2.97 us (1%)
    pallas_call x8, Pallas kernels, update_chunk(): pl.pallas_call(functools.partial(update_kernel, chunk, depth), grid=(colu...  75.7 us
    ppermute x10, starting transfers between devices, per_device(): got = lax.ppermute(block, 'col', hops)  26.9 us
    ppermute x10, waiting for transfers between devices, per_device(): got = lax.ppermute(block, 'col', hops)  25.2 us
    pallas_call x1, Pallas kernels, factor_corner(): pl.pallas_call(corner_kernel, out_shape=(shape, shape, shape), compiler_p...  22.5 us
    ppermute x11, starting transfers between devices, per_device(): other.append(lax.ppermute(block, 'col', [(c, c ^ 1) for c in busy]))  9.86 us
    ppermute x3, starting transfers between devices, share_corner(): got.append(lax.ppermute(strip, 'row', pairs))  8.13 us
    ppermute x2, starting transfers between devices, share_rows(): got = lax.ppermute(block, 'row', pairs)  7.89 us
    select_n x7, other arithmetic, per_device(): block = own if got is None else jnp.where(place == 0, own, got)  7.09 us
  transfers between devices with their start and end apart: 32, of which 5 were waited for; matrix products, arithmetic and copies ran while one was open for 6% of the time, Pallas kernels for 45%

profile of v1, /device:TPU:0, one launch (start us, length us, event | category | flops | bytes accessed | tf_op | source)
XLA Modules:
  0.0 204.0 jit_solution(963930105216323797)
XLA Ops:
  1.0 4.9 %collective-permute-start.11 = (f32[640,128]{1,0:T(8,128)S(1)}, f32[640,128]{1,0:T(8,128)S(1)}, u32[]{:S(2)}, u32[]{:S(2)}) collective-permute-start(f32[640,128]{1,0:T(8,128)S(1)} %slice.43.refs_0_), channel_id=1, source_target_pairs={{0,2},{1,3},{8,10},{9,11},{16,18},{17,19},{24,26},{25,27}} | collective-permute-start | bytes 983048 | tf_op jit(solution)/shard_map/ppermute | solution.py:296
  6.0 6.9 %collective-permute-done.11 = f32[640,128]{1,0:T(8,128)S(1)} collective-permute-done((f32[640,128]{1,0:T(8,128)S(1)}, f32[640,128]{1,0:T(8,128)S(1)}, u32[]{:S(2)}, u32[]{:S(2)}) %collective-permute-start.11) | collective-permute-done | bytes 327712 | tf_op jit(solution)/shard_map/ppermute | solution.py:296
  13.9 4.4 %collective-permute-start.12 = (f32[640,128]{1,0:T(8,128)S(1)}, f32[640,128]{1,0:T(8,128)S(1)}, u32[]{:S(2)}, u32[]{:S(2)}) collective-permute-start(f32[640,128]{1,0:T(8,128)S(1)} %slice_select_fusion.refs_1_.refs_0_), channel_id=1, source_target_pairs={{0,2},{1,3},{2,4},{3,5},{8,10},{9,11},{10,12},{11,13},{16,18},{17,... | collective-permute-start | bytes 983048 | tf_op jit(solution)/shard_map/ppermute | solution.py:296
  19.2 1.9 collective-permute-start
  22.2 3.5 %collective-permute-start.9 = (f32[128,1280]{1,0:T(8,128)S(1)}, f32[128,1280]{1,0:T(8,128)S(1)}, u32[]{:S(2)}, u32[]{:S(2)}) collective-permute-start(f32[128,1280]{1,0:T(8,128)S(1)} %slice.35), channel_id=1, source_target_pairs={{0,16},{8,24},{1,17},{9,25},{2,18},{10,26},{3,19},{11,27},{4,20},{... | collective-permute-start | bytes 1966088 | tf_op jit(solution)/shard_map/ppermute | solution.py:253
  26.8 3.0 %collective-permute-start.13 = (f32[640,128]{1,0:T(8,128)S(1)}, f32[640,128]{1,0:T(8,128)S(1)}, u32[]{:S(2)}, u32[]{:S(2)}) collective-permute-start(f32[640,128]{1,0:T(8,128)S(1)} %slice_select_fusion.1.refs_2_.refs_1_.refs_0_), channel_id=1, source_target_pairs={{0,2},{1,3},{2,4},{3,5},{4,6},{5,7},{8,10},{9,11},{10,12},{11,13},... | collective-permute-start | bytes 983048 | tf_op jit(solution)/shard_map/ppermute | solution.py:296
  30.7 4.4 %collective-permute-start.1 = (f32[128,256]{1,0:T(8,128)S(1)}, f32[128,256]{1,0:T(8,128)S(1)}, u32[]{:S(2)}, u32[]{:S(2)}) collective-permute-start(f32[128,256]{1,0:T(8,128)S(1)} %pad_maximum_fusion.1), channel_id=1, source_target_pairs={{0,24},{8,0},{1,25},{9,1},{2,26},{10,2},{3,27},{11,3},{4,28},{12,4... | collective-permute-start | bytes 393224 | tf_op jit(solution)/shard_map/ppermute | solution.py:234
  36.3 2.5 %collective-permute-start.3 = (f32[128,256]{1,0:T(8,128)S(1)}, f32[128,256]{1,0:T(8,128)S(1)}, u32[]{:S(2)}, u32[]{:S(2)}) collective-permute-start(f32[128,256]{1,0:T(8,128)S(1)} %pad_maximum_fusion.1), channel_id=1, source_target_pairs={{0,8},{8,16},{1,9},{9,17},{2,10},{10,18},{3,11},{11,19},{4,12},{12... | collective-permute-start | bytes 393224 | tf_op jit(solution)/shard_map/ppermute | solution.py:234
  39.9 2.2 %collective-permute-start.14 = (f32[640,128]{1,0:T(8,128)S(1)}, f32[640,128]{1,0:T(8,128)S(1)}, u32[]{:S(2)}, u32[]{:S(2)}) collective-permute-start(f32[640,128]{1,0:T(8,128)S(1)} %slice_select_fusion.2.refs_3_.refs_2_.refs_1_.refs_0_), channel_id=1, source_target_pairs={{0,2},{1,3},{2,4},{3,5},{4,6},{5,7},{8,10},{9,11},{10,12},{11,13},... | collective-permute-start | bytes 983048 | tf_op jit(solution)/shard_map/ppermute | solution.py:296
  42.1 1.4 collective-permute-done.9
  43.5 1.4 broadcast_select_fusion
  44.9 4.4 %collective-permute-start.7 = (f32[128,1280]{1,0:T(8,128)S(1)}, f32[128,1280]{1,0:T(8,128)S(1)}, u32[]{:S(2)}, u32[]{:S(2)}) collective-permute-start(f32[128,1280]{1,0:T(8,128)S(1)} %get-tuple-element.18), channel_id=1, source_target_pairs={{0,16},{8,24},{1,17},{9,25},{2,18},{10,26},{3,19},{11,27},{4,20},{... | collective-permute-start | bytes 1966088 | tf_op jit(solution)/shard_map/ppermute | solution.py:253
  50.3 1.7 collective-permute-start.15
  56.1 4.1 %collective-permute-done.15 = f32[640,128]{1,0:T(8,128)S(1)} collective-permute-done((f32[640,128]{1,0:T(8,128)S(1)}, f32[640,128]{1,0:T(8,128)S(1)}, u32[]{:S(2)}, u32[]{:S(2)}) %collective-permute-start.15) | collective-permute-done | bytes 327712 | tf_op jit(solution)/shard_map/ppermute | solution.py:296
  62.7 4.0 %collective-permute-start.16 = (f32[640,128]{1,0:T(8,128)S(1)}, f32[640,128]{1,0:T(8,128)S(1)}, u32[]{:S(2)}, u32[]{:S(2)}) collective-permute-start(f32[640,128]{1,0:T(8,128)S(1)} %slice_select_fusion.4.refs_3_.refs_2_.refs_1_.refs_0_), channel_id=1, source_target_pairs={{0,2},{1,3},{2,4},{3,5},{4,6},{5,7},{8,10},{9,11},{10,12},{11,13},... | collective-permute-start | bytes 983048 | tf_op jit(solution)/shard_map/ppermute | solution.py:296
  67.9 14.2 %collective-permute-done.16 = f32[640,128]{1,0:T(8,128)S(1)} collective-permute-done((f32[640,128]{1,0:T(8,128)S(1)}, f32[640,128]{1,0:T(8,128)S(1)}, u32[]{:S(2)}, u32[]{:S(2)}) %collective-permute-start.16) | collective-permute-done | bytes 327712 | tf_op jit(solution)/shard_map/ppermute | solution.py:296
  82.0 1.5 collective-permute-start.8
  84.6 1.9 collective-permute-start.31
  86.5 3.2 %collective-permute-start.17 = (f32[640,128]{1,0:T(8,128)S(1)}, f32[640,128]{1,0:T(8,128)S(1)}, u32[]{:S(2)}, u32[]{:S(2)}) collective-permute-start(f32[640,128]{1,0:T(8,128)S(1)} %slice_select_fusion.5.refs_3_.refs_2_.refs_1_.refs_0_), channel_id=1, source_target_pairs={{0,2},{1,3},{2,4},{3,5},{4,6},{5,7},{8,10},{9,11},{10,12},{11,13},... | collective-permute-start | bytes 983048 | tf_op jit(solution)/shard_map/ppermute | solution.py:296
  89.8 1.9 collective-permute-start.30
  91.8 22.5 %shard_map.17 = (f32[256,256]{1,0:T(8,128)S(1)}, f32[256,256]{1,0:T(8,128)S(1)}, f32[256,256]{1,0:T(8,128)S(1)}) custom-call(f32[256,256]{1,0:T(8,128)S(1)} %select_select_fusion.corner_ref), custom_call_target="tpu_custom_call" | custom-call | flops 40000000 | bytes 1048576 | tf_op jit(solution)/shard_map/pallas_call | solution.py:93
  114.3 2.4 %collective-permute-start.29 = (f32[640,128]{1,0:T(8,128)S(1)}, f32[640,128]{1,0:T(8,128)S(1)}, u32[]{:S(2)}, u32[]{:S(2)}) collective-permute-start(f32[640,128]{1,0:T(8,128)S(1)} %slice_select_fusion.1.refs_2_.refs_1_.refs_0_), channel_id=1, source_target_pairs={{0,1},{1,0},{2,3},{3,2},{4,5},{5,4},{8,9},{9,8},{10,11},{11,10},{1... | collective-permute-start | bytes 983048 | tf_op jit(solution)/shard_map/ppermute | solution.py:293
  118.4 2.1 %collective-permute-start.18 = (f32[640,128]{1,0:T(8,128)S(1)}, f32[640,128]{1,0:T(8,128)S(1)}, u32[]{:S(2)}, u32[]{:S(2)}) collective-permute-start(f32[640,128]{1,0:T(8,128)S(1)} %slice_select_fusion.6.refs_3_.refs_2_.refs_1_.refs_0_), channel_id=1, source_target_pairs={{0,2},{1,3},{2,4},{3,5},{4,6},{5,7},{8,10},{9,11},{10,12},{11,13},... | collective-permute-start | bytes 983048 | tf_op jit(solution)/shard_map/ppermute | solution.py:296
  120.5 3.1 %shard_map.18 = (bf16[256,2560]{1,0:T(8,128)(2,1)S(1)}, bf16[256,2560]{1,0:T(8,128)(2,1)S(1)}) custom-call(s32[4]{0:T(128)S(1)} %pad_add_fusion.info_ref, f32[256,256]{1,0:T(8,128)S(1)} %get-tuple-element.10.inv_ref, f32[128,1280]{1,0:T(8,128)S(1)} %broadcast_select_fusion.1.refs_0_, f32[128,1280]{1,0:T(8,128)S(1)} %collective-permute-done.8.refs_1_, ...), custom_call_target="tpu_custom_call" | custom-call | flops 2013265920 | bytes 5242880 | tf_op jit(solution)/shard_map/pallas_call | solution.py:123
  124.2 9.4 %shard_map.19.refs_8_ = f32[5120,2560]{1,0:T(8,128)} custom-call(s32[4]{0:T(128)S(1)} %pad_add_fusion.info_ref, f32[5120,2560]{1,0:T(8,128)} %mat_ref.15, bf16[256,2560]{1,0:T(8,128)(2,1)S(1)} %get-tuple-element.11.high_ref, bf16[256,2560]{1,0:T(8,128)(2,1)S(1)} %get-tuple-element.12.low_ref, f32[256,256]{1,0:T(8,128)S(1)} %get-tuple-element.13.lower_ref, ...), custom_call_target="tpu_custom_call" | custom-call | flops 2516582400 | bytes 13107200 | tf_op jit(solution)/shard_map/pallas_call | solution.py:197
  134.3 9.5 %shard_map.20.refs_8_ = f32[5120,2560]{1,0:T(8,128)} custom-call(s32[4]{0:T(128)S(1)} %pad_add_fusion.info_ref, f32[5120,2560]{1,0:T(8,128)} %mat_ref.15, bf16[256,2560]{1,0:T(8,128)(2,1)S(1)} %get-tuple-element.11.high_ref, bf16[256,2560]{1,0:T(8,128)(2,1)S(1)} %get-tuple-element.12.low_ref, ...), custom_call_target="tpu_custom_call", output_to_operand_aliasing={{}: (14, {})} | custom-call | flops 2516582400 | bytes 13107200 | tf_op jit(solution)/shard_map/pallas_call | solution.py:197
  143.9 9.5 %shard_map.21.refs_8_ = f32[5120,2560]{1,0:T(8,128)} custom-call(s32[4]{0:T(128)S(1)} %pad_add_fusion.info_ref, f32[5120,2560]{1,0:T(8,128)} %mat_ref.15, bf16[256,2560]{1,0:T(8,128)(2,1)S(1)} %get-tuple-element.11.high_ref, bf16[256,2560]{1,0:T(8,128)(2,1)S(1)} %get-tuple-element.12.low_ref, ...), custom_call_target="tpu_custom_call", output_to_operand_aliasing={{}: (14, {})} | custom-call | flops 2516582400 | bytes 13107200 | tf_op jit(solution)/shard_map/pallas_call | solution.py:197
  154.8 9.5 %shard_map.22.refs_8_ = f32[5120,2560]{1,0:T(8,128)} custom-call(s32[4]{0:T(128)S(1)} %pad_add_fusion.info_ref, f32[5120,2560]{1,0:T(8,128)} %mat_ref.15, bf16[256,2560]{1,0:T(8,128)(2,1)S(1)} %get-tuple-element.11.high_ref, bf16[256,2560]{1,0:T(8,128)(2,1)S(1)} %get-tuple-element.12.low_ref, ...), custom_call_target="tpu_custom_call", output_to_operand_aliasing={{}: (14, {})} | custom-call | flops 2516582400 | bytes 13107200 | tf_op jit(solution)/shard_map/pallas_call | solution.py:197
  165.0 9.5 %shard_map.23.refs_8_ = f32[5120,2560]{1,0:T(8,128)} custom-call(s32[4]{0:T(128)S(1)} %pad_add_fusion.info_ref, f32[5120,2560]{1,0:T(8,128)} %mat_ref.15, bf16[256,2560]{1,0:T(8,128)(2,1)S(1)} %get-tuple-element.11.high_ref, bf16[256,2560]{1,0:T(8,128)(2,1)S(1)} %get-tuple-element.12.low_ref, ...), custom_call_target="tpu_custom_call", output_to_operand_aliasing={{}: (14, {})} | custom-call | flops 2516582400 | bytes 13107200 | tf_op jit(solution)/shard_map/pallas_call | solution.py:197
  175.4 9.5 %shard_map.24.refs_8_ = f32[5120,2560]{1,0:T(8,128)} custom-call(s32[4]{0:T(128)S(1)} %pad_add_fusion.info_ref, f32[5120,2560]{1,0:T(8,128)} %mat_ref.15, bf16[256,2560]{1,0:T(8,128)(2,1)S(1)} %get-tuple-element.11.high_ref, bf16[256,2560]{1,0:T(8,128)(2,1)S(1)} %get-tuple-element.12.low_ref, ...), custom_call_target="tpu_custom_call", output_to_operand_aliasing={{}: (14, {})} | custom-call | flops 2516582400 | bytes 13107200 | tf_op jit(solution)/shard_map/pallas_call | solution.py:197
  184.9 9.5 %shard_map.25.refs_8_ = f32[5120,2560]{1,0:T(8,128)} custom-call(s32[4]{0:T(128)S(1)} %pad_add_fusion.info_ref, f32[5120,2560]{1,0:T(8,128)} %mat_ref.15, bf16[256,2560]{1,0:T(8,128)(2,1)S(1)} %get-tuple-element.11.high_ref, bf16[256,2560]{1,0:T(8,128)(2,1)S(1)} %get-tuple-element.12.low_ref, ...), custom_call_target="tpu_custom_call", output_to_operand_aliasing={{}: (14, {})} | custom-call | flops 2516582400 | bytes 13107200 | tf_op jit(solution)/shard_map/pallas_call | solution.py:197
  194.4 9.5 %shard_map.26 = f32[5120,2560]{1,0:T(8,128)} custom-call(s32[4]{0:T(128)S(1)} %pad_add_fusion.info_ref, f32[5120,2560]{1,0:T(8,128)} %mat_ref.15, bf16[256,2560]{1,0:T(8,128)(2,1)S(1)} %get-tuple-element.11.high_ref, bf16[256,2560]{1,0:T(8,128)(2,1)S(1)} %get-tuple-element.12.low_ref, ...), custom_call_target="tpu_custom_call", output_to_operand_aliasing={{}: (14, {})} | custom-call | flops 2516582400 | bytes 13107200 | tf_op jit(solution)/shard_map/pallas_call | solution.py:197
  (60 shorter events, 24.1 us)
Async XLA Ops:
  1.0 11.9 %collective-permute-start.11 = (f32[640,128]{1,0:T(8,128)S(1)}, f32[640,128]{1,0:T(8,128)S(1)}, u32[]{:S(2)}, u32[]{:S(2)}) collective-permute-start(f32[640,128]{1,0:T(8,128)S(1)} %slice.43.refs_0_), channel_id=1, source_target_pairs={{0,2},{1,3},{8,10},{9,11},{16,18},{17,19},{24,26},{25,27}} | collective-permute-start | bytes 983048 | tf_op jit(solution)/shard_map/ppermute | solution.py:296
  13.9 11.9 %collective-permute-start.12 = (f32[640,128]{1,0:T(8,128)S(1)}, f32[640,128]{1,0:T(8,128)S(1)}, u32[]{:S(2)}, u32[]{:S(2)}) collective-permute-start(f32[640,128]{1,0:T(8,128)S(1)} %slice_select_fusion.refs_1_.refs_0_), channel_id=1, source_target_pairs={{0,2},{1,3},{2,4},{3,5},{8,10},{9,11},{10,12},{11,13},{16,18},{17,... | collective-permute-start | bytes 983048 | tf_op jit(solution)/shard_map/ppermute | solution.py:296
  19.2 10.6 %collective-permute-start = (f32[128,128]{1,0:T(8,128)S(1)}, f32[128,128]{1,0:T(8,128)S(1)}, u32[]{:S(2)}, u32[]{:S(2)}) collective-permute-start(f32[128,128]{1,0:T(8,128)S(1)} %slice.33), channel_id=1, source_target_pairs={{0,1},{1,0},{8,9},{9,8},{16,17},{17,16},{24,25},{25,24}} | collective-permute-start | bytes 196616 | tf_op jit(solution)/shard_map/ppermute | solution.py:227
  22.2 21.3 %collective-permute-start.9 = (f32[128,1280]{1,0:T(8,128)S(1)}, f32[128,1280]{1,0:T(8,128)S(1)}, u32[]{:S(2)}, u32[]{:S(2)}) collective-permute-start(f32[128,1280]{1,0:T(8,128)S(1)} %slice.35), channel_id=1, source_target_pairs={{0,16},{8,24},{1,17},{9,25},{2,18},{10,26},{3,19},{11,27},{4,20},{... | collective-permute-start | bytes 1966088 | tf_op jit(solution)/shard_map/ppermute | solution.py:253
  26.8 12.1 %collective-permute-start.13 = (f32[640,128]{1,0:T(8,128)S(1)}, f32[640,128]{1,0:T(8,128)S(1)}, u32[]{:S(2)}, u32[]{:S(2)}) collective-permute-start(f32[640,128]{1,0:T(8,128)S(1)} %slice_select_fusion.1.refs_2_.refs_1_.refs_0_), channel_id=1, source_target_pairs={{0,2},{1,3},{2,4},{3,5},{4,6},{5,7},{8,10},{9,11},{10,12},{11,13},... | collective-permute-start | bytes 983048 | tf_op jit(solution)/shard_map/ppermute | solution.py:296
  30.7 21.4 %collective-permute-start.1 = (f32[128,256]{1,0:T(8,128)S(1)}, f32[128,256]{1,0:T(8,128)S(1)}, u32[]{:S(2)}, u32[]{:S(2)}) collective-permute-start(f32[128,256]{1,0:T(8,128)S(1)} %pad_maximum_fusion.1), channel_id=1, source_target_pairs={{0,24},{8,0},{1,25},{9,1},{2,26},{10,2},{3,27},{11,3},{4,28},{12,4... | collective-permute-start | bytes 393224 | tf_op jit(solution)/shard_map/ppermute | solution.py:234
  35.0 17.0 %collective-permute-start.2 = (f32[128,256]{1,0:T(8,128)S(1)}, f32[128,256]{1,0:T(8,128)S(1)}, u32[]{:S(2)}, u32[]{:S(2)}) collective-permute-start(f32[128,256]{1,0:T(8,128)S(1)} %pad_maximum_fusion.1), channel_id=1, source_target_pairs={{0,16},{8,24},{1,17},{9,25},{2,18},{10,26},{3,19},{11,27},{4,20},{... | collective-permute-start | bytes 393224 | tf_op jit(solution)/shard_map/ppermute | solution.py:234
  36.3 15.7 %collective-permute-start.3 = (f32[128,256]{1,0:T(8,128)S(1)}, f32[128,256]{1,0:T(8,128)S(1)}, u32[]{:S(2)}, u32[]{:S(2)}) collective-permute-start(f32[128,256]{1,0:T(8,128)S(1)} %pad_maximum_fusion.1), channel_id=1, source_target_pairs={{0,8},{8,16},{1,9},{9,17},{2,10},{10,18},{3,11},{11,19},{4,12},{12... | collective-permute-start | bytes 393224 | tf_op jit(solution)/shard_map/ppermute | solution.py:234
  39.9 9.5 %collective-permute-start.14 = (f32[640,128]{1,0:T(8,128)S(1)}, f32[640,128]{1,0:T(8,128)S(1)}, u32[]{:S(2)}, u32[]{:S(2)}) collective-permute-start(f32[640,128]{1,0:T(8,128)S(1)} %slice_select_fusion.2.refs_3_.refs_2_.refs_1_.refs_0_), channel_id=1, source_target_pairs={{0,2},{1,3},{2,4},{3,5},{4,6},{5,7},{8,10},{9,11},{10,12},{11,13},... | collective-permute-start | bytes 983048 | tf_op jit(solution)/shard_map/ppermute | solution.py:296
  44.9 17.9 %collective-permute-start.7 = (f32[128,1280]{1,0:T(8,128)S(1)}, f32[128,1280]{1,0:T(8,128)S(1)}, u32[]{:S(2)}, u32[]{:S(2)}) collective-permute-start(f32[128,1280]{1,0:T(8,128)S(1)} %get-tuple-element.18), channel_id=1, source_target_pairs={{0,16},{8,24},{1,17},{9,25},{2,18},{10,26},{3,19},{11,27},{4,20},{... | collective-permute-start | bytes 1966088 | tf_op jit(solution)/shard_map/ppermute | solution.py:253
  50.3 9.9 %collective-permute-start.15 = (f32[640,128]{1,0:T(8,128)S(1)}, f32[640,128]{1,0:T(8,128)S(1)}, u32[]{:S(2)}, u32[]{:S(2)}) collective-permute-start(f32[640,128]{1,0:T(8,128)S(1)} %slice_select_fusion.3.refs_3_.refs_2_.refs_1_.refs_0_), channel_id=1, source_target_pairs={{0,2},{1,3},{2,4},{3,5},{4,6},{5,7},{8,10},{9,11},{10,12},{11,13},... | collective-permute-start | bytes 983048 | tf_op jit(solution)/shard_map/ppermute | solution.py:296
  52.2 32.4 %collective-permute-start.4 = (f32[256,256]{1,0:T(8,128)S(1)}, f32[256,256]{1,0:T(8,128)S(1)}, u32[]{:S(2)}, u32[]{:S(2)}) collective-permute-start(f32[256,256]{1,0:T(8,128)S(1)} %pad_maximum_fusion), channel_id=1, source_target_pairs={{0,6},{1,7},{8,14},{9,15},{16,22},{17,23},{24,30},{25,31}} | collective-permute-start | bytes 786440 | tf_op jit(solution)/shard_map/ppermute | solution.py:245
  53.5 33.0 %collective-permute-start.5 = (f32[256,256]{1,0:T(8,128)S(1)}, f32[256,256]{1,0:T(8,128)S(1)}, u32[]{:S(2)}, u32[]{:S(2)}) collective-permute-start(f32[256,256]{1,0:T(8,128)S(1)} %pad_maximum_fusion), channel_id=1, source_target_pairs={{0,4},{1,5},{8,12},{9,13},{16,20},{17,21},{24,28},{25,29}} | collective-permute-start | bytes 786440 | tf_op jit(solution)/shard_map/ppermute | solution.py:245
  54.8 35.0 %collective-permute-start.6 = (f32[256,256]{1,0:T(8,128)S(1)}, f32[256,256]{1,0:T(8,128)S(1)}, u32[]{:S(2)}, u32[]{:S(2)}) collective-permute-start(f32[256,256]{1,0:T(8,128)S(1)} %pad_maximum_fusion), channel_id=1, source_target_pairs={{0,2},{1,3},{8,10},{9,11},{16,18},{17,19},{24,26},{25,27}} | collective-permute-start | bytes 786440 | tf_op jit(solution)/shard_map/ppermute | solution.py:245
  60.2 57.6 %collective-permute-start.10 = (f32[128,1280]{1,0:T(8,128)S(1)}, f32[128,1280]{1,0:T(8,128)S(1)}, u32[]{:S(2)}, u32[]{:S(2)}) collective-permute-start(f32[128,1280]{1,0:T(8,128)S(1)} %get-tuple-element.17.refs_2_), channel_id=1, source_target_pairs={{0,8},{8,0},{16,24},{24,16},{1,9},{9,1},{17,25},{25,17},{2,10},{10... | collective-permute-start | bytes 1966088 | tf_op jit(solution)/shard_map/ppermute | solution.py:256
  62.7 19.3 %collective-permute-start.16 = (f32[640,128]{1,0:T(8,128)S(1)}, f32[640,128]{1,0:T(8,128)S(1)}, u32[]{:S(2)}, u32[]{:S(2)}) collective-permute-start(f32[640,128]{1,0:T(8,128)S(1)} %slice_select_fusion.4.refs_3_.refs_2_.refs_1_.refs_0_), channel_id=1, source_target_pairs={{0,2},{1,3},{2,4},{3,5},{4,6},{5,7},{8,10},{9,11},{10,12},{11,13},... | collective-permute-start | bytes 983048 | tf_op jit(solution)/shard_map/ppermute | solution.py:296
  82.0 36.4 %collective-permute-start.8 = (f32[128,1280]{1,0:T(8,128)S(1)}, f32[128,1280]{1,0:T(8,128)S(1)}, u32[]{:S(2)}, u32[]{:S(2)}) collective-permute-start(f32[128,1280]{1,0:T(8,128)S(1)} %broadcast_select_fusion.1.refs_0_), channel_id=1, source_target_pairs={{0,8},{8,0},{16,24},{24,16},{1,9},{9,1},{17,25},{25,17},{2,10},{10... | collective-permute-start | bytes 1966088 | tf_op jit(solution)/shard_map/ppermute | solution.py:256
  84.6 29.7 %collective-permute-start.31 = (f32[640,128]{1,0:T(8,128)S(1)}, f32[640,128]{1,0:T(8,128)S(1)}, u32[]{:S(2)}, u32[]{:S(2)}) collective-permute-start(f32[640,128]{1,0:T(8,128)S(1)} %slice.43.refs_0_), channel_id=1, source_target_pairs={{0,1},{1,0},{8,9},{9,8},{16,17},{17,16},{24,25},{25,24}} | collective-permute-start | bytes 983048 | tf_op jit(solution)/shard_map/ppermute | solution.py:293
  86.5 30.2 %collective-permute-start.17 = (f32[640,128]{1,0:T(8,128)S(1)}, f32[640,128]{1,0:T(8,128)S(1)}, u32[]{:S(2)}, u32[]{:S(2)}) collective-permute-start(f32[640,128]{1,0:T(8,128)S(1)} %slice_select_fusion.5.refs_3_.refs_2_.refs_1_.refs_0_), channel_id=1, source_target_pairs={{0,2},{1,3},{2,4},{3,5},{4,6},{5,7},{8,10},{9,11},{10,12},{11,13},... | collective-permute-start | bytes 983048 | tf_op jit(solution)/shard_map/ppermute | solution.py:296
  89.8 33.8 %collective-permute-start.30 = (f32[640,128]{1,0:T(8,128)S(1)}, f32[640,128]{1,0:T(8,128)S(1)}, u32[]{:S(2)}, u32[]{:S(2)}) collective-permute-start(f32[640,128]{1,0:T(8,128)S(1)} %slice_select_fusion.refs_1_.refs_0_), channel_id=1, source_target_pairs={{0,1},{1,0},{2,3},{3,2},{8,9},{9,8},{10,11},{11,10},{16,17},{17,16... | collective-permute-start | bytes 983048 | tf_op jit(solution)/shard_map/ppermute | solution.py:293
  114.3 9.4 %collective-permute-start.29 = (f32[640,128]{1,0:T(8,128)S(1)}, f32[640,128]{1,0:T(8,128)S(1)}, u32[]{:S(2)}, u32[]{:S(2)}) collective-permute-start(f32[640,128]{1,0:T(8,128)S(1)} %slice_select_fusion.1.refs_2_.refs_1_.refs_0_), channel_id=1, source_target_pairs={{0,1},{1,0},{2,3},{3,2},{4,5},{5,4},{8,9},{9,8},{10,11},{11,10},{1... | collective-permute-start | bytes 983048 | tf_op jit(solution)/shard_map/ppermute | solution.py:293
  116.7 7.4 %collective-permute-start.28 = (f32[640,128]{1,0:T(8,128)S(1)}, f32[640,128]{1,0:T(8,128)S(1)}, u32[]{:S(2)}, u32[]{:S(2)}) collective-permute-start(f32[640,128]{1,0:T(8,128)S(1)} %slice_select_fusion.2.refs_3_.refs_2_.refs_1_.refs_0_), channel_id=1, source_target_pairs={{0,1},{1,0},{2,3},{3,2},{4,5},{5,4},{6,7},{7,6},{8,9},{9,8},{10,11... | collective-permute-start | bytes 983048 | tf_op jit(solution)/shard_map/ppermute | solution.py:293
  117.8 16.4 %collective-permute-start.27 = (f32[640,128]{1,0:T(8,128)S(1)}, f32[640,128]{1,0:T(8,128)S(1)}, u32[]{:S(2)}, u32[]{:S(2)}) collective-permute-start(f32[640,128]{1,0:T(8,128)S(1)} %slice_select_fusion.3.refs_3_.refs_2_.refs_1_.refs_0_), channel_id=1, source_target_pairs={{0,1},{1,0},{2,3},{3,2},{4,5},{5,4},{6,7},{7,6},{8,9},{9,8},{10,11... | collective-permute-start | bytes 983048 | tf_op jit(solution)/shard_map/ppermute | solution.py:293
  118.4 15.2 %collective-permute-start.18 = (f32[640,128]{1,0:T(8,128)S(1)}, f32[640,128]{1,0:T(8,128)S(1)}, u32[]{:S(2)}, u32[]{:S(2)}) collective-permute-start(f32[640,128]{1,0:T(8,128)S(1)} %slice_select_fusion.6.refs_3_.refs_2_.refs_1_.refs_0_), channel_id=1, source_target_pairs={{0,2},{1,3},{2,4},{3,5},{4,6},{5,7},{8,10},{9,11},{10,12},{11,13},... | collective-permute-start | bytes 983048 | tf_op jit(solution)/shard_map/ppermute | solution.py:296
  123.6 20.4 %collective-permute-start.26 = (f32[640,128]{1,0:T(8,128)S(1)}, f32[640,128]{1,0:T(8,128)S(1)}, u32[]{:S(2)}, u32[]{:S(2)}) collective-permute-start(f32[640,128]{1,0:T(8,128)S(1)} %slice_select_fusion.4.refs_3_.refs_2_.refs_1_.refs_0_), channel_id=1, source_target_pairs={{0,1},{1,0},{2,3},{3,2},{4,5},{5,4},{6,7},{7,6},{8,9},{9,8},{10,11... | collective-permute-start | bytes 983048 | tf_op jit(solution)/shard_map/ppermute | solution.py:293
  123.7 31.1 %collective-permute-start.25 = (f32[640,128]{1,0:T(8,128)S(1)}, f32[640,128]{1,0:T(8,128)S(1)}, u32[]{:S(2)}, u32[]{:S(2)}) collective-permute-start(f32[640,128]{1,0:T(8,128)S(1)} %slice_select_fusion.5.refs_3_.refs_2_.refs_1_.refs_0_), channel_id=1, source_target_pairs={{0,1},{1,0},{2,3},{3,2},{4,5},{5,4},{6,7},{7,6},{8,9},{9,8},{10,11... | collective-permute-start | bytes 983048 | tf_op jit(solution)/shard_map/ppermute | solution.py:293
  133.6 20.5 %collective-permute-start.19 = (f32[640,128]{1,0:T(8,128)S(1)}, f32[640,128]{1,0:T(8,128)S(1)}, u32[]{:S(2)}, u32[]{:S(2)}) collective-permute-start(f32[640,128]{1,0:T(8,128)S(1)} %collective-permute-done.18.refs_3_.refs_2_.refs_1_), channel_id=1, source_target_pairs={{2,4},{3,5},{4,6},{5,7},{10,12},{11,13},{12,14},{13,15},{18,20},{1... | collective-permute-start | bytes 983048 | tf_op jit(solution)/shard_map/ppermute | solution.py:296
  143.8 21.2 %collective-permute-start.21 = (f32[640,128]{1,0:T(8,128)S(1)}, f32[640,128]{1,0:T(8,128)S(1)}, u32[]{:S(2)}, u32[]{:S(2)}) collective-permute-start(f32[640,128]{1,0:T(8,128)S(1)} %slice_select_fusion.6.refs_3_.refs_2_.refs_1_.refs_0_), channel_id=1, source_target_pairs={{0,1},{1,0},{2,3},{3,2},{4,5},{5,4},{6,7},{7,6},{8,9},{9,8},{10,11... | collective-permute-start | bytes 983048 | tf_op jit(solution)/shard_map/ppermute | solution.py:293
  153.4 22.0 %collective-permute-start.22 = (f32[640,128]{1,0:T(8,128)S(1)}, f32[640,128]{1,0:T(8,128)S(1)}, u32[]{:S(2)}, u32[]{:S(2)}) collective-permute-start(f32[640,128]{1,0:T(8,128)S(1)} %collective-permute-done.18.refs_3_.refs_2_.refs_1_), channel_id=1, source_target_pairs={{2,3},{3,2},{4,5},{5,4},{6,7},{7,6},{10,11},{11,10},{12,13},{13,12... | collective-permute-start | bytes 983048 | tf_op jit(solution)/shard_map/ppermute | solution.py:293
  154.1 20.4 %collective-permute-start.20 = (f32[640,128]{1,0:T(8,128)S(1)}, f32[640,128]{1,0:T(8,128)S(1)}, u32[]{:S(2)}, u32[]{:S(2)}) collective-permute-start(f32[640,128]{1,0:T(8,128)S(1)} %collective-permute-done.19.refs_3_.refs_2_), channel_id=1, source_target_pairs={{4,6},{5,7},{12,14},{13,15},{20,22},{21,23},{28,30},{29,31}} | collective-permute-start | bytes 983048 | tf_op jit(solution)/shard_map/ppermute | solution.py:296
  164.3 20.6 %collective-permute-start.23 = (f32[640,128]{1,0:T(8,128)S(1)}, f32[640,128]{1,0:T(8,128)S(1)}, u32[]{:S(2)}, u32[]{:S(2)}) collective-permute-start(f32[640,128]{1,0:T(8,128)S(1)} %collective-permute-done.19.refs_3_.refs_2_), channel_id=1, source_target_pairs={{4,5},{5,4},{6,7},{7,6},{12,13},{13,12},{14,15},{15,14},{20,21},{2... | collective-permute-start | bytes 983048 | tf_op jit(solution)/shard_map/ppermute | solution.py:293
  174.5 19.9 %collective-permute-start.24 = (f32[640,128]{1,0:T(8,128)S(1)}, f32[640,128]{1,0:T(8,128)S(1)}, u32[]{:S(2)}, u32[]{:S(2)}) collective-permute-start(f32[640,128]{1,0:T(8,128)S(1)} %collective-permute-done.20.refs_3_), channel_id=1, source_target_pairs={{6,7},{7,6},{14,15},{15,14},{22,23},{23,22},{30,31},{31,30}} | collective-permute-start | bytes 983048 | tf_op jit(solution)/shard_map/ppermute | solution.py:293

commit v2 on v1

v2 whole, which is shorter than its diff:
```python
import functools

import jax
import jax.numpy as jnp
from jax import lax
from jax.experimental import pallas as pl
from jax.experimental.pallas import tpu as pltpu
from jax.sharding import PartitionSpec as P

TILE = 128
PANELS = 2
WIDE = PANELS * TILE
CORES = 2
VMEM_LIMIT = 40 * 1024 * 1024
GROUP = 8
IN_SLOTS = 3
OUT_SLOTS = 2
PIECES = 4


def dot_full(left, right, dims=((1,), (0,))):
    return lax.dot_general(
        left,
        right,
        (dims, ((), ())),
        precision=lax.Precision.HIGHEST,
        preferred_element_type=jnp.float32,
    )


def dot_half(left, right):
    return lax.dot_general(
        left, right, (((1,), (0,)), ((), ())), preferred_element_type=jnp.float32
    )


def split_half(value):
    high = value.astype(jnp.bfloat16)
    low = (value - high.astype(jnp.float32)).astype(jnp.bfloat16)
    return high, low


def stack_halves(ref, value):
    high, low = split_half(value)
    ref[:WIDE] = high
    ref[WIDE : 2 * WIDE] = low
    ref[2 * WIDE :] = high


def spread_halves(value):
    high, low = split_half(value)
    return jnp.concatenate([high, high, low], axis=1)


def factor_tile(square):
    groups = TILE // GROUP
    shape = (GROUP, TILE)
    lane = lax.broadcasted_iota(jnp.int32, shape, 1)
    sub = lax.broadcasted_iota(jnp.int32, shape, 0)
    left = [square[g * GROUP : (g + 1) * GROUP] for g in range(groups)]
    right = [jnp.where(lane == sub + g * GROUP, 1.0, 0.0) for g in range(groups)]

    def row_of(value, index):
        return jnp.broadcast_to(value[index : index + 1], shape)

    def column_of(value, index):
        return jnp.broadcast_to(value[:, index : index + 1], shape)

    for g in range(groups):
        first = g * GROUP
        span = range(GROUP)
        columns = [column_of(left[g], first + b) for b in span]
        block = [[row_of(columns[b], a) if a <= b else None for b in span] for a in span]
        ratio = [[None] * GROUP for _ in span]
        inverse = []
        for s in span:
            inverse.append(1.0 / block[s][s])
            for t in range(s + 1, GROUP):
                ratio[t][s] = block[s][t] * inverse[s]
            for t in range(s + 1, GROUP):
                for b in range(t, GROUP):
                    block[t][b] = block[t][b] - ratio[t][s] * block[s][b]
        rows_left = [row_of(left[g], s) for s in span]
        rows_right = [row_of(right[g], s) for s in span]
        for t in span:
            for s in range(t):
                rows_left[t] = rows_left[t] - ratio[t][s] * rows_left[s]
                rows_right[t] = rows_right[t] - ratio[t][s] * rows_right[s]
        for s in span:
            left[g] = jnp.where(sub == s, rows_left[s], left[g])
            right[g] = jnp.where(sub == s, rows_right[s], right[g])
        rows_left = [rows_left[s] * inverse[s] for s in span]
        rows_right = [rows_right[s] * inverse[s] for s in span]
        for other in range(g + 1, groups):
            columns = [column_of(left[other], first + s) for s in span]
            for s in span:
                for t in range(s):
                    columns[s] = columns[s] - ratio[s][t] * columns[t]
            for s in span:
                left[other] = left[other] - columns[s] * rows_left[s]
                right[other] = right[other] - columns[s] * rows_right[s]
    upper, inverse = [], []
    for g in range(groups):
        row = sub + g * GROUP
        pivot = jnp.sum(jnp.where(lane == row, left[g], 0.0), axis=1, keepdims=True)
        scale = 1.0 / jnp.sqrt(pivot)
        upper.append(jnp.where(lane >= row, left[g] * scale, 0.0))
        inverse.append(right[g] * scale)
    return jnp.concatenate(upper, axis=0), jnp.concatenate(inverse, axis=0)


def corner_kernel(corner_ref, low_ref, inv_ref, inv_t_ref):
    zero = jnp.zeros((TILE, TILE), jnp.float32)
    upper_0, inv_0 = factor_tile(corner_ref[:TILE, :TILE])
    low_10 = dot_full(corner_ref[TILE:, :TILE], inv_0, ((1,), (1,)))
    square = corner_ref[TILE:, TILE:] - dot_full(low_10, low_10, ((1,), (1,)))
    upper_1, inv_1 = factor_tile(square)
    inv_10 = -dot_full(inv_1, dot_full(low_10, inv_0))
    low_ref[:TILE, :TILE] = upper_0.T
    low_ref[:TILE, TILE:] = zero
    low_ref[TILE:, :TILE] = low_10
    low_ref[TILE:, TILE:] = upper_1.T
    first = jnp.concatenate([inv_0, zero], axis=1)
    second = jnp.concatenate([inv_10, inv_1], axis=1)
    inv_ref[...] = spread_halves(jnp.concatenate([first, second], axis=0))
    first = jnp.concatenate([inv_0.T, inv_10.T], axis=1)
    second = jnp.concatenate([zero, inv_1.T], axis=1)
    stack_halves(inv_t_ref, jnp.concatenate([first, second], axis=0))


def factor_corner(corner):
    return pl.pallas_call(
        corner_kernel,
        out_shape=(
            jax.ShapeDtypeStruct((WIDE, WIDE), jnp.float32),
            jax.ShapeDtypeStruct((WIDE, 3 * WIDE), jnp.bfloat16),
            jax.ShapeDtypeStruct((3 * WIDE, WIDE), jnp.bfloat16),
        ),
        compiler_params=pltpu.CompilerParams(vmem_limit_bytes=VMEM_LIMIT),
        cost_estimate=pl.CostEstimate(flops=40_000_000, bytes_accessed=1 << 20, transcendentals=0),
    )(corner)


def columns_kernel(info_ref, inv_ref, *refs):
    out_ref, stack = refs[-2:]
    odd = info_ref[0] % 2 == 1
    start = 0
    for mine_ref, other_ref in zip(refs[0:-2:2], refs[1:-2:2]):
        size = mine_ref.shape[1]
        here = pl.ds(start, size)
        mine, other = mine_ref[...], other_ref[...]
        first = jnp.where(odd, other, mine)
        second = jnp.where(odd, mine, other)
        stack_halves(stack.at[:, here], jnp.concatenate([first, second], axis=0))
        stack_halves(out_ref.at[:, here], dot_half(inv_ref[...], stack[:, here]))
        start += size


def solve_columns(info, inverse, pairs):
    flat = [array for pair in pairs for array in pair]
    total = sum(pair[0].shape[1] for pair in pairs)
    vmem = pl.BlockSpec(memory_space=pltpu.VMEM)
    return pl.pallas_call(
        columns_kernel,
        in_specs=[pl.BlockSpec(memory_space=pltpu.SMEM)] + [vmem] * (1 + len(flat)),
        out_specs=vmem,
        out_shape=jax.ShapeDtypeStruct((3 * WIDE, total), jnp.bfloat16),
        scratch_shapes=[pltpu.VMEM((3 * WIDE, total), jnp.bfloat16)],
        compiler_params=pltpu.CompilerParams(vmem_limit_bytes=VMEM_LIMIT),
        cost_estimate=pl.CostEstimate(
            flops=6 * WIDE * WIDE * total, bytes_accessed=WIDE * total * 8, transcendentals=0
        ),
    )(info, inverse, *flat)


def update_kernel(
    start,
    rows,
    offset,
    strip,
    info_ref,
    mat_ref,
    right_ref,
    lower_ref,
    inv_t_ref,
    mine_ref,
    other_ref,
    *refs,
):
    out_ref, taken, given, panel, first_panel, in_sems, out_sems = refs[-7:]
    row, core, col = info_ref[0], info_ref[2], info_ref[3]
    columns = mat_ref.shape[1]
    steps = rows // strip
    block = next(b for b in (512, 640, 256, TILE) if columns % b == 0)
    piece = strip // PIECES

    def rows_at(ref, step, skip, count):
        return ref.at[pl.ds(pl.multiple_of(start + step * strip + skip, 8), count)]

    def take(step, slot):
        for p in range(PIECES):
            pltpu.make_async_copy(
                rows_at(mat_ref, step, p * piece, piece),
                taken.at[slot, pl.ds(p * piece, piece)],
                in_sems.at[slot],
            ).start()

    def give(step, slot):
        for p in range(PIECES):
            pltpu.make_async_copy(
                given.at[slot, pl.ds(p * piece, piece)],
                rows_at(out_ref, step, p * piece, piece),
                out_sems.at[slot],
            ).start()

    def wait_taken(step, slot):
        whole = rows_at(mat_ref, step, 0, strip)
        pltpu.make_async_copy(whole, taken.at[slot], in_sems.at[slot]).wait()

    def wait_given(step, slot):
        whole = rows_at(out_ref, step, 0, strip)
        pltpu.make_async_copy(given.at[slot], whole, out_sems.at[slot]).wait()

    for step in range(min(IN_SLOTS, steps)):
        take(step, step)

    @pl.loop(0, steps)
    def _(step):
        in_slot, out_slot = lax.rem(step, IN_SLOTS), lax.rem(step, OUT_SLOTS)
        here = pl.ds(pl.multiple_of(offset + step * strip, TILE), strip)
        mine, other = mine_ref[here], other_ref[here]
        raw = jnp.concatenate(
            [jnp.where(core == 1, other, mine), jnp.where(core == 1, mine, other)], axis=1
        )
        solved = dot_half(spread_halves(raw), inv_t_ref[...])
        panel[...] = spread_halves(solved)
        first_panel[...] = jnp.where(col == 1, solved[:, TILE:], solved[:, :TILE])
        top = jnp.logical_and(step == 0, row < PANELS)
        if start == 0:

            @pl.when(top)
            def _():
                head = jnp.where(row == 0, lower_ref[:TILE], lower_ref[TILE:])
                panel[:TILE] = spread_halves(head)
                first_panel[:TILE] = jnp.where(col == 1, head[:, TILE:], head[:, :TILE])

        wait_taken(step, in_slot)

        @pl.when(step >= OUT_SLOTS)
        def _():
            wait_given(step - OUT_SLOTS, out_slot)

        @pl.loop(0, columns // block)
        def _(index):
            across = pl.ds(pl.multiple_of(index * block, block), block)
            product = dot_half(panel[...], right_ref[:, across])
            given[out_slot, :, across] = taken[in_slot, :, across] - product

        if start == 0:

            @pl.when(top)
            def _():
                given[out_slot, :TILE] = jnp.zeros((TILE, columns), jnp.float32)

        @pl.when(col < PANELS)
        def _():
            given[out_slot, :, :TILE] = first_panel[...]

        give(step, out_slot)

        @pl.when(step + IN_SLOTS < steps)
        def _():
            take(step + IN_SLOTS, in_slot)

    for step in range(max(steps - OUT_SLOTS, 0), steps):
        wait_given(step, step % OUT_SLOTS)


def update_rows(start, end, base, info, matrix, right, lower, inv_t, mine, other, out):
    rows, columns = end - start, matrix.shape[1]
    strip = 2 * TILE if rows % (2 * TILE) == 0 else TILE
    any_spec = pl.BlockSpec(memory_space=pl.ANY)
    vmem = pl.BlockSpec(memory_space=pltpu.VMEM)
    in_specs = [pl.BlockSpec(memory_space=pltpu.SMEM), any_spec] + [vmem] * 5
    operands = [info, matrix, right, lower, inv_t, mine, other]
    aliases = {}
    if out is not None:
        aliases = {len(operands): 0}
        in_specs.append(any_spec)
        operands.append(out)
    return pl.pallas_call(
        functools.partial(update_kernel, start, rows, start - base, strip),
        in_specs=in_specs,
        out_specs=any_spec,
        out_shape=jax.ShapeDtypeStruct(matrix.shape, jnp.float32),
        scratch_shapes=[
            pltpu.VMEM((IN_SLOTS, strip, columns), jnp.float32),
            pltpu.VMEM((OUT_SLOTS, strip, columns), jnp.float32),
            pltpu.VMEM((strip, 3 * WIDE), jnp.bfloat16),
            pltpu.VMEM((strip, TILE), jnp.float32),
            pltpu.SemaphoreType.DMA((IN_SLOTS,)),
            pltpu.SemaphoreType.DMA((OUT_SLOTS,)),
        ],
        input_output_aliases=aliases,
        compiler_params=pltpu.CompilerParams(vmem_limit_bytes=VMEM_LIMIT),
        cost_estimate=pl.CostEstimate(
            flops=6 * rows * columns * WIDE,
            bytes_accessed=8 * rows * columns,
            transcendentals=0,
        ),
    )(*operands)


def after(value, *earlier):
    return lax.optimization_barrier((value, *earlier))[0]


def double_rows(block, row, row_count):
    stride = PANELS
    while stride < row_count:
        pairs = [(i, i + stride) for i in range(min(stride, row_count - stride))]
        got = lax.ppermute(block, "row", pairs)
        block = jnp.where(jnp.logical_and(row >= stride, row < 2 * stride), got, block)
        stride *= 2
    return block


def swap_rows(block, row_count):
    return lax.ppermute(block, "row", [(i, i ^ 1) for i in range(row_count)])


def pick(blocks, index):
    chosen = blocks[0]
    for shift in range(1, len(blocks)):
        chosen = jnp.where(index == shift, blocks[shift], chosen)
    return chosen


def share_corner(matrix, row, place, core, row_count, col_count):
    depth = col_count // CORES
    tile = matrix[:TILE, :TILE]
    got = [tile]
    for shift in range(1, row_count):
        pairs = [
            (p * col_count + c, (p + shift) % row_count * col_count + c)
            for p in range(PANELS)
            for c in range(CORES)
        ]
        got.append(lax.ppermute(tile, ("row", "col"), pairs))
    column = jnp.concatenate([pick(got, (row - p) % row_count) for p in range(PANELS)], axis=0)
    beside = lax.ppermute(column, "col", [(0, 1), (1, 0)])
    square = jnp.concatenate(
        [jnp.where(core == 0, column, beside), jnp.where(core == 0, beside, column)], axis=1
    )
    got = [square]
    for shift in range(1, depth):
        pairs = [(c, c + CORES * shift) for c in range(CORES)]
        got.append(lax.ppermute(square, "col", pairs))
    return pick(got, place)


def spread_columns(block, place, col_count, between):
    stride = col_count // CORES // 2
    levels = []
    while stride > 0:
        block = after(block, *between[len(levels)])
        pairs = [(c, c + CORES * stride) for c in range(col_count) if c // CORES % (2 * stride) == 0]
        got = lax.ppermute(block, "col", pairs)
        block = jnp.where(place % (2 * stride) == stride, got, block)
        levels.append(block)
        stride //= 2
    return levels


def per_device(matrix):
    row_count = lax.axis_size("row")
    col_count = lax.axis_size("col")
    row = lax.axis_index("row")
    col = lax.axis_index("col")
    place, core = col // CORES, col % CORES
    info = jnp.stack([row, place, core, col]).astype(jnp.int32)
    tiles = matrix.shape[0] // TILE
    cut = tiles // 4 * 2 * TILE
    half = matrix.shape[1] // 2

    bands = [matrix[:TILE, :half], matrix[:TILE, half:]]
    bands = [double_rows(band, row, row_count) for band in bands]
    corner = share_corner(matrix, row, place, core, row_count, col_count)
    between = [()] + [(corner,)] * col_count
    first = spread_columns(matrix[:cut, :TILE], place, col_count, between)
    besides = [swap_rows(band, row_count) for band in bands]
    lower, inverse, inv_t = factor_corner(after(corner, besides[0], bands[1]))
    between = [(first[0],)] + [(inverse, besides[1])] * col_count
    second = spread_columns(matrix[cut:, :TILE], place, col_count, between)
    right = solve_columns(info, inverse, list(zip(bands, besides)))

    swap = [(c, c ^ 1) for c in range(col_count)]
    mine = first[-1]
    other = after(lax.ppermute(mine, "col", swap), *second[:-1])
    early = tiles // 8 * TILE
    shared = (info, matrix, right, lower, inv_t)
    out = update_rows(0, early, 0, *shared, mine, other, None)
    late_mine = second[-1]
    late_other = lax.ppermute(after(late_mine, out), "col", swap)
    out = update_rows(early, cut, 0, *shared, mine, other, out)
    return update_rows(cut, tiles * TILE, cut, *shared, late_mine, late_other, out)


def solution(mesh):
    return jax.shard_map(
        per_device,
        mesh=mesh,
        in_specs=(P("row", "col"),),
        out_specs=P("row", "col"),
        check_vma=False,
    )
```

time: 206 us -> 216 us (1.049)
  the two profiles are of different devices: /device:TPU:0 before, /device:TPU:25 now
where the time goes in v2:
time: 216 us
  waiting for transfers between devices  100 us (46%)
  Pallas kernels  74.6 us (35%)
  starting transfers between devices  29.2 us (14%)
  other arithmetic  6.58 us (3%)
  local copies, waits for them, and re-layouts  4.71 us (2%)
    pallas_call x3, Pallas kernels, update_rows(): pl.pallas_call(functools.partial(update_kernel, start, rows, start - base...  62.8 us
    ppermute x4, waiting for transfers between devices, spread_columns(): got = lax.ppermute(block, 'col', pairs)  44 us
    ppermute x3, waiting for transfers between devices, share_corner(): got.append(lax.ppermute(square, 'col', pairs))  34.1 us
    ppermute x2, waiting for transfers between devices, swap_rows(): return lax.ppermute(block, 'row', [(i, i ^ 1) for i in range(row_count)])  11.5 us
    ppermute x2, waiting for transfers between devices, double_rows(): got = lax.ppermute(block, 'row', pairs)  10.7 us
    pallas_call x1, Pallas kernels, factor_corner(): pl.pallas_call(corner_kernel, out_shape=(jax.ShapeDtypeStruct((WIDE, WIDE...  9.83 us
    ppermute x2, starting transfers between devices, double_rows(): got = lax.ppermute(block, 'row', pairs)  7.65 us
    ppermute x4, starting transfers between devices, spread_columns(): got = lax.ppermute(block, 'col', pairs)  6.24 us
  transfers between devices with their start and end apart: 17, of which 5 were waited for; matrix products, arithmetic and copies ran while one was open for 4% of the time, Pallas kernels for 23%

profile of v2, /device:TPU:25, one launch (start us, length us, event | category | flops | bytes accessed | tf_op | source)
XLA Modules:
  0.0 215.7 jit_solution(7034477973224890492)
XLA Ops:
  0.0 0.8 slice.15
  1.5 0.7 collective-permute-start.1
  2.2 0.7 collective-permute-start.2
  2.9 0.9 select_select_fusion.2
  3.8 0.7 collective-permute-start.3
  4.5 1.9 fusion
  6.4 1.7 collective-permute-start.11
  8.1 2.0 slice.17
  10.1 4.0 %collective-permute-start.9 = (f32[128,1280]{1,0:T(8,128)}, f32[128,1280]{1,0:T(8,128)}, u32[]{:S(2)}, u32[]{:S(2)}) collective-permute-start(f32[128,1280]{1,0:T(8,128)} %slice.17), channel_id=1, source_target_pairs={{0,16},{8,24},{1,17},{9,25},{2,18},{10,26},{3,19},{11,27},{4,20},{... | collective-permute-start | bytes 1966088 | tf_op jit(solution)/shard_map/ppermute | solution.py:322
  14.1 1.3 collective-permute-start.4
  15.4 1.4 collective-permute-start.5
  16.8 1.4 collective-permute-start.6
  18.2 34.1 %collective-permute-done.4 = f32[256,256]{1,0:T(8,128)S(1)} collective-permute-done((f32[256,256]{1,0:T(8,128)S(1)}, f32[256,256]{1,0:T(8,128)S(1)}, u32[]{:S(2)}, u32[]{:S(2)}) %collective-permute-start.4) | collective-permute-done | bytes 262176 | tf_op jit(solution)/shard_map/ppermute | solution.py:358
  52.3 1.4 broadcast_select_fusion.4
  53.7 3.7 %collective-permute-start.7 = (f32[128,1280]{1,0:T(8,128)S(1)}, f32[128,1280]{1,0:T(8,128)S(1)}, u32[]{:S(2)}, u32[]{:S(2)}) collective-permute-start(f32[128,1280]{1,0:T(8,128)S(1)} %get-tuple-element.28), channel_id=1, source_target_pairs={{0,16},{8,24},{1,17},{9,25},{2,18},{10,26},{3,19},{11,27},{4,20},{... | collective-permute-start | bytes 1966088 | tf_op jit(solution)/shard_map/ppermute | solution.py:322
  57.4 1.2 broadcast_select_fusion.1
  58.6 1.3 collective-permute-start.14
  59.9 10.7 %collective-permute-done.7 = f32[128,1280]{1,0:T(8,128)S(1)} collective-permute-done((f32[128,1280]{1,0:T(8,128)S(1)}, f32[128,1280]{1,0:T(8,128)S(1)}, u32[]{:S(2)}, u32[]{:S(2)}) %collective-permute-start.7) | collective-permute-done | bytes 655392 | tf_op jit(solution)/shard_map/ppermute | solution.py:322
  70.6 1.2 broadcast_select_fusion.5.refs_0_
  71.9 1.7 collective-permute-start.12
  73.6 1.4 collective-permute-start.10
  75.1 11.5 %collective-permute-done.8.refs_1_ = f32[128,1280]{1,0:T(8,128)S(1)} collective-permute-done((f32[128,1280]{1,0:T(8,128)S(1)}, f32[128,1280]{1,0:T(8,128)S(1)}, u32[]{:S(2)}, u32[]{:S(2)}) %collective-permute-start.8) | collective-permute-done | bytes 655392 | tf_op jit(solution)/shard_map/ppermute | solution.py:329
  86.5 9.8 %shard_map.17 = (f32[256,256]{1,0:T(8,128)S(1)}, bf16[256,768]{1,0:T(8,128)(2,1)S(1)}, bf16[768,256]{1,0:T(8,128)(2,1)S(1)}) custom-call(f32[256,256]{1,0:T(8,128)S(1)} %select_select_fusion.corner_ref), custom_call_target="tpu_custom_call" | custom-call | flops 40000000 | bytes 1048576 | tf_op jit(solution)/shard_map/pallas_call | solution.py:132
  96.5 1.5 broadcast_select_fusion.2.mine_ref
  98.0 4.6 %collective-permute-start.15 = (f32[2560,128]{1,0:T(8,128)S(1)}, f32[2560,128]{1,0:T(8,128)S(1)}, u32[]{:S(2)}, u32[]{:S(2)}) collective-permute-start(f32[2560,128]{1,0:T(8,128)S(1)} %broadcast_select_fusion.2.mine_ref), channel_id=1, source_target_pairs={{0,1},{1,0},{2,3},{3,2},{4,5},{5,4},{6,7},{7,6},{8,9},{9,8},{10,11... | collective-permute-start | bytes 3932168 | tf_op jit(solution)/shard_map/ppermute | solution.py:399
  102.7 1.5 collective-permute-start.13
  104.3 1.9 shard_map.18.right_ref
  106.2 10.9 %shard_map.19.refs_0_ = f32[5120,2560]{1,0:T(8,128)} custom-call(s32[4]{0:T(128)S(1)} %pad_add_fusion.info_ref, f32[5120,2560]{1,0:T(8,128)} %mat_ref.5, bf16[768,2560]{1,0:T(8,128)(2,1)S(1)} %shard_map.18.right_ref, f32[256,256]{1,0:T(8,128)S(1)} %get-tuple-element.16.lower_ref, bf16[768,256]{1,0:T(8,128)(2,1)S(1)} %get-tuple-element.17.inv_t_ref, ...), custom_call_target="tpu_custom_call" | custom-call | flops 2516582400 | bytes 13107200 | tf_op jit(solution)/shard_map/pallas_call | solution.py:291
  117.1 43.9 %collective-permute-done.13 = f32[2560,128]{1,0:T(8,128)S(1)} collective-permute-done((f32[2560,128]{1,0:T(8,128)S(1)}, f32[2560,128]{1,0:T(8,128)S(1)}, u32[]{:S(2)}, u32[]{:S(2)}) %collective-permute-start.13) | collective-permute-done | bytes 1310752 | tf_op jit(solution)/shard_map/ppermute | solution.py:368
  161.1 2.5 %collective-permute-start.16 = (f32[2560,128]{1,0:T(8,128)S(1)}, f32[2560,128]{1,0:T(8,128)S(1)}, u32[]{:S(2)}, u32[]{:S(2)}) collective-permute-start(f32[2560,128]{1,0:T(8,128)S(1)} %broadcast_select_fusion.3.mine_ref), channel_id=1, source_target_pairs={{0,1},{1,0},{2,3},{3,2},{4,5},{5,4},{6,7},{7,6},{8,9},{9,8},{10,11... | collective-permute-start | bytes 3932168 | tf_op jit(solution)/shard_map/ppermute | solution.py:404
  163.5 27.0 %shard_map.20.refs_0_ = f32[5120,2560]{1,0:T(8,128)} custom-call(s32[4]{0:T(128)S(1)} %pad_add_fusion.info_ref, f32[5120,2560]{1,0:T(8,128)} %mat_ref.5, bf16[768,2560]{1,0:T(8,128)(2,1)S(1)} %shard_map.18.right_ref, f32[256,256]{1,0:T(8,128)S(1)} %get-tuple-element.16.lower_ref, ...), custom_call_target="tpu_custom_call", output_to_operand_aliasing={{}: (7, {})} | custom-call | flops 7549747200 | bytes 39321600 | tf_op jit(solution)/shard_map/pallas_call | solution.py:291
  190.5 25.0 %shard_map.21 = f32[5120,2560]{1,0:T(8,128)} custom-call(s32[4]{0:T(128)S(1)} %pad_add_fusion.info_ref, f32[5120,2560]{1,0:T(8,128)} %mat_ref.5, bf16[768,2560]{1,0:T(8,128)(2,1)S(1)} %shard_map.18.right_ref, f32[256,256]{1,0:T(8,128)S(1)} %get-tuple-element.16.lower_ref, ...), custom_call_target="tpu_custom_call", output_to_operand_aliasing={{}: (7, {})} | custom-call | flops 10066329600 | bytes 52428800 | tf_op jit(solution)/shard_map/pallas_call | solution.py:291
  (22 shorter events, 1.4 us)
Async XLA Ops:
  0.8 2.0 collective-permute-start
  1.5 1.4 collective-permute-start.1
  2.2 0.7 collective-permute-start.2
  3.8 10.3 %collective-permute-start.3 = (f32[256,128]{1,0:T(8,128)S(1)}, f32[256,128]{1,0:T(8,128)S(1)}, u32[]{:S(2)}, u32[]{:S(2)}) collective-permute-start(f32[256,128]{1,0:T(8,128)S(1)} %pad_maximum_fusion.1), channel_id=1, source_target_pairs={{0,1},{1,0},{8,9},{9,8},{16,17},{17,16},{24,25},{25,24}} | collective-permute-start | bytes 393224 | tf_op jit(solution)/shard_map/ppermute | solution.py:351
  6.4 51.0 %collective-permute-start.11 = (f32[2560,128]{1,0:T(8,128)S(1)}, f32[2560,128]{1,0:T(8,128)}, u32[]{:S(2)}, u32[]{:S(2)}) collective-permute-start(f32[2560,128]{1,0:T(8,128)S(1)} %get-tuple-element.25), channel_id=1, source_target_pairs={{0,4},{1,5},{8,12},{9,13},{16,20},{17,21},{24,28},{25,29}} | collective-permute-start | bytes 3932168 | tf_op jit(solution)/shard_map/ppermute | solution.py:368
  10.1 42.2 %collective-permute-start.9 = (f32[128,1280]{1,0:T(8,128)}, f32[128,1280]{1,0:T(8,128)}, u32[]{:S(2)}, u32[]{:S(2)}) collective-permute-start(f32[128,1280]{1,0:T(8,128)} %slice.17), channel_id=1, source_target_pairs={{0,16},{8,24},{1,17},{9,25},{2,18},{10,26},{3,19},{11,27},{4,20},{... | collective-permute-start | bytes 1966088 | tf_op jit(solution)/shard_map/ppermute | solution.py:322
  14.1 38.1 %collective-permute-start.4 = (f32[256,256]{1,0:T(8,128)S(1)}, f32[256,256]{1,0:T(8,128)S(1)}, u32[]{:S(2)}, u32[]{:S(2)}) collective-permute-start(f32[256,256]{1,0:T(8,128)S(1)} %pad_maximum_fusion), channel_id=1, source_target_pairs={{0,6},{1,7},{8,14},{9,15},{16,22},{17,23},{24,30},{25,31}} | collective-permute-start | bytes 786440 | tf_op jit(solution)/shard_map/ppermute | solution.py:358
  15.4 36.8 %collective-permute-start.5 = (f32[256,256]{1,0:T(8,128)S(1)}, f32[256,256]{1,0:T(8,128)}, u32[]{:S(2)}, u32[]{:S(2)}) collective-permute-start(f32[256,256]{1,0:T(8,128)S(1)} %pad_maximum_fusion), channel_id=1, source_target_pairs={{0,4},{1,5},{8,12},{9,13},{16,20},{17,21},{24,28},{25,29}} | collective-permute-start | bytes 786440 | tf_op jit(solution)/shard_map/ppermute | solution.py:358
  16.8 35.4 %collective-permute-start.6 = (f32[256,256]{1,0:T(8,128)S(1)}, f32[256,256]{1,0:T(8,128)}, u32[]{:S(2)}, u32[]{:S(2)}) collective-permute-start(f32[256,256]{1,0:T(8,128)S(1)} %pad_maximum_fusion), channel_id=1, source_target_pairs={{0,2},{1,3},{8,10},{9,11},{16,18},{17,19},{24,26},{25,27}} | collective-permute-start | bytes 786440 | tf_op jit(solution)/shard_map/ppermute | solution.py:358
  53.7 16.9 %collective-permute-start.7 = (f32[128,1280]{1,0:T(8,128)S(1)}, f32[128,1280]{1,0:T(8,128)S(1)}, u32[]{:S(2)}, u32[]{:S(2)}) collective-permute-start(f32[128,1280]{1,0:T(8,128)S(1)} %get-tuple-element.28), channel_id=1, source_target_pairs={{0,16},{8,24},{1,17},{9,25},{2,18},{10,26},{3,19},{11,27},{4,20},{... | collective-permute-start | bytes 1966088 | tf_op jit(solution)/shard_map/ppermute | solution.py:322
  58.6 37.9 %collective-permute-start.14 = (f32[2560,128]{1,0:T(8,128)}, f32[2560,128]{1,0:T(8,128)}, u32[]{:S(2)}, u32[]{:S(2)}) collective-permute-start(f32[2560,128]{1,0:T(8,128)} %broadcast_select_fusion.1), channel_id=1, source_target_pairs={{0,2},{1,3},{4,6},{5,7},{8,10},{9,11},{12,14},{13,15},{16,18},{17,... | collective-permute-start | bytes 3932168 | tf_op jit(solution)/shard_map/ppermute | solution.py:368
  71.8 14.7 %collective-permute-start.8 = (f32[128,1280]{1,0:T(8,128)S(1)}, f32[128,1280]{1,0:T(8,128)S(1)}, u32[]{:S(2)}, u32[]{:S(2)}) collective-permute-start(f32[128,1280]{1,0:T(8,128)S(1)} %broadcast_select_fusion.5.refs_0_), channel_id=1, source_target_pairs={{0,8},{8,0},{16,24},{24,16},{1,9},{9,1},{17,25},{25,17},{2,10},{10... | collective-permute-start | bytes 1966088 | tf_op jit(solution)/shard_map/ppermute | solution.py:329
  71.9 30.7 %collective-permute-start.12 = (f32[2560,128]{1,0:T(8,128)S(1)}, f32[2560,128]{1,0:T(8,128)}, u32[]{:S(2)}, u32[]{:S(2)}) collective-permute-start(f32[2560,128]{1,0:T(8,128)S(1)} %get-tuple-element.18), channel_id=1, source_target_pairs={{0,4},{1,5},{8,12},{9,13},{16,20},{17,21},{24,28},{25,29}} | collective-permute-start | bytes 3932168 | tf_op jit(solution)/shard_map/ppermute | solution.py:368
  73.6 29.1 %collective-permute-start.10 = (f32[128,1280]{1,0:T(8,128)S(1)}, f32[128,1280]{1,0:T(8,128)S(1)}, u32[]{:S(2)}, u32[]{:S(2)}) collective-permute-start(f32[128,1280]{1,0:T(8,128)S(1)} %get-tuple-element.27.refs_2_), channel_id=1, source_target_pairs={{0,8},{8,0},{16,24},{24,16},{1,9},{9,1},{17,25},{25,17},{2,10},{10... | collective-permute-start | bytes 1966088 | tf_op jit(solution)/shard_map/ppermute | solution.py:329
  98.0 8.2 %collective-permute-start.15 = (f32[2560,128]{1,0:T(8,128)S(1)}, f32[2560,128]{1,0:T(8,128)S(1)}, u32[]{:S(2)}, u32[]{:S(2)}) collective-permute-start(f32[2560,128]{1,0:T(8,128)S(1)} %broadcast_select_fusion.2.mine_ref), channel_id=1, source_target_pairs={{0,1},{1,0},{2,3},{3,2},{4,5},{5,4},{6,7},{7,6},{8,9},{9,8},{10,11... | collective-permute-start | bytes 3932168 | tf_op jit(solution)/shard_map/ppermute | solution.py:399
  102.7 58.2 %collective-permute-start.13 = (f32[2560,128]{1,0:T(8,128)S(1)}, f32[2560,128]{1,0:T(8,128)S(1)}, u32[]{:S(2)}, u32[]{:S(2)}) collective-permute-start(f32[2560,128]{1,0:T(8,128)S(1)} %broadcast_select_fusion), channel_id=1, source_target_pairs={{0,2},{1,3},{4,6},{5,7},{8,10},{9,11},{12,14},{13,15},{16,18},{17,... | collective-permute-start | bytes 3932168 | tf_op jit(solution)/shard_map/ppermute | solution.py:368
  161.1 29.5 %collective-permute-start.16 = (f32[2560,128]{1,0:T(8,128)S(1)}, f32[2560,128]{1,0:T(8,128)S(1)}, u32[]{:S(2)}, u32[]{:S(2)}) collective-permute-start(f32[2560,128]{1,0:T(8,128)S(1)} %broadcast_select_fusion.3.mine_ref), channel_id=1, source_target_pairs={{0,1},{1,0},{2,3},{3,2},{4,5},{5,4},{6,7},{7,6},{8,9},{9,8},{10,11... | collective-permute-start | bytes 3932168 | tf_op jit(solution)/shard_map/ppermute | solution.py:404

commit v3 on v2

--- a/solution.py
+++ b/solution.py
@@ -356,20 +356,7 @@
     for shift in range(1, depth):
         pairs = [(c, c + CORES * shift) for c in range(CORES)]
         got.append(lax.ppermute(square, "col", pairs))
-    return pick(got, place)
-
-
-def spread_columns(block, place, col_count, between):
-    stride = col_count // CORES // 2
-    levels = []
-    while stride > 0:
-        block = after(block, *between[len(levels)])
-        pairs = [(c, c + CORES * stride) for c in range(col_count) if c // CORES % (2 * stride) == 0]
-        got = lax.ppermute(block, "col", pairs)
-        block = jnp.where(place % (2 * stride) == stride, got, block)
-        levels.append(block)
-        stride //= 2
-    return levels
+    return column, pick(got, place)
 
 
 def per_device(matrix):
@@ -377,33 +364,60 @@
     col_count = lax.axis_size("col")
     row = lax.axis_index("row")
     col = lax.axis_index("col")
+    depth = col_count // CORES
     place, core = col // CORES, col % CORES
     info = jnp.stack([row, place, core, col]).astype(jnp.int32)
     tiles = matrix.shape[0] // TILE
-    cut = tiles // 4 * 2 * TILE
+    chunks = next(n for n in (5, 4, 2, 1) if tiles % n == 0)
+    rows = tiles // chunks * TILE
     half = matrix.shape[1] // 2
 
-    bands = [matrix[:TILE, :half], matrix[:TILE, half:]]
+    column, corner = share_corner(matrix, row, place, core, row_count, col_count)
+    bands = [after(matrix[:TILE, :half], column), after(matrix[:TILE, half:], column)]
     bands = [double_rows(band, row, row_count) for band in bands]
-    corner = share_corner(matrix, row, place, core, row_count, col_count)
-    between = [()] + [(corner,)] * col_count
-    first = spread_columns(matrix[:cut, :TILE], place, col_count, between)
+
+    last = chunks + depth - 2
+    held, got = [], None
+
+    def fill(slot, *earlier):
+        if slot < chunks:
+            own = matrix[slot * rows : (slot + 1) * rows, :TILE]
+            block = own if got is None else jnp.where(place == 0, own, got)
+        else:
+            block = got
+        block = after(block, *earlier)
+        held.append(block)
+        if slot == last:
+            return None
+        busy = [c for c in range(col_count) if 0 <= slot - c // CORES < chunks]
+        hops = [(c, c + CORES) for c in busy if c + CORES < col_count]
+        return lax.ppermute(block, "col", hops)
+
+    got = fill(0)
+    got = fill(1, corner)
+    got = fill(2, bands[0])
+    lower, inverse, inv_t = factor_corner(after(corner, held[2]))
     besides = [swap_rows(band, row_count) for band in bands]
-    lower, inverse, inv_t = factor_corner(after(corner, besides[0], bands[1]))
-    between = [(first[0],)] + [(inverse, besides[1])] * col_count
-    second = spread_columns(matrix[cut:, :TILE], place, col_count, between)
-    right = solve_columns(info, inverse, list(zip(bands, besides)))
-
-    swap = [(c, c ^ 1) for c in range(col_count)]
-    mine = first[-1]
-    other = after(lax.ppermute(mine, "col", swap), *second[:-1])
-    early = tiles // 8 * TILE
-    shared = (info, matrix, right, lower, inv_t)
-    out = update_rows(0, early, 0, *shared, mine, other, None)
-    late_mine = second[-1]
-    late_other = lax.ppermute(after(late_mine, out), "col", swap)
-    out = update_rows(early, cut, 0, *shared, mine, other, out)
-    return update_rows(cut, tiles * TILE, cut, *shared, late_mine, late_other, out)
+    slot = 3
+    while slot < depth:
+        got = fill(slot, inverse, bands[1], besides[0])
+        slot += 1
+    right = None
+    out = None
+    for chunk in range(chunks):
+        mine = pick(held[chunk : chunk + depth], place)
+        other = lax.ppermute(mine, "col", [(c, c ^ 1) for c in range(col_count)])
+        if slot <= last:
+            got = fill(slot) if out is None else fill(slot, out)
+            slot += 1
+        if right is None:
+            right = solve_columns(info, inverse, list(zip(bands, besides)))
+        other = after(other, held[-1])
+        first = chunk * rows
+        out = update_rows(
+            first, first + rows, first, info, matrix, right, lower, inv_t, mine, other, out
+        )
+    return out
 
 
 def solution(mesh):

time: 216 us -> 170 us (0.79)
  waiting for transfers between devices: 100 us -> 57.7 us
  Pallas kernels: 74.6 us -> 72.2 us
    ppermute x3, waiting for transfers between devices: 34.1 us -> 19.7 us  [share_corner(): got.append(lax.ppermute(square, 'col', pairs))]
    ppermute x6 -> x12, waiting for transfers between devices: 44 us -> 30.2 us  [the longest x7 30.1 us: fill(): return lax.ppermute(block, 'col', hops)]
    ppermute x2, waiting for transfers between devices: 11.5 us -> 0.01 us  [swap_rows(): return lax.ppermute(block, 'row', [(i, i ^ 1) for i in range(row_count)])]
    ppermute x2, waiting for transfers between devices: 10.7 us -> 7.76 us  [double_rows(): got = lax.ppermute(block, 'row', pairs)]
    select_n x2, other arithmetic: 2.58 us -> 0.15 us  [double_rows(): jnp.where(jnp.logical_and(row >= stride, row < 2 * stride), got, block)]
    pallas_call x3 -> x5, Pallas kernels: 62.8 us -> 60.5 us  [update_rows(): pl.pallas_call(functools.partial(update_kernel, start, rows, start - base...]
    ppermute x6 -> x12, starting transfers between devices: 13.3 us -> 12.6 us  [the longest x7 8.01 us: fill(): return lax.ppermute(block, 'col', hops)]
  transfers between devices with their start and end apart: 17 -> 23, of which waited for: 5 -> 7; matrix products, arithmetic and copies ran while one was open for 4% -> 5% of each run, Pallas kernels for 23% -> 36%
where the time goes in v3:
time: 170 us; the launch traced here: 169 us
  Pallas kernels  72.2 us (42%)
  waiting for transfers between devices  57.7 us (34%)
  starting transfers between devices  28.1 us (17%)
  other arithmetic  6.95 us (4%)
  local copies, waits for them, and re-layouts  3.29 us (2%)
    pallas_call x5, Pallas kernels, update_rows(): pl.pallas_call(functools.partial(update_kernel, start, rows, start - base...  60.5 us
    ppermute x7, waiting for transfers between devices, fill(): return lax.ppermute(block, 'col', hops)  30.1 us
    ppermute x3, waiting for transfers between devices, share_corner(): got.append(lax.ppermute(square, 'col', pairs))  19.7 us
    pallas_call x1, Pallas kernels, factor_corner(): pl.pallas_call(corner_kernel, out_shape=(jax.ShapeDtypeStruct((WIDE, WIDE...  9.83 us
    ppermute x7, starting transfers between devices, fill(): return lax.ppermute(block, 'col', hops)  8.01 us
    ppermute x2, waiting for transfers between devices, double_rows(): got = lax.ppermute(block, 'row', pairs)  7.76 us
    ppermute x2, starting transfers between devices, double_rows(): got = lax.ppermute(block, 'row', pairs)  6.65 us
    ppermute x5, starting transfers between devices, per_device(): other = lax.ppermute(mine, 'col', [(c, c ^ 1) for c in range(col_count)])  4.57 us
  transfers between devices with their start and end apart: 23, of which 7 were waited for; matrix products, arithmetic and copies ran while one was open for 5% of the time, Pallas kernels for 36%

profile of v3, /device:TPU:25, one launch (start us, length us, event | category | flops | bytes accessed | tf_op | source)
XLA Modules:
  0.0 168.8 jit_solution(9614264178850612225)
XLA Ops:
  4.5 1.1 slice.27
  6.3 1.3 collective-permute-start.4
  7.6 1.4 collective-permute-start.5
  9.0 1.4 collective-permute-start.6
  10.4 1.4 fusion
  11.8 3.2 %collective-permute-start.9 = (f32[128,1280]{1,0:T(8,128)S(1)}, f32[128,1280]{1,0:T(8,128)S(1)}, u32[]{:S(2)}, u32[]{:S(2)}) collective-permute-start(f32[128,1280]{1,0:T(8,128)S(1)} %get-tuple-element.23), channel_id=1, source_target_pairs={{0,16},{8,24},{1,17},{9,25},{2,18},{10,26},{3,19},{11,27},{4,20},{... | collective-permute-start | bytes 1966088 | tf_op jit(solution)/shard_map/ppermute | solution.py:322
  15.0 19.7 %collective-permute-done.4 = f32[256,256]{1,0:T(8,128)} collective-permute-done((f32[256,256]{1,0:T(8,128)S(1)}, f32[256,256]{1,0:T(8,128)}, u32[]{:S(2)}, u32[]{:S(2)}) %collective-permute-start.4) | collective-permute-done | bytes 262176 | tf_op jit(solution)/shard_map/ppermute | solution.py:358
  34.6 3.5 %collective-permute-start.11 = (f32[128,1280]{1,0:T(8,128)S(1)}, f32[128,1280]{1,0:T(8,128)S(1)}, u32[]{:S(2)}, u32[]{:S(2)}) collective-permute-start(f32[128,1280]{1,0:T(8,128)S(1)} %get-tuple-element.27), channel_id=1, source_target_pairs={{0,16},{8,24},{1,17},{9,25},{2,18},{10,26},{3,19},{11,27},{4,20},{... | collective-permute-start | bytes 1966088 | tf_op jit(solution)/shard_map/ppermute | solution.py:322
  38.1 1.0 select_select_fusion.5.corner_ref
  39.2 1.1 slice_select_fusion.2
  41.1 1.1 slice_select_fusion.3
  42.3 1.3 collective-permute-start.13
  43.6 7.8 %collective-permute-done.11 = f32[128,1280]{1,0:T(8,128)S(1)} collective-permute-done((f32[128,1280]{1,0:T(8,128)S(1)}, f32[128,1280]{1,0:T(8,128)S(1)}, u32[]{:S(2)}, u32[]{:S(2)}) %collective-permute-start.11) | collective-permute-done | bytes 655392 | tf_op jit(solution)/shard_map/ppermute | solution.py:322
  51.4 9.8 %shard_map.17 = (f32[256,256]{1,0:T(8,128)S(1)}, bf16[256,768]{1,0:T(8,128)(2,1)S(1)}, bf16[768,256]{1,0:T(8,128)(2,1)S(1)}) custom-call(f32[256,256]{1,0:T(8,128)S(1)} %select_select_fusion.5.corner_ref), custom_call_target="tpu_custom_call" | custom-call | flops 40000000 | bytes 1048576 | tf_op jit(solution)/shard_map/pallas_call | solution.py:132
  61.2 15.1 %collective-permute-done.13 = f32[1024,128]{1,0:T(8,128)S(1)} collective-permute-done((f32[1024,128]{1,0:T(8,128)S(1)}, f32[1024,128]{1,0:T(8,128)S(1)}, u32[]{:S(2)}, u32[]{:S(2)}) %collective-permute-start.13) | collective-permute-done | bytes 524320 | tf_op jit(solution)/shard_map/ppermute | solution.py:394
  76.4 1.1 slice_select_fusion
  77.5 1.3 collective-permute-start.14
  78.8 2.1 %collective-permute-start.12 = (f32[128,1280]{1,0:T(8,128)S(1)}, f32[128,1280]{1,0:T(8,128)S(1)}, u32[]{:S(2)}, u32[]{:S(2)}) collective-permute-start(f32[128,1280]{1,0:T(8,128)S(1)} %broadcast_select_fusion.refs_2_), channel_id=1, source_target_pairs={{0,8},{8,0},{16,24},{24,16},{1,9},{9,1},{17,25},{25,17},{2,10},{10... | collective-permute-start | bytes 1966088 | tf_op jit(solution)/shard_map/ppermute | solution.py:329
  80.9 10.1 %collective-permute-done.14 = f32[1024,128]{1,0:T(8,128)S(1)} collective-permute-done((f32[1024,128]{1,0:T(8,128)S(1)}, f32[1024,128]{1,0:T(8,128)S(1)}, u32[]{:S(2)}, u32[]{:S(2)}) %collective-permute-start.14) | collective-permute-done | bytes 524320 | tf_op jit(solution)/shard_map/ppermute | solution.py:394
  91.0 1.1 slice_select_fusion.1
  92.3 2.7 %collective-permute-start.16 = (f32[1024,128]{1,0:T(8,128)S(1)}, f32[1024,128]{1,0:T(8,128)S(1)}, u32[]{:S(2)}, u32[]{:S(2)}) collective-permute-start(f32[1024,128]{1,0:T(8,128)S(1)} %get-tuple-element.46.mine_ref), channel_id=1, source_target_pairs={{0,1},{1,0},{2,3},{3,2},{4,5},{5,4},{6,7},{7,6},{8,9},{9,8},{10,11... | collective-permute-start | bytes 1572872 | tf_op jit(solution)/shard_map/ppermute | solution.py:409
  95.0 1.5 collective-permute-start.15
  96.6 1.9 %shard_map.18.right_ref = bf16[768,2560]{1,0:T(8,128)(2,1)S(1)} custom-call(s32[4]{0:T(128)S(1)} %pad_add_fusion.info_ref, bf16[256,768]{1,0:T(8,128)(2,1)S(1)} %get-tuple-element.26.inv_ref, f32[128,1280]{1,0:T(8,128)S(1)} %broadcast_select_fusion.1.refs_0_, f32[128,1280]{1,0:T(8,128)S(1)} %collective-permute-done.10.refs_1_, ...), custom_call_target="tpu_custom_call" | custom-call | flops 1006632960 | bytes 5242880 | tf_op jit(solution)/shard_map/pallas_call | solution.py:163
  98.6 12.2 %shard_map.19.refs_0_ = f32[5120,2560]{1,0:T(8,128)} custom-call(s32[4]{0:T(128)S(1)} %pad_add_fusion.info_ref, f32[5120,2560]{1,0:T(8,128)} %mat_ref.9, bf16[768,2560]{1,0:T(8,128)(2,1)S(1)} %shard_map.18.right_ref, f32[256,256]{1,0:T(8,128)S(1)} %get-tuple-element.28.lower_ref, bf16[768,256]{1,0:T(8,128)(2,1)S(1)} %get-tuple-element.29.inv_t_ref, ...), custom_call_target="tpu_custom_call" | custom-call | flops 4026531840 | bytes 20971520 | tf_op jit(solution)/shard_map/pallas_call | solution.py:291
  110.8 1.3 collective-permute-start.17
  112.1 12.1 %shard_map.20.refs_0_ = f32[5120,2560]{1,0:T(8,128)} custom-call(s32[4]{0:T(128)S(1)} %pad_add_fusion.info_ref, f32[5120,2560]{1,0:T(8,128)} %mat_ref.9, bf16[768,2560]{1,0:T(8,128)(2,1)S(1)} %shard_map.18.right_ref, f32[256,256]{1,0:T(8,128)S(1)} %get-tuple-element.28.lower_ref, ...), custom_call_target="tpu_custom_call", output_to_operand_aliasing={{}: (7, {})} | custom-call | flops 4026531840 | bytes 20971520 | tf_op jit(solution)/shard_map/pallas_call | solution.py:291
  124.2 3.0 %collective-permute-done.17 = f32[1024,128]{1,0:T(8,128)S(1)} collective-permute-done((f32[1024,128]{1,0:T(8,128)S(1)}, f32[1024,128]{1,0:T(8,128)S(1)}, u32[]{:S(2)}, u32[]{:S(2)}) %collective-permute-start.17) | collective-permute-done | bytes 524320 | tf_op jit(solution)/shard_map/ppermute | solution.py:394
  128.1 1.3 collective-permute-start.19
  129.7 12.1 %shard_map.21.refs_0_ = f32[5120,2560]{1,0:T(8,128)} custom-call(s32[4]{0:T(128)S(1)} %pad_add_fusion.info_ref, f32[5120,2560]{1,0:T(8,128)} %mat_ref.9, bf16[768,2560]{1,0:T(8,128)(2,1)S(1)} %shard_map.18.right_ref, f32[256,256]{1,0:T(8,128)S(1)} %get-tuple-element.28.lower_ref, ...), custom_call_target="tpu_custom_call", output_to_operand_aliasing={{}: (7, {})} | custom-call | flops 4026531840 | bytes 20971520 | tf_op jit(solution)/shard_map/pallas_call | solution.py:291
  141.7 1.8 %collective-permute-done.19 = f32[1024,128]{1,0:T(8,128)S(1)} collective-permute-done((f32[1024,128]{1,0:T(8,128)S(1)}, f32[1024,128]{1,0:T(8,128)S(1)}, u32[]{:S(2)}, u32[]{:S(2)}) %collective-permute-start.19) | collective-permute-done | bytes 524320 | tf_op jit(solution)/shard_map/ppermute | solution.py:394
  144.5 12.1 %shard_map.22.refs_0_ = f32[5120,2560]{1,0:T(8,128)} custom-call(s32[4]{0:T(128)S(1)} %pad_add_fusion.info_ref, f32[5120,2560]{1,0:T(8,128)} %mat_ref.9, bf16[768,2560]{1,0:T(8,128)(2,1)S(1)} %shard_map.18.right_ref, f32[256,256]{1,0:T(8,128)S(1)} %get-tuple-element.28.lower_ref, ...), custom_call_target="tpu_custom_call", output_to_operand_aliasing={{}: (7, {})} | custom-call | flops 4026531840 | bytes 20971520 | tf_op jit(solution)/shard_map/pallas_call | solution.py:291
  156.6 12.1 %shard_map.23 = f32[5120,2560]{1,0:T(8,128)} custom-call(s32[4]{0:T(128)S(1)} %pad_add_fusion.info_ref, f32[5120,2560]{1,0:T(8,128)} %mat_ref.9, bf16[768,2560]{1,0:T(8,128)(2,1)S(1)} %shard_map.18.right_ref, f32[256,256]{1,0:T(8,128)S(1)} %get-tuple-element.28.lower_ref, ...), custom_call_target="tpu_custom_call", output_to_operand_aliasing={{}: (7, {})} | custom-call | flops 4026531840 | bytes 20971520 | tf_op jit(solution)/shard_map/pallas_call | solution.py:291
  (39 shorter events, 8.5 us)
Async XLA Ops:
  0.8 2.0 %collective-permute-start = (f32[128,128]{1,0:T(8,128)S(1)}, f32[128,128]{1,0:T(8,128)S(1)}, u32[]{:S(2)}, u32[]{:S(2)}) collective-permute-start(f32[128,128]{1,0:T(8,128)S(1)} %slice.24), channel_id=1, source_target_pairs={{0,24},{1,25},{8,0},{9,1}} | collective-permute-start | bytes 196616 | tf_op jit(solution)/shard_map/ppermute | solution.py:349
  1.5 1.4 collective-permute-start.1
  2.2 0.7 collective-permute-start.2
  3.8 2.5 %collective-permute-start.3 = (f32[256,128]{1,0:T(8,128)S(1)}, f32[256,128]{1,0:T(8,128)S(1)}, u32[]{:S(2)}, u32[]{:S(2)}) collective-permute-start(f32[256,128]{1,0:T(8,128)S(1)} %pad_maximum_fusion.1), channel_id=1, source_target_pairs={{0,1},{1,0},{8,9},{9,8},{16,17},{17,16},{24,25},{25,24}} | collective-permute-start | bytes 393224 | tf_op jit(solution)/shard_map/ppermute | solution.py:351
  5.6 33.6 %collective-permute-start.7 = (f32[1024,128]{1,0:T(8,128)S(1)}, f32[1024,128]{1,0:T(8,128)S(1)}, u32[]{:S(2)}, u32[]{:S(2)}) collective-permute-start(f32[1024,128]{1,0:T(8,128)S(1)} %slice.27), channel_id=1, source_target_pairs={{0,2},{1,3},{8,10},{9,11},{16,18},{17,19},{24,26},{25,27}} | collective-permute-start | bytes 1572872 | tf_op jit(solution)/shard_map/ppermute | solution.py:394
  6.3 28.3 %collective-permute-start.4 = (f32[256,256]{1,0:T(8,128)S(1)}, f32[256,256]{1,0:T(8,128)}, u32[]{:S(2)}, u32[]{:S(2)}) collective-permute-start(f32[256,256]{1,0:T(8,128)S(1)} %pad_maximum_fusion), channel_id=1, source_target_pairs={{0,6},{1,7},{8,14},{9,15},{16,22},{17,23},{24,30},{25,31}} | collective-permute-start | bytes 786440 | tf_op jit(solution)/shard_map/ppermute | solution.py:358
  7.6 30.5 %collective-permute-start.5 = (f32[256,256]{1,0:T(8,128)S(1)}, f32[256,256]{1,0:T(8,128)}, u32[]{:S(2)}, u32[]{:S(2)}) collective-permute-start(f32[256,256]{1,0:T(8,128)S(1)} %pad_maximum_fusion), channel_id=1, source_target_pairs={{0,4},{1,5},{8,12},{9,13},{16,20},{17,21},{24,28},{25,29}} | collective-permute-start | bytes 786440 | tf_op jit(solution)/shard_map/ppermute | solution.py:358
  9.0 29.1 %collective-permute-start.6 = (f32[256,256]{1,0:T(8,128)S(1)}, f32[256,256]{1,0:T(8,128)}, u32[]{:S(2)}, u32[]{:S(2)}) collective-permute-start(f32[256,256]{1,0:T(8,128)S(1)} %pad_maximum_fusion), channel_id=1, source_target_pairs={{0,2},{1,3},{8,10},{9,11},{16,18},{17,19},{24,26},{25,27}} | collective-permute-start | bytes 786440 | tf_op jit(solution)/shard_map/ppermute | solution.py:358
  11.8 29.2 %collective-permute-start.9 = (f32[128,1280]{1,0:T(8,128)S(1)}, f32[128,1280]{1,0:T(8,128)S(1)}, u32[]{:S(2)}, u32[]{:S(2)}) collective-permute-start(f32[128,1280]{1,0:T(8,128)S(1)} %get-tuple-element.23), channel_id=1, source_target_pairs={{0,16},{8,24},{1,17},{9,25},{2,18},{10,26},{3,19},{11,27},{4,20},{... | collective-permute-start | bytes 1966088 | tf_op jit(solution)/shard_map/ppermute | solution.py:322
  34.6 16.7 %collective-permute-start.11 = (f32[128,1280]{1,0:T(8,128)S(1)}, f32[128,1280]{1,0:T(8,128)S(1)}, u32[]{:S(2)}, u32[]{:S(2)}) collective-permute-start(f32[128,1280]{1,0:T(8,128)S(1)} %get-tuple-element.27), channel_id=1, source_target_pairs={{0,16},{8,24},{1,17},{9,25},{2,18},{10,26},{3,19},{11,27},{4,20},{... | collective-permute-start | bytes 1966088 | tf_op jit(solution)/shard_map/ppermute | solution.py:322
  40.3 0.9 collective-permute-start.8
  41.1 36.4 %collective-permute-start.10 = (f32[128,1280]{1,0:T(8,128)S(1)}, f32[128,1280]{1,0:T(8,128)S(1)}, u32[]{:S(2)}, u32[]{:S(2)}) collective-permute-start(f32[128,1280]{1,0:T(8,128)S(1)} %broadcast_select_fusion.1.refs_0_), channel_id=1, source_target_pairs={{0,8},{8,0},{16,24},{24,16},{1,9},{9,1},{17,25},{25,17},{2,10},{10... | collective-permute-start | bytes 1966088 | tf_op jit(solution)/shard_map/ppermute | solution.py:329
  42.3 34.1 %collective-permute-start.13 = (f32[1024,128]{1,0:T(8,128)S(1)}, f32[1024,128]{1,0:T(8,128)S(1)}, u32[]{:S(2)}, u32[]{:S(2)}) collective-permute-start(f32[1024,128]{1,0:T(8,128)S(1)} %slice_select_fusion.3), channel_id=1, source_target_pairs={{0,2},{1,3},{2,4},{3,5},{4,6},{5,7},{8,10},{9,11},{10,12},{11,13},... | collective-permute-start | bytes 1572872 | tf_op jit(solution)/shard_map/ppermute | solution.py:394
  77.5 13.6 %collective-permute-start.14 = (f32[1024,128]{1,0:T(8,128)S(1)}, f32[1024,128]{1,0:T(8,128)S(1)}, u32[]{:S(2)}, u32[]{:S(2)}) collective-permute-start(f32[1024,128]{1,0:T(8,128)S(1)} %slice_select_fusion), channel_id=1, source_target_pairs={{0,2},{1,3},{2,4},{3,5},{4,6},{5,7},{8,10},{9,11},{10,12},{11,13},... | collective-permute-start | bytes 1572872 | tf_op jit(solution)/shard_map/ppermute | solution.py:394
  78.8 17.8 %collective-permute-start.12 = (f32[128,1280]{1,0:T(8,128)S(1)}, f32[128,1280]{1,0:T(8,128)S(1)}, u32[]{:S(2)}, u32[]{:S(2)}) collective-permute-start(f32[128,1280]{1,0:T(8,128)S(1)} %broadcast_select_fusion.refs_2_), channel_id=1, source_target_pairs={{0,8},{8,0},{16,24},{24,16},{1,9},{9,1},{17,25},{25,17},{2,10},{10... | collective-permute-start | bytes 1966088 | tf_op jit(solution)/shard_map/ppermute | solution.py:329
  92.3 6.3 %collective-permute-start.16 = (f32[1024,128]{1,0:T(8,128)S(1)}, f32[1024,128]{1,0:T(8,128)S(1)}, u32[]{:S(2)}, u32[]{:S(2)}) collective-permute-start(f32[1024,128]{1,0:T(8,128)S(1)} %get-tuple-element.46.mine_ref), channel_id=1, source_target_pairs={{0,1},{1,0},{2,3},{3,2},{4,5},{5,4},{6,7},{7,6},{8,9},{9,8},{10,11... | collective-permute-start | bytes 1572872 | tf_op jit(solution)/shard_map/ppermute | solution.py:409
  95.0 15.8 %collective-permute-start.15 = (f32[1024,128]{1,0:T(8,128)S(1)}, f32[1024,128]{1,0:T(8,128)S(1)}, u32[]{:S(2)}, u32[]{:S(2)}) collective-permute-start(f32[1024,128]{1,0:T(8,128)S(1)} %slice_select_fusion.1), channel_id=1, source_target_pairs={{0,2},{1,3},{2,4},{3,5},{4,6},{5,7},{8,10},{9,11},{10,12},{11,13},... | collective-permute-start | bytes 1572872 | tf_op jit(solution)/shard_map/ppermute | solution.py:394
  98.5 13.6 %collective-permute-start.18 = (f32[1024,128]{1,0:T(8,128)S(1)}, f32[1024,128]{1,0:T(8,128)S(1)}, u32[]{:S(2)}, u32[]{:S(2)}) collective-permute-start(f32[1024,128]{1,0:T(8,128)S(1)} %get-tuple-element.45.mine_ref), channel_id=1, source_target_pairs={{0,1},{1,0},{2,3},{3,2},{4,5},{5,4},{6,7},{7,6},{8,9},{9,8},{10,11... | collective-permute-start | bytes 1572872 | tf_op jit(solution)/shard_map/ppermute | solution.py:409
  110.8 16.4 %collective-permute-start.17 = (f32[1024,128]{1,0:T(8,128)S(1)}, f32[1024,128]{1,0:T(8,128)S(1)}, u32[]{:S(2)}, u32[]{:S(2)}) collective-permute-start(f32[1024,128]{1,0:T(8,128)S(1)} %collective-permute-done.15), channel_id=1, source_target_pairs={{2,4},{3,5},{4,6},{5,7},{10,12},{11,13},{12,14},{13,15},{18,20},{1... | collective-permute-start | bytes 1572872 | tf_op jit(solution)/shard_map/ppermute | solution.py:394
  127.3 2.3 %collective-permute-start.20 = (f32[1024,128]{1,0:T(8,128)S(1)}, f32[1024,128]{1,0:T(8,128)S(1)}, u32[]{:S(2)}, u32[]{:S(2)}) collective-permute-start(f32[1024,128]{1,0:T(8,128)S(1)} %get-tuple-element.44.mine_ref), channel_id=1, source_target_pairs={{0,1},{1,0},{2,3},{3,2},{4,5},{5,4},{6,7},{7,6},{8,9},{9,8},{10,11... | collective-permute-start | bytes 1572872 | tf_op jit(solution)/shard_map/ppermute | solution.py:409
  128.1 15.4 %collective-permute-start.19 = (f32[1024,128]{1,0:T(8,128)S(1)}, f32[1024,128]{1,0:T(8,128)S(1)}, u32[]{:S(2)}, u32[]{:S(2)}) collective-permute-start(f32[1024,128]{1,0:T(8,128)S(1)} %collective-permute-done.17), channel_id=1, source_target_pairs={{4,6},{5,7},{12,14},{13,15},{20,22},{21,23},{28,30},{29,31}} | collective-permute-start | bytes 1572872 | tf_op jit(solution)/shard_map/ppermute | solution.py:394
  129.4 15.1 %collective-permute-start.22 = (f32[1024,128]{1,0:T(8,128)S(1)}, f32[1024,128]{1,0:T(8,128)S(1)}, u32[]{:S(2)}, u32[]{:S(2)}) collective-permute-start(f32[1024,128]{1,0:T(8,128)S(1)} %get-tuple-element.43.mine_ref), channel_id=1, source_target_pairs={{0,1},{1,0},{2,3},{3,2},{4,5},{5,4},{6,7},{7,6},{8,9},{9,8},{10,11... | collective-permute-start | bytes 1572872 | tf_op jit(solution)/shard_map/ppermute | solution.py:409
  143.6 13.0 %collective-permute-start.21 = (f32[1024,128]{1,0:T(8,128)S(1)}, f32[1024,128]{1,0:T(8,128)S(1)}, u32[]{:S(2)}, u32[]{:S(2)}) collective-permute-start(f32[1024,128]{1,0:T(8,128)S(1)} %select_select_fusion.1.mine_ref), channel_id=1, source_target_pairs={{0,1},{1,0},{2,3},{3,2},{4,5},{5,4},{6,7},{7,6},{8,9},{9,8},{10,11... | collective-permute-start | bytes 1572872 | tf_op jit(solution)/shard_map/ppermute | solution.py:409

commit v4 on v3

--- a/solution.py
+++ b/solution.py
@@ -174,33 +174,22 @@
 
 
 def update_kernel(
-    start,
-    rows,
-    offset,
-    strip,
-    info_ref,
-    mat_ref,
-    right_ref,
-    lower_ref,
-    inv_t_ref,
-    mine_ref,
-    other_ref,
-    *refs,
+    start, block, info_ref, mat_ref, right_ref, lower_ref, inv_t_ref, mine_ref, other_ref, *refs
 ):
     out_ref, taken, given, panel, first_panel, in_sems, out_sems = refs[-7:]
     row, core, col = info_ref[0], info_ref[2], info_ref[3]
-    columns = mat_ref.shape[1]
-    steps = rows // strip
-    block = next(b for b in (512, 640, 256, TILE) if columns % b == 0)
-    piece = strip // PIECES
-
-    def rows_at(ref, step, skip, count):
-        return ref.at[pl.ds(pl.multiple_of(start + step * strip + skip, 8), count)]
+    rows, columns = mine_ref.shape[0], mat_ref.shape[1]
+    steps = columns // block
+    part = next(p for p in (512, 256, TILE) if rows % p == 0)
+    piece = rows // PIECES
+
+    def across(step):
+        return pl.ds(pl.multiple_of(step * block, TILE), block)
 
     def take(step, slot):
         for p in range(PIECES):
             pltpu.make_async_copy(
-                rows_at(mat_ref, step, p * piece, piece),
+                mat_ref.at[pl.ds(start + p * piece, piece), across(step)],
                 taken.at[slot, pl.ds(p * piece, piece)],
                 in_sems.at[slot],
             ).start()
@@ -209,60 +198,62 @@
         for p in range(PIECES):
             pltpu.make_async_copy(
                 given.at[slot, pl.ds(p * piece, piece)],
-                rows_at(out_ref, step, p * piece, piece),
+                out_ref.at[pl.ds(start + p * piece, piece), across(step)],
                 out_sems.at[slot],
             ).start()
 
     def wait_taken(step, slot):
-        whole = rows_at(mat_ref, step, 0, strip)
+        whole = mat_ref.at[pl.ds(start, rows), across(step)]
         pltpu.make_async_copy(whole, taken.at[slot], in_sems.at[slot]).wait()
 
     def wait_given(step, slot):
-        whole = rows_at(out_ref, step, 0, strip)
+        whole = out_ref.at[pl.ds(start, rows), across(step)]
         pltpu.make_async_copy(given.at[slot], whole, out_sems.at[slot]).wait()
 
     for step in range(min(IN_SLOTS, steps)):
         take(step, step)
 
-    @pl.loop(0, steps)
-    def _(step):
-        in_slot, out_slot = lax.rem(step, IN_SLOTS), lax.rem(step, OUT_SLOTS)
-        here = pl.ds(pl.multiple_of(offset + step * strip, TILE), strip)
+    @pl.loop(0, rows // part)
+    def _(index):
+        here = pl.ds(pl.multiple_of(index * part, part), part)
         mine, other = mine_ref[here], other_ref[here]
         raw = jnp.concatenate(
             [jnp.where(core == 1, other, mine), jnp.where(core == 1, mine, other)], axis=1
         )
         solved = dot_half(spread_halves(raw), inv_t_ref[...])
-        panel[...] = spread_halves(solved)
-        first_panel[...] = jnp.where(col == 1, solved[:, TILE:], solved[:, :TILE])
-        top = jnp.logical_and(step == 0, row < PANELS)
-        if start == 0:
-
-            @pl.when(top)
-            def _():
-                head = jnp.where(row == 0, lower_ref[:TILE], lower_ref[TILE:])
-                panel[:TILE] = spread_halves(head)
-                first_panel[:TILE] = jnp.where(col == 1, head[:, TILE:], head[:, :TILE])
-
+        panel[here] = spread_halves(solved)
+        first_panel[here] = jnp.where(col == 1, solved[:, TILE:], solved[:, :TILE])
+
+    if start == 0:
+
+        @pl.when(row < PANELS)
+        def _():
+            head = jnp.where(row == 0, lower_ref[:TILE], lower_ref[TILE:])
+            panel[:TILE] = spread_halves(head)
+            first_panel[:TILE] = jnp.where(col == 1, head[:, TILE:], head[:, :TILE])
+
+    @pl.loop(0, steps)
+    def _(step):
+        in_slot, out_slot = lax.rem(step, IN_SLOTS), lax.rem(step, OUT_SLOTS)
         wait_taken(step, in_slot)
 
         @pl.when(step >= OUT_SLOTS)
         def _():
             wait_given(step - OUT_SLOTS, out_slot)
 
-        @pl.loop(0, columns // block)
+        @pl.loop(0, rows // part)
         def _(index):
-            across = pl.ds(pl.multiple_of(index * block, block), block)
-            product = dot_half(panel[...], right_ref[:, across])
-            given[out_slot, :, across] = taken[in_slot, :, across] - product
+            here = pl.ds(pl.multiple_of(index * part, part), part)
+            product = dot_half(panel[here], right_ref[:, across(step)])
+            given[out_slot, here] = taken[in_slot, here] - product
 
         if start == 0:
 
-            @pl.when(top)
+            @pl.when(row < PANELS)
             def _():
-                given[out_slot, :TILE] = jnp.zeros((TILE, columns), jnp.float32)
-
-        @pl.when(col < PANELS)
+                given[out_slot, :TILE] = jnp.zeros((TILE, block), jnp.float32)
+
+        @pl.when(jnp.logical_and(step == 0, col < PANELS))
         def _():
             given[out_slot, :, :TILE] = first_panel[...]
 
@@ -276,9 +267,9 @@
         wait_given(step, step % OUT_SLOTS)
 
 
-def update_rows(start, end, base, info, matrix, right, lower, inv_t, mine, other, out):
-    rows, columns = end - start, matrix.shape[1]
-    strip = 2 * TILE if rows % (2 * TILE) == 0 else TILE
+def update_rows(start, info, matrix, right, lower, inv_t, mine, other, out):
+    rows, columns = mine.shape[0], matrix.shape[1]
+    block = next(b for b in (512, 640, 256, TILE) if columns % b == 0)
     any_spec = pl.BlockSpec(memory_space=pl.ANY)
     vmem = pl.BlockSpec(memory_space=pltpu.VMEM)
     in_specs = [pl.BlockSpec(memory_space=pltpu.SMEM), any_spec] + [vmem] * 5
@@ -289,15 +280,15 @@
         in_specs.append(any_spec)
         operands.append(out)
     return pl.pallas_call(
-        functools.partial(update_kernel, start, rows, start - base, strip),
+        functools.partial(update_kernel, start, block),
         in_specs=in_specs,
         out_specs=any_spec,
         out_shape=jax.ShapeDtypeStruct(matrix.shape, jnp.float32),
         scratch_shapes=[
-            pltpu.VMEM((IN_SLOTS, strip, columns), jnp.float32),
-            pltpu.VMEM((OUT_SLOTS, strip, columns), jnp.float32),
-            pltpu.VMEM((strip, 3 * WIDE), jnp.bfloat16),
-            pltpu.VMEM((strip, TILE), jnp.float32),
+            pltpu.VMEM((IN_SLOTS, rows, block), jnp.float32),
+            pltpu.VMEM((OUT_SLOTS, rows, block), jnp.float32),
+            pltpu.VMEM((rows, 3 * WIDE), jnp.bfloat16),
+            pltpu.VMEM((rows, TILE), jnp.float32),
             pltpu.SemaphoreType.DMA((IN_SLOTS,)),
             pltpu.SemaphoreType.DMA((OUT_SLOTS,)),
         ],
@@ -336,9 +327,8 @@
     return chosen
 
 
-def share_corner(matrix, row, place, core, row_count, col_count):
+def share_corner(tile, earlier, row, place, core, row_count, col_count):
     depth = col_count // CORES
-    tile = matrix[:TILE, :TILE]
     got = [tile]
     for shift in range(1, row_count):
         pairs = [
@@ -348,6 +338,7 @@
         ]
         got.append(lax.ppermute(tile, ("row", "col"), pairs))
     column = jnp.concatenate([pick(got, (row - p) % row_count) for p in range(PANELS)], axis=0)
+    column = after(column, earlier)
     beside = lax.ppermute(column, "col", [(0, 1), (1, 0)])
     square = jnp.concatenate(
         [jnp.where(core == 0, column, beside), jnp.where(core == 0, beside, column)], axis=1
@@ -356,7 +347,7 @@
     for shift in range(1, depth):
         pairs = [(c, c + CORES * shift) for c in range(CORES)]
         got.append(lax.ppermute(square, "col", pairs))
-    return column, pick(got, place)
+    return column, square, pick(got, place)
 
 
 def per_device(matrix):
@@ -371,10 +362,6 @@
     chunks = next(n for n in (5, 4, 2, 1) if tiles % n == 0)
     rows = tiles // chunks * TILE
     half = matrix.shape[1] // 2
-
-    column, corner = share_corner(matrix, row, place, core, row_count, col_count)
-    bands = [after(matrix[:TILE, :half], column), after(matrix[:TILE, half:], column)]
-    bands = [double_rows(band, row, row_count) for band in bands]
 
     last = chunks + depth - 2
     held, got = [], None
@@ -394,8 +381,12 @@
         return lax.ppermute(block, "col", hops)
 
     got = fill(0)
-    got = fill(1, corner)
-    got = fill(2, bands[0])
+    tile = after(matrix[:TILE, :TILE], held[0])
+    column, square, corner = share_corner(tile, got, row, place, core, row_count, col_count)
+    bands = [after(matrix[:TILE, :half], column), after(matrix[:TILE, half:], column)]
+    bands = [double_rows(band, row, row_count) for band in bands]
+    got = fill(1, square)
+    got = fill(2, bands[0], corner)
     lower, inverse, inv_t = factor_corner(after(corner, held[2]))
     besides = [swap_rows(band, row_count) for band in bands]
     slot = 3
@@ -413,10 +404,8 @@
         if right is None:
             right = solve_columns(info, inverse, list(zip(bands, besides)))
         other = after(other, held[-1])
-        first = chunk * rows
-        out = update_rows(
-            first, first + rows, first, info, matrix, right, lower, inv_t, mine, other, out
-        )
+        shared = (info, matrix, right, lower, inv_t)
+        out = update_rows(chunk * rows, *shared, mine, other, out)
     return out
 
 

time: 170 us -> 155 us (0.912)
  Pallas kernels: 72.2 us -> 62.6 us
  waiting for transfers between devices: 57.7 us -> 51.4 us
    ppermute x7, waiting for transfers between devices: 30.1 us -> 40.5 us  [fill(): return lax.ppermute(block, 'col', hops)]
    pallas_call x5, Pallas kernels: 60.5 us -> 50.9 us  [update_rows(): pl.pallas_call(functools.partial(update_kernel, start, block), in_specs=i...]
    ppermute x3, waiting for transfers between devices: 19.7 us -> 10.7 us  [share_corner(): got.append(lax.ppermute(square, 'col', pairs))]
    ppermute x2, waiting for transfers between devices: 7.76 us -> 0.01 us  [double_rows(): got = lax.ppermute(block, 'row', pairs)]
  transfers between devices with their start and end apart: 23 -> 23, of which waited for: 7 -> 7; matrix products, arithmetic and copies ran while one was open for 5% -> 5% of each run, Pallas kernels for 36% -> 34%
where the time goes in v4:
time: 155 us; the launch traced here: 154 us
  Pallas kernels  62.6 us (40%)
  waiting for transfers between devices  51.4 us (33%)
  starting transfers between devices  29.6 us (19%)
  other arithmetic  6.3 us (4%)
  local copies, waits for them, and re-layouts  3.29 us (2%)
    pallas_call x5, Pallas kernels, update_rows(): pl.pallas_call(functools.partial(update_kernel, start, block), in_specs=i...  50.9 us
    ppermute x7, waiting for transfers between devices, fill(): return lax.ppermute(block, 'col', hops)  40.5 us
    ppermute x3, waiting for transfers between devices, share_corner(): got.append(lax.ppermute(square, 'col', pairs))  10.7 us
    pallas_call x1, Pallas kernels, factor_corner(): pl.pallas_call(corner_kernel, out_shape=(jax.ShapeDtypeStruct((WIDE, WIDE...  9.83 us
    ppermute x7, starting transfers between devices, fill(): return lax.ppermute(block, 'col', hops)  8.77 us
    ppermute x2, starting transfers between devices, double_rows(): got = lax.ppermute(block, 'row', pairs)  6.44 us
    select_n x4, other arithmetic, fill(): block = own if got is None else jnp.where(place == 0, own, got)  4.59 us
    ppermute x5, starting transfers between devices, per_device(): other = lax.ppermute(mine, 'col', [(c, c ^ 1) for c in range(col_count)])  4.53 us
  transfers between devices with their start and end apart: 23, of which 7 were waited for; matrix products, arithmetic and copies ran while one was open for 5% of the time, Pallas kernels for 34%

profile of v4, /device:TPU:25, one launch (start us, length us, event | category | flops | bytes accessed | tf_op | source)
XLA Modules:
  0.0 153.7 jit_solution(1211611331893806974)
XLA Ops:
  6.6 1.3 collective-permute-start.5
  7.9 1.4 collective-permute-start.6
  9.3 1.4 collective-permute-start.7
  10.7 1.5 collective-permute-start.8
  12.2 1.4 fusion
  13.5 3.2 %collective-permute-start.9 = (f32[128,1280]{1,0:T(8,128)S(1)}, f32[128,1280]{1,0:T(8,128)S(1)}, u32[]{:S(2)}, u32[]{:S(2)}) collective-permute-start(f32[128,1280]{1,0:T(8,128)S(1)} %get-tuple-element.27), channel_id=1, source_target_pairs={{0,16},{8,24},{1,17},{9,25},{2,18},{10,26},{3,19},{11,27},{4,20},{... | collective-permute-start | bytes 1966088 | tf_op jit(solution)/shard_map/ppermute | solution.py:313
  16.7 10.7 %collective-permute-done.5 = f32[256,256]{1,0:T(8,128)} collective-permute-done((f32[256,256]{1,0:T(8,128)S(1)}, f32[256,256]{1,0:T(8,128)}, u32[]{:S(2)}, u32[]{:S(2)}) %collective-permute-start.5) | collective-permute-done | bytes 262176 | tf_op jit(solution)/shard_map/ppermute | solution.py:349
  27.4 3.3 %collective-permute-start.11 = (f32[128,1280]{1,0:T(8,128)S(1)}, f32[128,1280]{1,0:T(8,128)S(1)}, u32[]{:S(2)}, u32[]{:S(2)}) collective-permute-start(f32[128,1280]{1,0:T(8,128)S(1)} %get-tuple-element.31), channel_id=1, source_target_pairs={{0,16},{8,24},{1,17},{9,25},{2,18},{10,26},{3,19},{11,27},{4,20},{... | collective-permute-start | bytes 1966088 | tf_op jit(solution)/shard_map/ppermute | solution.py:313
  31.7 1.3 slice_select_fusion.3
  33.1 1.3 collective-permute-start.13
  34.4 1.2 collective-permute-start.10
  35.6 9.8 %shard_map.17 = (f32[256,256]{1,0:T(8,128)S(1)}, bf16[256,768]{1,0:T(8,128)(2,1)S(1)}, bf16[768,256]{1,0:T(8,128)(2,1)S(1)}) custom-call(f32[256,256]{1,0:T(8,128)S(1)} %select_select_fusion.5.corner_ref), custom_call_target="tpu_custom_call" | custom-call | flops 40000000 | bytes 1048576 | tf_op jit(solution)/shard_map/pallas_call | solution.py:132
  45.5 14.3 %collective-permute-done.13 = f32[1024,128]{1,0:T(8,128)S(1)} collective-permute-done((f32[1024,128]{1,0:T(8,128)S(1)}, f32[1024,128]{1,0:T(8,128)S(1)}, u32[]{:S(2)}, u32[]{:S(2)}) %collective-permute-start.13) | collective-permute-done | bytes 524320 | tf_op jit(solution)/shard_map/ppermute | solution.py:381
  59.8 1.1 slice_select_fusion
  60.9 1.3 collective-permute-start.14
  62.2 1.9 %collective-permute-start.12 = (f32[128,1280]{1,0:T(8,128)S(1)}, f32[128,1280]{1,0:T(8,128)S(1)}, u32[]{:S(2)}, u32[]{:S(2)}) collective-permute-start(f32[128,1280]{1,0:T(8,128)S(1)} %broadcast_select_fusion.refs_2_), channel_id=1, source_target_pairs={{0,8},{8,0},{16,24},{24,16},{1,9},{9,1},{17,25},{25,17},{2,10},{10... | collective-permute-start | bytes 1966088 | tf_op jit(solution)/shard_map/ppermute | solution.py:320
  64.2 15.2 %collective-permute-done.14 = f32[1024,128]{1,0:T(8,128)S(1)} collective-permute-done((f32[1024,128]{1,0:T(8,128)S(1)}, f32[1024,128]{1,0:T(8,128)S(1)}, u32[]{:S(2)}, u32[]{:S(2)}) %collective-permute-start.14) | collective-permute-done | bytes 524320 | tf_op jit(solution)/shard_map/ppermute | solution.py:381
  79.3 1.1 slice_select_fusion.1
  80.6 2.0 %collective-permute-start.16 = (f32[1024,128]{1,0:T(8,128)S(1)}, f32[1024,128]{1,0:T(8,128)S(1)}, u32[]{:S(2)}, u32[]{:S(2)}) collective-permute-start(f32[1024,128]{1,0:T(8,128)S(1)} %get-tuple-element.48.mine_ref), channel_id=1, source_target_pairs={{0,1},{1,0},{2,3},{3,2},{4,5},{5,4},{6,7},{7,6},{8,9},{9,8},{10,11... | collective-permute-start | bytes 1572872 | tf_op jit(solution)/shard_map/ppermute | solution.py:400
  82.6 1.5 collective-permute-start.15
  84.1 1.9 %shard_map.18.right_ref = bf16[768,2560]{1,0:T(8,128)(2,1)S(1)} custom-call(s32[4]{0:T(128)S(1)} %pad_add_fusion.info_ref, bf16[256,768]{1,0:T(8,128)(2,1)S(1)} %get-tuple-element.30.inv_ref, f32[128,1280]{1,0:T(8,128)S(1)} %broadcast_select_fusion.1.refs_0_, f32[128,1280]{1,0:T(8,128)S(1)} %collective-permute-done.10.refs_1_, ...), custom_call_target="tpu_custom_call" | custom-call | flops 1006632960 | bytes 5242880 | tf_op jit(solution)/shard_map/pallas_call | solution.py:163
  86.1 10.2 %shard_map.19.refs_0_ = f32[5120,2560]{1,0:T(8,128)} custom-call(s32[4]{0:T(128)S(1)} %pad_add_fusion.info_ref, f32[5120,2560]{1,0:T(8,128)} %mat_ref.9, bf16[768,2560]{1,0:T(8,128)(2,1)S(1)} %shard_map.18.right_ref, f32[256,256]{1,0:T(8,128)S(1)} %get-tuple-element.32.lower_ref, bf16[768,256]{1,0:T(8,128)(2,1)S(1)} %get-tuple-element.33.inv_t_ref, ...), custom_call_target="tpu_custom_call" | custom-call | flops 4026531840 | bytes 20971520 | tf_op jit(solution)/shard_map/pallas_call | solution.py:282
  96.4 4.0 %collective-permute-done.15 = f32[1024,128]{1,0:T(8,128)S(1)} collective-permute-done((f32[1024,128]{1,0:T(8,128)S(1)}, f32[1024,128]{1,0:T(8,128)S(1)}, u32[]{:S(2)}, u32[]{:S(2)}) %collective-permute-start.15) | collective-permute-done | bytes 524320 | tf_op jit(solution)/shard_map/ppermute | solution.py:381
  100.4 1.3 collective-permute-start.17
  101.7 10.2 %shard_map.20.refs_0_ = f32[5120,2560]{1,0:T(8,128)} custom-call(s32[4]{0:T(128)S(1)} %pad_add_fusion.info_ref, f32[5120,2560]{1,0:T(8,128)} %mat_ref.9, bf16[768,2560]{1,0:T(8,128)(2,1)S(1)} %shard_map.18.right_ref, f32[256,256]{1,0:T(8,128)S(1)} %get-tuple-element.32.lower_ref, ...), custom_call_target="tpu_custom_call", output_to_operand_aliasing={{}: (7, {})} | custom-call | flops 4026531840 | bytes 20971520 | tf_op jit(solution)/shard_map/pallas_call | solution.py:282
  111.8 3.3 %collective-permute-done.17 = f32[1024,128]{1,0:T(8,128)S(1)} collective-permute-done((f32[1024,128]{1,0:T(8,128)S(1)}, f32[1024,128]{1,0:T(8,128)S(1)}, u32[]{:S(2)}, u32[]{:S(2)}) %collective-permute-start.17) | collective-permute-done | bytes 524320 | tf_op jit(solution)/shard_map/ppermute | solution.py:381
  115.3 1.5 collective-permute-start.20
  116.8 1.3 collective-permute-start.19
  118.3 10.2 %shard_map.21.refs_0_ = f32[5120,2560]{1,0:T(8,128)} custom-call(s32[4]{0:T(128)S(1)} %pad_add_fusion.info_ref, f32[5120,2560]{1,0:T(8,128)} %mat_ref.9, bf16[768,2560]{1,0:T(8,128)(2,1)S(1)} %shard_map.18.right_ref, f32[256,256]{1,0:T(8,128)S(1)} %get-tuple-element.32.lower_ref, ...), custom_call_target="tpu_custom_call", output_to_operand_aliasing={{}: (7, {})} | custom-call | flops 4026531840 | bytes 20971520 | tf_op jit(solution)/shard_map/pallas_call | solution.py:282
  128.5 3.7 %collective-permute-done.19 = f32[1024,128]{1,0:T(8,128)S(1)} collective-permute-done((f32[1024,128]{1,0:T(8,128)S(1)}, f32[1024,128]{1,0:T(8,128)S(1)}, u32[]{:S(2)}, u32[]{:S(2)}) %collective-permute-start.19) | collective-permute-done | bytes 524320 | tf_op jit(solution)/shard_map/ppermute | solution.py:381
  133.2 10.2 %shard_map.22.refs_0_ = f32[5120,2560]{1,0:T(8,128)} custom-call(s32[4]{0:T(128)S(1)} %pad_add_fusion.info_ref, f32[5120,2560]{1,0:T(8,128)} %mat_ref.9, bf16[768,2560]{1,0:T(8,128)(2,1)S(1)} %shard_map.18.right_ref, f32[256,256]{1,0:T(8,128)S(1)} %get-tuple-element.32.lower_ref, ...), custom_call_target="tpu_custom_call", output_to_operand_aliasing={{}: (7, {})} | custom-call | flops 4026531840 | bytes 20971520 | tf_op jit(solution)/shard_map/pallas_call | solution.py:282
  143.4 10.2 %shard_map.23 = f32[5120,2560]{1,0:T(8,128)} custom-call(s32[4]{0:T(128)S(1)} %pad_add_fusion.info_ref, f32[5120,2560]{1,0:T(8,128)} %mat_ref.9, bf16[768,2560]{1,0:T(8,128)(2,1)S(1)} %shard_map.18.right_ref, f32[256,256]{1,0:T(8,128)S(1)} %get-tuple-element.32.lower_ref, ...), custom_call_target="tpu_custom_call", output_to_operand_aliasing={{}: (7, {})} | custom-call | flops 4026531840 | bytes 20971520 | tf_op jit(solution)/shard_map/pallas_call | solution.py:282
  (39 shorter events, 9.3 us)
Async XLA Ops:
  1.1 3.7 %collective-permute-start.3 = (f32[1024,128]{1,0:T(8,128)S(1)}, f32[1024,128]{1,0:T(8,128)S(1)}, u32[]{:S(2)}, u32[]{:S(2)}) collective-permute-start(f32[1024,128]{1,0:T(8,128)S(1)} %slice.25), channel_id=1, source_target_pairs={{0,2},{1,3},{8,10},{9,11},{16,18},{17,19},{24,26},{25,27}} | collective-permute-start | bytes 1572872 | tf_op jit(solution)/shard_map/ppermute | solution.py:381
  2.6 2.1 %collective-permute-start = (f32[128,128]{1,0:T(8,128)S(1)}, f32[128,128]{1,0:T(8,128)S(1)}, u32[]{:S(2)}, u32[]{:S(2)}) collective-permute-start(f32[128,128]{1,0:T(8,128)S(1)} %slice.24), channel_id=1, source_target_pairs={{0,24},{1,25},{8,0},{9,1}} | collective-permute-start | bytes 196616 | tf_op jit(solution)/shard_map/ppermute | solution.py:339
  3.3 1.4 collective-permute-start.1
  4.0 0.8 collective-permute-start.2
  4.8 1.8 %collective-permute-start.4 = (f32[256,128]{1,0:T(8,128)S(1)}, f32[256,128]{1,0:T(8,128)S(1)}, u32[]{:S(2)}, u32[]{:S(2)}) collective-permute-start(f32[256,128]{1,0:T(8,128)S(1)} %pad_maximum_fusion.1), channel_id=1, source_target_pairs={{0,1},{1,0},{8,9},{9,8},{16,17},{17,16},{24,25},{25,24}} | collective-permute-start | bytes 393224 | tf_op jit(solution)/shard_map/ppermute | solution.py:342
  6.6 20.8 %collective-permute-start.5 = (f32[256,256]{1,0:T(8,128)S(1)}, f32[256,256]{1,0:T(8,128)}, u32[]{:S(2)}, u32[]{:S(2)}) collective-permute-start(f32[256,256]{1,0:T(8,128)S(1)} %pad_maximum_fusion), channel_id=1, source_target_pairs={{0,6},{1,7},{8,14},{9,15},{16,22},{17,23},{24,30},{25,31}} | collective-permute-start | bytes 786440 | tf_op jit(solution)/shard_map/ppermute | solution.py:349
  7.9 22.7 %collective-permute-start.6 = (f32[256,256]{1,0:T(8,128)S(1)}, f32[256,256]{1,0:T(8,128)}, u32[]{:S(2)}, u32[]{:S(2)}) collective-permute-start(f32[256,256]{1,0:T(8,128)S(1)} %pad_maximum_fusion), channel_id=1, source_target_pairs={{0,4},{1,5},{8,12},{9,13},{16,20},{17,21},{24,28},{25,29}} | collective-permute-start | bytes 786440 | tf_op jit(solution)/shard_map/ppermute | solution.py:349
  9.3 21.4 %collective-permute-start.7 = (f32[256,256]{1,0:T(8,128)S(1)}, f32[256,256]{1,0:T(8,128)}, u32[]{:S(2)}, u32[]{:S(2)}) collective-permute-start(f32[256,256]{1,0:T(8,128)S(1)} %pad_maximum_fusion), channel_id=1, source_target_pairs={{0,2},{1,3},{8,10},{9,11},{16,18},{17,19},{24,26},{25,27}} | collective-permute-start | bytes 786440 | tf_op jit(solution)/shard_map/ppermute | solution.py:349
  10.7 21.0 %collective-permute-start.8 = (f32[1024,128]{1,0:T(8,128)S(1)}, f32[1024,128]{1,0:T(8,128)}, u32[]{:S(2)}, u32[]{:S(2)}) collective-permute-start(f32[1024,128]{1,0:T(8,128)S(1)} %slice_select_fusion.2), channel_id=1, source_target_pairs={{0,2},{1,3},{2,4},{3,5},{8,10},{9,11},{10,12},{11,13},{16,18},{17,... | collective-permute-start | bytes 1572872 | tf_op jit(solution)/shard_map/ppermute | solution.py:381
  13.5 19.5 %collective-permute-start.9 = (f32[128,1280]{1,0:T(8,128)S(1)}, f32[128,1280]{1,0:T(8,128)S(1)}, u32[]{:S(2)}, u32[]{:S(2)}) collective-permute-start(f32[128,1280]{1,0:T(8,128)S(1)} %get-tuple-element.27), channel_id=1, source_target_pairs={{0,16},{8,24},{1,17},{9,25},{2,18},{10,26},{3,19},{11,27},{4,20},{... | collective-permute-start | bytes 1966088 | tf_op jit(solution)/shard_map/ppermute | solution.py:313
  27.4 18.0 %collective-permute-start.11 = (f32[128,1280]{1,0:T(8,128)S(1)}, f32[128,1280]{1,0:T(8,128)S(1)}, u32[]{:S(2)}, u32[]{:S(2)}) collective-permute-start(f32[128,1280]{1,0:T(8,128)S(1)} %get-tuple-element.31), channel_id=1, source_target_pairs={{0,16},{8,24},{1,17},{9,25},{2,18},{10,26},{3,19},{11,27},{4,20},{... | collective-permute-start | bytes 1966088 | tf_op jit(solution)/shard_map/ppermute | solution.py:313
  33.1 26.7 %collective-permute-start.13 = (f32[1024,128]{1,0:T(8,128)S(1)}, f32[1024,128]{1,0:T(8,128)S(1)}, u32[]{:S(2)}, u32[]{:S(2)}) collective-permute-start(f32[1024,128]{1,0:T(8,128)S(1)} %slice_select_fusion.3), channel_id=1, source_target_pairs={{0,2},{1,3},{2,4},{3,5},{4,6},{5,7},{8,10},{9,11},{10,12},{11,13},... | collective-permute-start | bytes 1572872 | tf_op jit(solution)/shard_map/ppermute | solution.py:381
  34.4 26.5 %collective-permute-start.10 = (f32[128,1280]{1,0:T(8,128)S(1)}, f32[128,1280]{1,0:T(8,128)S(1)}, u32[]{:S(2)}, u32[]{:S(2)}) collective-permute-start(f32[128,1280]{1,0:T(8,128)S(1)} %broadcast_select_fusion.1.refs_0_), channel_id=1, source_target_pairs={{0,8},{8,0},{16,24},{24,16},{1,9},{9,1},{17,25},{25,17},{2,10},{10... | collective-permute-start | bytes 1966088 | tf_op jit(solution)/shard_map/ppermute | solution.py:320
  60.9 18.4 %collective-permute-start.14 = (f32[1024,128]{1,0:T(8,128)S(1)}, f32[1024,128]{1,0:T(8,128)S(1)}, u32[]{:S(2)}, u32[]{:S(2)}) collective-permute-start(f32[1024,128]{1,0:T(8,128)S(1)} %slice_select_fusion), channel_id=1, source_target_pairs={{0,2},{1,3},{2,4},{3,5},{4,6},{5,7},{8,10},{9,11},{10,12},{11,13},... | collective-permute-start | bytes 1572872 | tf_op jit(solution)/shard_map/ppermute | solution.py:381
  62.2 21.9 %collective-permute-start.12 = (f32[128,1280]{1,0:T(8,128)S(1)}, f32[128,1280]{1,0:T(8,128)S(1)}, u32[]{:S(2)}, u32[]{:S(2)}) collective-permute-start(f32[128,1280]{1,0:T(8,128)S(1)} %broadcast_select_fusion.refs_2_), channel_id=1, source_target_pairs={{0,8},{8,0},{16,24},{24,16},{1,9},{9,1},{17,25},{25,17},{2,10},{10... | collective-permute-start | bytes 1966088 | tf_op jit(solution)/shard_map/ppermute | solution.py:320
  80.6 5.5 %collective-permute-start.16 = (f32[1024,128]{1,0:T(8,128)S(1)}, f32[1024,128]{1,0:T(8,128)S(1)}, u32[]{:S(2)}, u32[]{:S(2)}) collective-permute-start(f32[1024,128]{1,0:T(8,128)S(1)} %get-tuple-element.48.mine_ref), channel_id=1, source_target_pairs={{0,1},{1,0},{2,3},{3,2},{4,5},{5,4},{6,7},{7,6},{8,9},{9,8},{10,11... | collective-permute-start | bytes 1572872 | tf_op jit(solution)/shard_map/ppermute | solution.py:400
  82.6 17.8 %collective-permute-start.15 = (f32[1024,128]{1,0:T(8,128)S(1)}, f32[1024,128]{1,0:T(8,128)S(1)}, u32[]{:S(2)}, u32[]{:S(2)}) collective-permute-start(f32[1024,128]{1,0:T(8,128)S(1)} %slice_select_fusion.1), channel_id=1, source_target_pairs={{0,2},{1,3},{2,4},{3,5},{4,6},{5,7},{8,10},{9,11},{10,12},{11,13},... | collective-permute-start | bytes 1572872 | tf_op jit(solution)/shard_map/ppermute | solution.py:381
  86.0 15.6 %collective-permute-start.18 = (f32[1024,128]{1,0:T(8,128)S(1)}, f32[1024,128]{1,0:T(8,128)S(1)}, u32[]{:S(2)}, u32[]{:S(2)}) collective-permute-start(f32[1024,128]{1,0:T(8,128)S(1)} %get-tuple-element.47.mine_ref), channel_id=1, source_target_pairs={{0,1},{1,0},{2,3},{3,2},{4,5},{5,4},{6,7},{7,6},{8,9},{9,8},{10,11... | collective-permute-start | bytes 1572872 | tf_op jit(solution)/shard_map/ppermute | solution.py:400
  100.4 14.8 %collective-permute-start.17 = (f32[1024,128]{1,0:T(8,128)S(1)}, f32[1024,128]{1,0:T(8,128)S(1)}, u32[]{:S(2)}, u32[]{:S(2)}) collective-permute-start(f32[1024,128]{1,0:T(8,128)S(1)} %collective-permute-done.15), channel_id=1, source_target_pairs={{2,4},{3,5},{4,6},{5,7},{10,12},{11,13},{12,14},{13,15},{18,20},{1... | collective-permute-start | bytes 1572872 | tf_op jit(solution)/shard_map/ppermute | solution.py:381
  115.3 3.1 %collective-permute-start.20 = (f32[1024,128]{1,0:T(8,128)S(1)}, f32[1024,128]{1,0:T(8,128)S(1)}, u32[]{:S(2)}, u32[]{:S(2)}) collective-permute-start(f32[1024,128]{1,0:T(8,128)S(1)} %get-tuple-element.46.mine_ref), channel_id=1, source_target_pairs={{0,1},{1,0},{2,3},{3,2},{4,5},{5,4},{6,7},{7,6},{8,9},{9,8},{10,11... | collective-permute-start | bytes 1572872 | tf_op jit(solution)/shard_map/ppermute | solution.py:400
  116.8 15.4 %collective-permute-start.19 = (f32[1024,128]{1,0:T(8,128)S(1)}, f32[1024,128]{1,0:T(8,128)S(1)}, u32[]{:S(2)}, u32[]{:S(2)}) collective-permute-start(f32[1024,128]{1,0:T(8,128)S(1)} %collective-permute-done.17), channel_id=1, source_target_pairs={{4,6},{5,7},{12,14},{13,15},{20,22},{21,23},{28,30},{29,31}} | collective-permute-start | bytes 1572872 | tf_op jit(solution)/shard_map/ppermute | solution.py:381
  118.1 15.1 %collective-permute-start.22 = (f32[1024,128]{1,0:T(8,128)S(1)}, f32[1024,128]{1,0:T(8,128)S(1)}, u32[]{:S(2)}, u32[]{:S(2)}) collective-permute-start(f32[1024,128]{1,0:T(8,128)S(1)} %get-tuple-element.45.mine_ref), channel_id=1, source_target_pairs={{0,1},{1,0},{2,3},{3,2},{4,5},{5,4},{6,7},{7,6},{8,9},{9,8},{10,11... | collective-permute-start | bytes 1572872 | tf_op jit(solution)/shard_map/ppermute | solution.py:400
  132.3 11.0 %collective-permute-start.21 = (f32[1024,128]{1,0:T(8,128)S(1)}, f32[1024,128]{1,0:T(8,128)S(1)}, u32[]{:S(2)}, u32[]{:S(2)}) collective-permute-start(f32[1024,128]{1,0:T(8,128)S(1)} %select_select_fusion.1.mine_ref), channel_id=1, source_target_pairs={{0,1},{1,0},{2,3},{3,2},{4,5},{5,4},{6,7},{7,6},{8,9},{9,8},{10,11... | collective-permute-start | bytes 1572872 | tf_op jit(solution)/shard_map/ppermute | solution.py:400

commit v5 on v4

--- a/solution.py
+++ b/solution.py
@@ -141,36 +141,29 @@
     )(corner)
 
 
-def columns_kernel(info_ref, inv_ref, *refs):
-    out_ref, stack = refs[-2:]
-    odd = info_ref[0] % 2 == 1
-    start = 0
-    for mine_ref, other_ref in zip(refs[0:-2:2], refs[1:-2:2]):
-        size = mine_ref.shape[1]
-        here = pl.ds(start, size)
-        mine, other = mine_ref[...], other_ref[...]
-        first = jnp.where(odd, other, mine)
-        second = jnp.where(odd, mine, other)
-        stack_halves(stack.at[:, here], jnp.concatenate([first, second], axis=0))
-        stack_halves(out_ref.at[:, here], dot_half(inv_ref[...], stack[:, here]))
-        start += size
-
-
-def solve_columns(info, inverse, pairs):
-    flat = [array for pair in pairs for array in pair]
-    total = sum(pair[0].shape[1] for pair in pairs)
-    vmem = pl.BlockSpec(memory_space=pltpu.VMEM)
+def columns_kernel(inv_ref, raw_ref, out_ref, stack):
+    stack_halves(stack, raw_ref[...])
+    stack_halves(out_ref, dot_half(inv_ref[...], stack[...]))
+
+
+def solve_columns(inverse, bands):
+    total = bands.shape[1]
+    block = next(b for b in (512, 640, 256, TILE) if total % b == 0)
     return pl.pallas_call(
         columns_kernel,
-        in_specs=[pl.BlockSpec(memory_space=pltpu.SMEM)] + [vmem] * (1 + len(flat)),
-        out_specs=vmem,
+        grid=(total // block,),
+        in_specs=[
+            pl.BlockSpec(memory_space=pltpu.VMEM),
+            pl.BlockSpec((WIDE, block), lambda j: (0, j)),
+        ],
+        out_specs=pl.BlockSpec((3 * WIDE, block), lambda j: (0, j)),
         out_shape=jax.ShapeDtypeStruct((3 * WIDE, total), jnp.bfloat16),
-        scratch_shapes=[pltpu.VMEM((3 * WIDE, total), jnp.bfloat16)],
+        scratch_shapes=[pltpu.VMEM((3 * WIDE, block), jnp.bfloat16)],
         compiler_params=pltpu.CompilerParams(vmem_limit_bytes=VMEM_LIMIT),
         cost_estimate=pl.CostEstimate(
             flops=6 * WIDE * WIDE * total, bytes_accessed=WIDE * total * 8, transcendentals=0
         ),
-    )(info, inverse, *flat)
+    )(inverse, bands)
 
 
 def update_kernel(
@@ -306,20 +299,6 @@
     return lax.optimization_barrier((value, *earlier))[0]
 
 
-def double_rows(block, row, row_count):
-    stride = PANELS
-    while stride < row_count:
-        pairs = [(i, i + stride) for i in range(min(stride, row_count - stride))]
-        got = lax.ppermute(block, "row", pairs)
-        block = jnp.where(jnp.logical_and(row >= stride, row < 2 * stride), got, block)
-        stride *= 2
-    return block
-
-
-def swap_rows(block, row_count):
-    return lax.ppermute(block, "row", [(i, i ^ 1) for i in range(row_count)])
-
-
 def pick(blocks, index):
     chosen = blocks[0]
     for shift in range(1, len(blocks)):
@@ -327,8 +306,7 @@
     return chosen
 
 
-def share_corner(tile, earlier, row, place, core, row_count, col_count):
-    depth = col_count // CORES
+def share_tile(tile, row, row_count, col_count):
     got = [tile]
     for shift in range(1, row_count):
         pairs = [
@@ -337,17 +315,18 @@
             for c in range(CORES)
         ]
         got.append(lax.ppermute(tile, ("row", "col"), pairs))
-    column = jnp.concatenate([pick(got, (row - p) % row_count) for p in range(PANELS)], axis=0)
-    column = after(column, earlier)
-    beside = lax.ppermute(column, "col", [(0, 1), (1, 0)])
-    square = jnp.concatenate(
-        [jnp.where(core == 0, column, beside), jnp.where(core == 0, beside, column)], axis=1
-    )
-    got = [square]
-    for shift in range(1, depth):
+    return jnp.concatenate([pick(got, (row - p) % row_count) for p in range(PANELS)], axis=0)
+
+
+def share_corner(column, place, core, col_count):
+    got = [column]
+    for shift in range(1, col_count // CORES):
         pairs = [(c, c + CORES * shift) for c in range(CORES)]
-        got.append(lax.ppermute(square, "col", pairs))
-    return column, square, pick(got, place)
+        got.append(lax.ppermute(column, "col", pairs))
+    column = pick(got, place)
+    beside = lax.ppermute(column, "col", [(c, c ^ 1) for c in range(col_count)])
+    halves = [jnp.where(core == 0, column, beside), jnp.where(core == 0, beside, column)]
+    return column, jnp.concatenate(halves, axis=1)
 
 
 def per_device(matrix):
@@ -361,51 +340,58 @@
     tiles = matrix.shape[0] // TILE
     chunks = next(n for n in (5, 4, 2, 1) if tiles % n == 0)
     rows = tiles // chunks * TILE
-    half = matrix.shape[1] // 2
+    swap = [(c, c ^ 1) for c in range(col_count)]
 
     last = chunks + depth - 2
     held, got = [], None
 
-    def fill(slot, *earlier):
+    def fill(*earlier):
+        slot = len(held)
         if slot < chunks:
             own = matrix[slot * rows : (slot + 1) * rows, :TILE]
             block = own if got is None else jnp.where(place == 0, own, got)
         else:
             block = got
-        block = after(block, *earlier)
-        held.append(block)
-        if slot == last:
-            return None
+        held.append(after(block, *earlier))
         busy = [c for c in range(col_count) if 0 <= slot - c // CORES < chunks]
         hops = [(c, c + CORES) for c in busy if c + CORES < col_count]
-        return lax.ppermute(block, "col", hops)
-
-    got = fill(0)
+        return lax.ppermute(held[-1], "col", hops) if slot < last else None
+
+    ready = []
+
+    def exchange(*earlier):
+        chunk = len(ready)
+        mine = after(pick(held[chunk : chunk + depth], place), *earlier)
+        ready.append((mine, lax.ppermute(mine, "col", swap)))
+        return mine
+
+    got = fill()
     tile = after(matrix[:TILE, :TILE], held[0])
-    column, square, corner = share_corner(tile, got, row, place, core, row_count, col_count)
-    bands = [after(matrix[:TILE, :half], column), after(matrix[:TILE, half:], column)]
-    bands = [double_rows(band, row, row_count) for band in bands]
-    got = fill(1, square)
-    got = fill(2, bands[0], corner)
-    lower, inverse, inv_t = factor_corner(after(corner, held[2]))
-    besides = [swap_rows(band, row_count) for band in bands]
-    slot = 3
-    while slot < depth:
-        got = fill(slot, inverse, bands[1], besides[0])
-        slot += 1
-    right = None
+    column = after(share_tile(tile, row, row_count, col_count), got)
+    bands = lax.all_gather(after(matrix[:TILE], column), "row", axis=0, tiled=True)
+    got = fill(column)
+    column, corner = share_corner(after(column, held[1]), place, core, col_count)
+    got = fill(column)
+    while len(held) < depth:
+        got = fill()
+    mark = exchange()
+    lower, inverse, inv_t = factor_corner(after(corner, held[-1], mark))
+    got = fill(inverse)
+    mark = exchange()
+    right = solve_columns(inverse, bands)
     out = None
     for chunk in range(chunks):
-        mine = pick(held[chunk : chunk + depth], place)
-        other = lax.ppermute(mine, "col", [(c, c ^ 1) for c in range(col_count)])
-        if slot <= last:
-            got = fill(slot) if out is None else fill(slot, out)
-            slot += 1
-        if right is None:
-            right = solve_columns(info, inverse, list(zip(bands, besides)))
-        other = after(other, held[-1])
-        shared = (info, matrix, right, lower, inv_t)
-        out = update_rows(chunk * rows, *shared, mine, other, out)
+        earlier = (mark,) if out is None else (mark, out)
+        closing = len(held) == last
+        if len(held) < last:
+            got = fill(*earlier)
+            mark = exchange(*earlier)
+        mine, other = ready[chunk]
+        other = after(other, held[-1], mark)
+        out = update_rows(chunk * rows, info, matrix, right, lower, inv_t, mine, other, out)
+        if closing:
+            fill(out)
+            mark = exchange(out)
     return out
 
 

time: 155 us -> 165 us (1.065)
  the two profiles are of different devices: /device:TPU:25 before, /device:TPU:17 now
where the time goes in v5:
time: 165 us; the launch traced here: 163 us
  Pallas kernels  63.1 us (38%)
  waiting for transfers between devices  38.7 us (23%)
  starting transfers between devices  30.8 us (19%)
  between operations  13.8 us (8%)
  local copies, waits for them, and re-layouts  9.74 us (6%)
  other arithmetic  7.25 us (4%)
    pallas_call x5, Pallas kernels, update_rows(): pl.pallas_call(functools.partial(update_kernel, start, block), in_specs=i...  50.9 us
    ppermute x3, waiting for transfers between devices, share_corner(): got.append(lax.ppermute(column, 'col', pairs))  23.6 us
    ppermute x7, waiting for transfers between devices, fill(): return lax.ppermute(held[-1], 'col', hops) if slot < last else None  15.1 us
    ppermute x7, starting transfers between devices, fill(): return lax.ppermute(held[-1], 'col', hops) if slot < last else None  12.8 us
    pallas_call x1, Pallas kernels, factor_corner(): pl.pallas_call(corner_kernel, out_shape=(jax.ShapeDtypeStruct((WIDE, WIDE...  9.83 us
    ppermute x5, starting transfers between devices, exchange(): ready.append((mine, lax.ppermute(mine, 'col', swap)))  9.26 us
    unnamed x18, local copies, waits for them, and re-layouts  5.35 us
    select_n x4, other arithmetic, fill(): block = own if got is None else jnp.where(place == 0, own, got)  4.44 us
  transfers between devices with their start and end apart: 20, of which 4 were waited for; matrix products, arithmetic and copies ran while one was open for 6% of the time, Pallas kernels for 32%

profile of v5, /device:TPU:17, one launch (start us, length us, event | category | flops | bytes accessed | tf_op | source)
XLA Modules:
  0.0 163.5 jit_solution(12793004161114812429)
XLA Ops:
  6.5 1.1 slice.22
  8.3 0.8 slice.21
  11.2 2.5 %slice.26 = f32[128,2560]{1,0:T(8,128)} slice(f32[5120,2560]{1,0:T(8,128)} %mat_ref.9), slice={[0:128], [0:2560]} | slice | bytes 2621440 | tf_op jit(solution)/shard_map/slice | solution.py:371
  13.8 1.1 slice_select_fusion.3
  14.9 1.3 collective-permute-start.8
  16.9 1.3 collective-permute-start.5
  18.9 23.6 %collective-permute-done.5 = f32[256,128]{1,0:T(8,128)S(1)} collective-permute-done((f32[256,128]{1,0:T(8,128)S(1)}, f32[256,128]{1,0:T(8,128)S(1)}, u32[]{:S(2)}, u32[]{:S(2)}) %collective-permute-start.5) | collective-permute-done | bytes 131104 | tf_op jit(solution)/shard_map/ppermute | solution.py:325
  42.5 1.1 slice_select_fusion.1
  43.6 1.9 %collective-permute-start.9 = (f32[1024,128]{1,0:T(8,128)S(1)}, f32[1024,128]{1,0:T(8,128)S(1)}, u32[]{:S(2)}, u32[]{:S(2)}) collective-permute-start(f32[1024,128]{1,0:T(8,128)S(1)} %slice_select_fusion.1), channel_id=1, source_target_pairs={{0,2},{1,3},{2,4},{3,5},{4,6},{5,7},{8,10},{9,11},{10,12},{11,13},... | collective-permute-start | bytes 1572872 | tf_op jit(solution)/shard_map/ppermute | solution.py:358
  45.6 4.2 %collective-permute-start.7 = (f32[256,128]{1,0:T(8,128)S(1)}, f32[256,128]{1,0:T(8,128)S(1)}, u32[]{:S(2)}, u32[]{:S(2)}) collective-permute-start(f32[256,128]{1,0:T(8,128)S(1)} %select_select_fusion.5), channel_id=1, source_target_pairs={{0,1},{1,0},{2,3},{3,2},{4,5},{5,4},{6,7},{7,6},{8,9},{9,8},{10,11... | collective-permute-start | bytes 393224 | tf_op jit(solution)/shard_map/ppermute | solution.py:327
  49.8 9.1 %collective-permute-done.9 = f32[1024,128]{1,0:T(8,128)S(1)} collective-permute-done((f32[1024,128]{1,0:T(8,128)S(1)}, f32[1024,128]{1,0:T(8,128)S(1)}, u32[]{:S(2)}, u32[]{:S(2)}) %collective-permute-start.9) | collective-permute-done | bytes 524320 | tf_op jit(solution)/shard_map/ppermute | solution.py:358
  58.9 1.1 slice_select_fusion.2
  60.0 1.9 %collective-permute-start.10 = (f32[1024,128]{1,0:T(8,128)S(1)}, f32[1024,128]{1,0:T(8,128)S(1)}, u32[]{:S(2)}, u32[]{:S(2)}) collective-permute-start(f32[1024,128]{1,0:T(8,128)S(1)} %slice_select_fusion.2), channel_id=1, source_target_pairs={{0,2},{1,3},{2,4},{3,5},{4,6},{5,7},{8,10},{9,11},{10,12},{11,13},... | collective-permute-start | bytes 1572872 | tf_op jit(solution)/shard_map/ppermute | solution.py:358
  62.1 9.8 %shard_map.17 = (f32[256,256]{1,0:T(8,128)S(1)}, bf16[256,768]{1,0:T(8,128)(2,1)S(1)}, bf16[768,256]{1,0:T(8,128)(2,1)S(1)}) custom-call(f32[256,256]{1,0:T(8,128)S(1)} %pad_maximum_fusion.corner_ref), custom_call_target="tpu_custom_call" | custom-call | flops 40000000 | bytes 1048576 | tf_op jit(solution)/shard_map/pallas_call | solution.py:132
  72.5 1.1 slice_select_fusion
  73.6 2.2 %collective-permute-start.11 = (f32[1024,128]{1,0:T(8,128)S(1)}, f32[1024,128]{1,0:T(8,128)}, u32[]{:S(2)}, u32[]{:S(2)}) collective-permute-start(f32[1024,128]{1,0:T(8,128)S(1)} %slice_select_fusion), channel_id=1, source_target_pairs={{0,2},{1,3},{2,4},{3,5},{4,6},{5,7},{8,10},{9,11},{10,12},{11,13},... | collective-permute-start | bytes 1572872 | tf_op jit(solution)/shard_map/ppermute | solution.py:358
  75.9 3.8 %collective-permute-start.13 = (f32[1024,128]{1,0:T(8,128)S(1)}, f32[1024,128]{1,0:T(8,128)S(1)}, u32[]{:S(2)}, u32[]{:S(2)}) collective-permute-start(f32[1024,128]{1,0:T(8,128)S(1)} %select_select_fusion.4.mine_ref), channel_id=1, source_target_pairs={{0,1},{1,0},{2,3},{3,2},{4,5},{5,4},{6,7},{7,6},{8,9},{9,8},{10,11... | collective-permute-start | bytes 1572872 | tf_op jit(solution)/shard_map/ppermute | solution.py:365
  79.9 5.4 %collective-permute-done.11 = f32[1024,128]{1,0:T(8,128)} collective-permute-done((f32[1024,128]{1,0:T(8,128)S(1)}, f32[1024,128]{1,0:T(8,128)}, u32[]{:S(2)}, u32[]{:S(2)}) %collective-permute-start.11) | collective-permute-done | bytes 524320 | tf_op jit(solution)/shard_map/ppermute | solution.py:358
  85.3 2.5 %collective-permute-start.12 = (f32[1024,128]{1,0:T(8,128)}, f32[1024,128]{1,0:T(8,128)}, u32[]{:S(2)}, u32[]{:S(2)}) collective-permute-start(f32[1024,128]{1,0:T(8,128)} %collective-permute-done.11), channel_id=1, source_target_pairs={{2,4},{3,5},{4,6},{5,7},{10,12},{11,13},{12,14},{13,15},{18,20},{1... | collective-permute-start | bytes 1572872 | tf_op jit(solution)/shard_map/ppermute | solution.py:358
  87.9 4.8 %collective-permute-start.15 = (f32[1024,128]{1,0:T(8,128)S(1)}, f32[1024,128]{1,0:T(8,128)S(1)}, u32[]{:S(2)}, u32[]{:S(2)}) collective-permute-start(f32[1024,128]{1,0:T(8,128)S(1)} %select_select_fusion.2.mine_ref), channel_id=1, source_target_pairs={{0,1},{1,0},{2,3},{3,2},{4,5},{5,4},{6,7},{7,6},{8,9},{9,8},{10,11... | collective-permute-start | bytes 1572872 | tf_op jit(solution)/shard_map/ppermute | solution.py:365
  93.5 2.5 %copy-done = f32[512,2560]{1,0:T(8,128)S(1)} copy-done((f32[512,2560]{1,0:T(8,128)S(1)}, f32[512,2560]{1,0:T(8,128)}, u32[]{:S(2)}) %copy-start) | copy-done | bytes 5242904
  96.0 1.0 copy-done.4
  97.0 2.4 %shard_map.18.right_ref = bf16[768,2560]{1,0:T(8,128)(2,1)S(1)} custom-call(bf16[256,768]{1,0:T(8,128)(2,1)S(1)} %copy-done.4, f32[512,2560]{1,0:T(8,128)S(1)} %copy-done), custom_call_target="tpu_custom_call" | custom-call | flops 1006632960 | bytes 5242880 | tf_op jit(solution)/shard_map/pallas_call | solution.py:152
  99.4 1.0 copy-done.2
  100.5 10.2 %shard_map.19.refs_0_ = f32[5120,2560]{1,0:T(8,128)} custom-call(s32[4]{0:T(128)S(1)} %pad_add_fusion.info_ref, f32[5120,2560]{1,0:T(8,128)} %mat_ref.9, bf16[768,2560]{1,0:T(8,128)(2,1)S(1)} %shard_map.18.right_ref, f32[256,256]{1,0:T(8,128)S(1)} %get-tuple-element.35.lower_ref, bf16[768,256]{1,0:T(8,128)(2,1)S(1)} %get-tuple-element.36.inv_t_ref, ...), custom_call_target="tpu_custom_call" | custom-call | flops 4026531840 | bytes 20971520 | tf_op jit(solution)/shard_map/pallas_call | solution.py:275
  110.7 2.3 %collective-permute-start.14 = (f32[1024,128]{1,0:T(8,128)}, f32[1024,128]{1,0:T(8,128)S(1)}, u32[]{:S(2)}, u32[]{:S(2)}) collective-permute-start(f32[1024,128]{1,0:T(8,128)} %collective-permute-done.12), channel_id=1, source_target_pairs={{4,6},{5,7},{12,14},{13,15},{20,22},{21,23},{28,30},{29,31}} | collective-permute-start | bytes 1572872 | tf_op jit(solution)/shard_map/ppermute | solution.py:358
  113.0 1.2 select_select_fusion.1.mine_ref
  114.5 10.2 %shard_map.20.refs_0_ = f32[5120,2560]{1,0:T(8,128)} custom-call(s32[4]{0:T(128)S(1)} %pad_add_fusion.info_ref, f32[5120,2560]{1,0:T(8,128)} %mat_ref.9, bf16[768,2560]{1,0:T(8,128)(2,1)S(1)} %shard_map.18.right_ref, f32[256,256]{1,0:T(8,128)S(1)} %get-tuple-element.35.lower_ref, ...), custom_call_target="tpu_custom_call", output_to_operand_aliasing={{}: (7, {})} | custom-call | flops 4026531840 | bytes 20971520 | tf_op jit(solution)/shard_map/pallas_call | solution.py:275
  124.7 10.2 %shard_map.21.refs_0_ = f32[5120,2560]{1,0:T(8,128)} custom-call(s32[4]{0:T(128)S(1)} %pad_add_fusion.info_ref, f32[5120,2560]{1,0:T(8,128)} %mat_ref.9, bf16[768,2560]{1,0:T(8,128)(2,1)S(1)} %shard_map.18.right_ref, f32[256,256]{1,0:T(8,128)S(1)} %get-tuple-element.35.lower_ref, ...), custom_call_target="tpu_custom_call", output_to_operand_aliasing={{}: (7, {})} | custom-call | flops 4026531840 | bytes 20971520 | tf_op jit(solution)/shard_map/pallas_call | solution.py:275
  134.9 1.1 select_select_fusion.mine_ref
  136.3 10.2 %shard_map.22.refs_0_ = f32[5120,2560]{1,0:T(8,128)} custom-call(s32[4]{0:T(128)S(1)} %pad_add_fusion.info_ref, f32[5120,2560]{1,0:T(8,128)} %mat_ref.9, bf16[768,2560]{1,0:T(8,128)(2,1)S(1)} %shard_map.18.right_ref, f32[256,256]{1,0:T(8,128)S(1)} %get-tuple-element.35.lower_ref, ...), custom_call_target="tpu_custom_call", output_to_operand_aliasing={{}: (7, {})} | custom-call | flops 4026531840 | bytes 20971520 | tf_op jit(solution)/shard_map/pallas_call | solution.py:275
  146.5 10.2 %shard_map.23 = f32[5120,2560]{1,0:T(8,128)} custom-call(s32[4]{0:T(128)S(1)} %pad_add_fusion.info_ref, f32[5120,2560]{1,0:T(8,128)} %mat_ref.9, bf16[768,2560]{1,0:T(8,128)(2,1)S(1)} %shard_map.18.right_ref, f32[256,256]{1,0:T(8,128)S(1)} %get-tuple-element.35.lower_ref, ...), custom_call_target="tpu_custom_call", output_to_operand_aliasing={{}: (7, {})} | custom-call | flops 4026531840 | bytes 20971520 | tf_op jit(solution)/shard_map/pallas_call | solution.py:275
  (52 shorter events, 6.7 us)
Async XLA Ops:
  6.5 87.0 %all-gather.2.cloned.1.call-start = ((), (), s32[]{:S(2)}) async-start(), calls=%async_computation | async-start | bytes 6553600 | tf_op jit(solution)/shard_map/all_gather | solution.py:371
  7.6 6.1 %collective-permute-start.3 = (f32[1024,128]{1,0:T(8,128)S(1)}, f32[1024,128]{1,0:T(8,128)S(1)}, u32[]{:S(2)}, u32[]{:S(2)}) collective-permute-start(f32[1024,128]{1,0:T(8,128)S(1)} %slice.22), channel_id=1, source_target_pairs={{0,2},{1,3},{8,10},{9,11},{16,18},{17,19},{24,26},{25,27}} | collective-permute-start | bytes 1572872 | tf_op jit(solution)/shard_map/ppermute | solution.py:358
  9.2 4.5 %collective-permute-start = (f32[128,128]{1,0:T(8,128)S(1)}, f32[128,128]{1,0:T(8,128)S(1)}, u32[]{:S(2)}, u32[]{:S(2)}) collective-permute-start(f32[128,128]{1,0:T(8,128)S(1)} %slice.21), channel_id=1, source_target_pairs={{0,24},{1,25},{8,0},{9,1}} | collective-permute-start | bytes 196616 | tf_op jit(solution)/shard_map/ppermute | solution.py:317
  9.8 3.9 %collective-permute-start.1 = (f32[128,128]{1,0:T(8,128)S(1)}, f32[128,128]{1,0:T(8,128)S(1)}, u32[]{:S(2)}, u32[]{:S(2)}) collective-permute-start(f32[128,128]{1,0:T(8,128)S(1)} %slice.21), channel_id=1, source_target_pairs={{0,16},{1,17},{8,24},{9,25}} | collective-permute-start | bytes 196616 | tf_op jit(solution)/shard_map/ppermute | solution.py:317
  10.5 3.2 %collective-permute-start.2 = (f32[128,128]{1,0:T(8,128)S(1)}, f32[128,128]{1,0:T(8,128)S(1)}, u32[]{:S(2)}, u32[]{:S(2)}) collective-permute-start(f32[128,128]{1,0:T(8,128)S(1)} %slice.21), channel_id=1, source_target_pairs={{0,8},{1,9},{8,16},{9,17}} | collective-permute-start | bytes 196616 | tf_op jit(solution)/shard_map/ppermute | solution.py:317
  14.9 27.6 %collective-permute-start.8 = (f32[1024,128]{1,0:T(8,128)S(1)}, f32[1024,128]{1,0:T(8,128)S(1)}, u32[]{:S(2)}, u32[]{:S(2)}) collective-permute-start(f32[1024,128]{1,0:T(8,128)S(1)} %slice_select_fusion.3), channel_id=1, source_target_pairs={{0,2},{1,3},{2,4},{3,5},{8,10},{9,11},{10,12},{11,13},{16,18},{17,... | collective-permute-start | bytes 1572872 | tf_op jit(solution)/shard_map/ppermute | solution.py:358
  16.2 2.7 %collective-permute-start.4 = (f32[256,128]{1,0:T(8,128)S(1)}, f32[256,128]{1,0:T(8,128)S(1)}, u32[]{:S(2)}, u32[]{:S(2)}) collective-permute-start(f32[256,128]{1,0:T(8,128)S(1)} %pad_maximum_fusion.1), channel_id=1, source_target_pairs={{0,6},{1,7},{8,14},{9,15},{16,22},{17,23},{24,30},{25,31}} | collective-permute-start | bytes 393224 | tf_op jit(solution)/shard_map/ppermute | solution.py:325
  16.9 25.6 %collective-permute-start.5 = (f32[256,128]{1,0:T(8,128)S(1)}, f32[256,128]{1,0:T(8,128)S(1)}, u32[]{:S(2)}, u32[]{:S(2)}) collective-permute-start(f32[256,128]{1,0:T(8,128)S(1)} %pad_maximum_fusion.1), channel_id=1, source_target_pairs={{0,4},{1,5},{8,12},{9,13},{16,20},{17,21},{24,28},{25,29}} | collective-permute-start | bytes 393224 | tf_op jit(solution)/shard_map/ppermute | solution.py:325
  18.2 24.3 %collective-permute-start.6 = (f32[256,128]{1,0:T(8,128)S(1)}, f32[256,128]{1,0:T(8,128)S(1)}, u32[]{:S(2)}, u32[]{:S(2)}) collective-permute-start(f32[256,128]{1,0:T(8,128)S(1)} %pad_maximum_fusion.1), channel_id=1, source_target_pairs={{0,2},{1,3},{8,10},{9,11},{16,18},{17,19},{24,26},{25,27}} | collective-permute-start | bytes 393224 | tf_op jit(solution)/shard_map/ppermute | solution.py:325
  43.6 15.3 %collective-permute-start.9 = (f32[1024,128]{1,0:T(8,128)S(1)}, f32[1024,128]{1,0:T(8,128)S(1)}, u32[]{:S(2)}, u32[]{:S(2)}) collective-permute-start(f32[1024,128]{1,0:T(8,128)S(1)} %slice_select_fusion.1), channel_id=1, source_target_pairs={{0,2},{1,3},{2,4},{3,5},{4,6},{5,7},{8,10},{9,11},{10,12},{11,13},... | collective-permute-start | bytes 1572872 | tf_op jit(solution)/shard_map/ppermute | solution.py:358
  45.6 16.4 %collective-permute-start.7 = (f32[256,128]{1,0:T(8,128)S(1)}, f32[256,128]{1,0:T(8,128)S(1)}, u32[]{:S(2)}, u32[]{:S(2)}) collective-permute-start(f32[256,128]{1,0:T(8,128)S(1)} %select_select_fusion.5), channel_id=1, source_target_pairs={{0,1},{1,0},{2,3},{3,2},{4,5},{5,4},{6,7},{7,6},{8,9},{9,8},{10,11... | collective-permute-start | bytes 393224 | tf_op jit(solution)/shard_map/ppermute | solution.py:327
  60.0 32.6 %copy-start.5 = (f32[1024,128]{1,0:T(8,128)}, f32[1024,128]{1,0:T(8,128)S(1)}, u32[]{:S(2)}) copy-start(f32[1024,128]{1,0:T(8,128)S(1)} %slice_select_fusion.2) | copy-start | bytes 1572868
  60.0 12.5 %collective-permute-start.10 = (f32[1024,128]{1,0:T(8,128)S(1)}, f32[1024,128]{1,0:T(8,128)S(1)}, u32[]{:S(2)}, u32[]{:S(2)}) collective-permute-start(f32[1024,128]{1,0:T(8,128)S(1)} %slice_select_fusion.2), channel_id=1, source_target_pairs={{0,2},{1,3},{2,4},{3,5},{4,6},{5,7},{8,10},{9,11},{10,12},{11,13},... | collective-permute-start | bytes 1572872 | tf_op jit(solution)/shard_map/ppermute | solution.py:358
  72.0 15.9 %copy-start.3 = (bf16[256,768]{1,0:T(8,128)(2,1)}, bf16[256,768]{1,0:T(8,128)(2,1)S(1)}, u32[]{:S(2)}) copy-start(bf16[256,768]{1,0:T(8,128)(2,1)S(1)} %get-tuple-element.33.inv_ref) | copy-start | bytes 1179652
  73.6 19.1 %copy-start.7 = (f32[1024,128]{1,0:T(8,128)}, f32[1024,128]{1,0:T(8,128)S(1)}, u32[]{:S(2)}) copy-start(f32[1024,128]{1,0:T(8,128)S(1)} %slice_select_fusion) | copy-start | bytes 1572868
  73.6 11.6 %collective-permute-start.11 = (f32[1024,128]{1,0:T(8,128)S(1)}, f32[1024,128]{1,0:T(8,128)}, u32[]{:S(2)}, u32[]{:S(2)}) collective-permute-start(f32[1024,128]{1,0:T(8,128)S(1)} %slice_select_fusion), channel_id=1, source_target_pairs={{0,2},{1,3},{2,4},{3,5},{4,6},{5,7},{8,10},{9,11},{10,12},{11,13},... | collective-permute-start | bytes 1572872 | tf_op jit(solution)/shard_map/ppermute | solution.py:358
  75.9 16.8 %collective-permute-start.13 = (f32[1024,128]{1,0:T(8,128)S(1)}, f32[1024,128]{1,0:T(8,128)S(1)}, u32[]{:S(2)}, u32[]{:S(2)}) collective-permute-start(f32[1024,128]{1,0:T(8,128)S(1)} %select_select_fusion.4.mine_ref), channel_id=1, source_target_pairs={{0,1},{1,0},{2,3},{3,2},{4,5},{5,4},{6,7},{7,6},{8,9},{9,8},{10,11... | collective-permute-start | bytes 1572872 | tf_op jit(solution)/shard_map/ppermute | solution.py:365
  79.8 34.7 %collective-permute-start.16 = (f32[1024,128]{1,0:T(8,128)S(1)}, f32[1024,128]{1,0:T(8,128)S(1)}, u32[]{:S(2)}, u32[]{:S(2)}) collective-permute-start(f32[1024,128]{1,0:T(8,128)S(1)} %select_select_fusion.3.mine_ref), channel_id=1, source_target_pairs={{0,1},{1,0},{2,3},{3,2},{4,5},{5,4},{6,7},{7,6},{8,9},{9,8},{10,11... | collective-permute-start | bytes 1572872 | tf_op jit(solution)/shard_map/ppermute | solution.py:365
  85.3 25.4 %collective-permute-start.12 = (f32[1024,128]{1,0:T(8,128)}, f32[1024,128]{1,0:T(8,128)}, u32[]{:S(2)}, u32[]{:S(2)}) collective-permute-start(f32[1024,128]{1,0:T(8,128)} %collective-permute-done.11), channel_id=1, source_target_pairs={{2,4},{3,5},{4,6},{5,7},{10,12},{11,13},{12,14},{13,15},{18,20},{1... | collective-permute-start | bytes 1572872 | tf_op jit(solution)/shard_map/ppermute | solution.py:358
  87.9 36.8 %collective-permute-start.15 = (f32[1024,128]{1,0:T(8,128)S(1)}, f32[1024,128]{1,0:T(8,128)S(1)}, u32[]{:S(2)}, u32[]{:S(2)}) collective-permute-start(f32[1024,128]{1,0:T(8,128)S(1)} %select_select_fusion.2.mine_ref), channel_id=1, source_target_pairs={{0,1},{1,0},{2,3},{3,2},{4,5},{5,4},{6,7},{7,6},{8,9},{9,8},{10,11... | collective-permute-start | bytes 1572872 | tf_op jit(solution)/shard_map/ppermute | solution.py:365
  92.7 0.8 copy-start.1
  93.5 2.5 %copy-start = (f32[512,2560]{1,0:T(8,128)S(1)}, f32[512,2560]{1,0:T(8,128)}, u32[]{:S(2)}) copy-start(f32[512,2560]{1,0:T(8,128)} %all-gather.2.cloned.1.call-done.raw_ref) | copy-start | bytes 15728644
  96.0 1.0 copy-start.4
  99.4 1.0 copy-start.2
  100.4 12.5 %copy-start.6 = (f32[1024,128]{1,0:T(8,128)S(1)}, f32[1024,128]{1,0:T(8,128)}, u32[]{:S(2)}) copy-start(f32[1024,128]{1,0:T(8,128)} %copy-done.5) | copy-start | bytes 1572868
  100.4 12.5 %copy-start.8 = (f32[1024,128]{1,0:T(8,128)S(1)}, f32[1024,128]{1,0:T(8,128)}, u32[]{:S(2)}) copy-start(f32[1024,128]{1,0:T(8,128)} %copy-done.7) | copy-start | bytes 1572868
  110.7 24.2 %collective-permute-start.14 = (f32[1024,128]{1,0:T(8,128)}, f32[1024,128]{1,0:T(8,128)S(1)}, u32[]{:S(2)}, u32[]{:S(2)}) collective-permute-start(f32[1024,128]{1,0:T(8,128)} %collective-permute-done.12), channel_id=1, source_target_pairs={{4,6},{5,7},{12,14},{13,15},{20,22},{21,23},{28,30},{29,31}} | collective-permute-start | bytes 1572872 | tf_op jit(solution)/shard_map/ppermute | solution.py:358
  114.1 22.2 %collective-permute-start.18 = (f32[1024,128]{1,0:T(8,128)S(1)}, f32[1024,128]{1,0:T(8,128)S(1)}, u32[]{:S(2)}, u32[]{:S(2)}) collective-permute-start(f32[1024,128]{1,0:T(8,128)S(1)} %select_select_fusion.1.mine_ref), channel_id=1, source_target_pairs={{0,1},{1,0},{2,3},{3,2},{4,5},{5,4},{6,7},{7,6},{8,9},{9,8},{10,11... | collective-permute-start | bytes 1572872 | tf_op jit(solution)/shard_map/ppermute | solution.py:365
  136.0 10.4 %collective-permute-start.17 = (f32[1024,128]{1,0:T(8,128)S(1)}, f32[1024,128]{1,0:T(8,128)S(1)}, u32[]{:S(2)}, u32[]{:S(2)}) collective-permute-start(f32[1024,128]{1,0:T(8,128)S(1)} %select_select_fusion.mine_ref), channel_id=1, source_target_pairs={{0,1},{1,0},{2,3},{3,2},{4,5},{5,4},{6,7},{7,6},{8,9},{9,8},{10,11... | collective-permute-start | bytes 1572872 | tf_op jit(solution)/shard_map/ppermute | solution.py:365
Sparse Core Ops, SparseCore 0:
  13.9 69.8 all-gather.1

commit v6 on v5

--- a/solution.py
+++ b/solution.py
@@ -13,8 +13,8 @@
 CORES = 2
 VMEM_LIMIT = 40 * 1024 * 1024
 GROUP = 8
-IN_SLOTS = 3
-OUT_SLOTS = 2
+IN_SLOTS = 5
+OUT_SLOTS = 3
 PIECES = 4
 
 
@@ -141,29 +141,36 @@
     )(corner)
 
 
-def columns_kernel(inv_ref, raw_ref, out_ref, stack):
-    stack_halves(stack, raw_ref[...])
-    stack_halves(out_ref, dot_half(inv_ref[...], stack[...]))
-
-
-def solve_columns(inverse, bands):
-    total = bands.shape[1]
-    block = next(b for b in (512, 640, 256, TILE) if total % b == 0)
+def columns_kernel(info_ref, inv_ref, *refs):
+    out_ref, stack = refs[-2:]
+    odd = info_ref[0] % 2 == 1
+    start = 0
+    for mine_ref, other_ref in zip(refs[0:-2:2], refs[1:-2:2]):
+        size = mine_ref.shape[1]
+        here = pl.ds(start, size)
+        mine, other = mine_ref[...], other_ref[...]
+        first = jnp.where(odd, other, mine)
+        second = jnp.where(odd, mine, other)
+        stack_halves(stack.at[:, here], jnp.concatenate([first, second], axis=0))
+        stack_halves(out_ref.at[:, here], dot_half(inv_ref[...], stack[:, here]))
+        start += size
+
+
+def solve_columns(info, inverse, pairs):
+    flat = [array for pair in pairs for array in pair]
+    total = sum(pair[0].shape[1] for pair in pairs)
+    vmem = pl.BlockSpec(memory_space=pltpu.VMEM)
     return pl.pallas_call(
         columns_kernel,
-        grid=(total // block,),
-        in_specs=[
-            pl.BlockSpec(memory_space=pltpu.VMEM),
-            pl.BlockSpec((WIDE, block), lambda j: (0, j)),
-        ],
-        out_specs=pl.BlockSpec((3 * WIDE, block), lambda j: (0, j)),
+        in_specs=[pl.BlockSpec(memory_space=pltpu.SMEM)] + [vmem] * (1 + len(flat)),
+        out_specs=vmem,
         out_shape=jax.ShapeDtypeStruct((3 * WIDE, total), jnp.bfloat16),
-        scratch_shapes=[pltpu.VMEM((3 * WIDE, block), jnp.bfloat16)],
+        scratch_shapes=[pltpu.VMEM((3 * WIDE, total), jnp.bfloat16)],
         compiler_params=pltpu.CompilerParams(vmem_limit_bytes=VMEM_LIMIT),
         cost_estimate=pl.CostEstimate(
             flops=6 * WIDE * WIDE * total, bytes_accessed=WIDE * total * 8, transcendentals=0
         ),
-    )(inverse, bands)
+    )(info, inverse, *flat)
 
 
 def update_kernel(
@@ -262,7 +269,7 @@
 
 def update_rows(start, info, matrix, right, lower, inv_t, mine, other, out):
     rows, columns = mine.shape[0], matrix.shape[1]
-    block = next(b for b in (512, 640, 256, TILE) if columns % b == 0)
+    block = 2 * TILE if columns % (2 * TILE) == 0 else TILE
     any_spec = pl.BlockSpec(memory_space=pl.ANY)
     vmem = pl.BlockSpec(memory_space=pltpu.VMEM)
     in_specs = [pl.BlockSpec(memory_space=pltpu.SMEM), any_spec] + [vmem] * 5
@@ -299,6 +306,20 @@
     return lax.optimization_barrier((value, *earlier))[0]
 
 
+def double_rows(block, row, row_count):
+    stride = PANELS
+    while stride < row_count:
+        pairs = [(i, i + stride) for i in range(min(stride, row_count - stride))]
+        got = lax.ppermute(block, "row", pairs)
+        block = jnp.where(jnp.logical_and(row >= stride, row < 2 * stride), got, block)
+        stride *= 2
+    return block
+
+
+def swap_rows(block, row_count):
+    return lax.ppermute(block, "row", [(i, i ^ 1) for i in range(row_count)])
+
+
 def pick(blocks, index):
     chosen = blocks[0]
     for shift in range(1, len(blocks)):
@@ -340,6 +361,7 @@
     tiles = matrix.shape[0] // TILE
     chunks = next(n for n in (5, 4, 2, 1) if tiles % n == 0)
     rows = tiles // chunks * TILE
+    half = matrix.shape[1] // 2
     swap = [(c, c ^ 1) for c in range(col_count)]
 
     last = chunks + depth - 2
@@ -368,17 +390,20 @@
     got = fill()
     tile = after(matrix[:TILE, :TILE], held[0])
     column = after(share_tile(tile, row, row_count, col_count), got)
-    bands = lax.all_gather(after(matrix[:TILE], column), "row", axis=0, tiled=True)
     got = fill(column)
-    column, corner = share_corner(after(column, held[1]), place, core, col_count)
-    got = fill(column)
+    bands = [after(matrix[:TILE, :half], held[1]), after(matrix[:TILE, half:], held[1])]
+    column = after(column, *bands)
+    bands = [double_rows(band, row, row_count) for band in bands]
+    column, corner = share_corner(column, place, core, col_count)
+    got = fill(column, bands[0])
     while len(held) < depth:
         got = fill()
     mark = exchange()
-    lower, inverse, inv_t = factor_corner(after(corner, held[-1], mark))
-    got = fill(inverse)
+    besides = [swap_rows(band, row_count) for band in bands]
+    lower, inverse, inv_t = factor_corner(after(corner, held[-1], mark, bands[1]))
+    got = fill(inverse, ready[0][1], besides[0])
     mark = exchange()
-    right = solve_columns(inverse, bands)
+    right = solve_columns(info, inverse, list(zip(bands, besides)))
     out = None
     for chunk in range(chunks):
         earlier = (mark,) if out is None else (mark, out)

time: 165 us -> 154 us (0.933)
  the two profiles are of different devices: /device:TPU:17 before, /device:TPU:25 now
where the time goes in v6:
time: 154 us; the launch traced here: 151 us
  Pallas kernels  64.4 us (42%)
  waiting for transfers between devices  39.9 us (26%)
  starting transfers between devices  35.4 us (23%)
  other arithmetic  6.99 us (5%)
  local copies, waits for them, and re-layouts  3.3 us (2%)
    pallas_call x5, Pallas kernels, update_rows(): pl.pallas_call(functools.partial(update_kernel, start, block), in_specs=i...  52.7 us
    ppermute x7, waiting for transfers between devices, fill(): return lax.ppermute(held[-1], 'col', hops) if slot < last else None  22.6 us
    ppermute x3, waiting for transfers between devices, share_corner(): got.append(lax.ppermute(column, 'col', pairs))  17.3 us
    pallas_call x1, Pallas kernels, factor_corner(): pl.pallas_call(corner_kernel, out_shape=(jax.ShapeDtypeStruct((WIDE, WIDE...  9.83 us
    ppermute x5, starting transfers between devices, exchange(): ready.append((mine, lax.ppermute(mine, 'col', swap)))  8.28 us
    ppermute x7, starting transfers between devices, fill(): return lax.ppermute(held[-1], 'col', hops) if slot < last else None  8.01 us
    ppermute x2, starting transfers between devices, double_rows(): got = lax.ppermute(block, 'row', pairs)  6.36 us
    ppermute x1, starting transfers between devices, share_corner(): beside = lax.ppermute(column, 'col', [(c, c ^ 1) for c in range(col_count)])  5.18 us
  transfers between devices with their start and end apart: 23, of which 4 were waited for; matrix products, arithmetic and copies ran while one was open for 5% of the time, Pallas kernels for 36%

profile of v6, /device:TPU:25, one launch (start us, length us, event | category | flops | bytes accessed | tf_op | source)
XLA Modules:
  0.0 150.6 jit_solution(5854100283771425653)
XLA Ops:
  5.4 1.1 slice_select_fusion.3
  7.2 1.4 fusion
  8.6 3.2 %collective-permute-start.9 = (f32[128,1280]{1,0:T(8,128)S(1)}, f32[128,1280]{1,0:T(8,128)S(1)}, u32[]{:S(2)}, u32[]{:S(2)}) collective-permute-start(f32[128,1280]{1,0:T(8,128)S(1)} %get-tuple-element.31), channel_id=1, source_target_pairs={{0,16},{8,24},{1,17},{9,25},{2,18},{10,26},{3,19},{11,27},{4,20},{... | collective-permute-start | bytes 1966088 | tf_op jit(solution)/shard_map/ppermute | solution.py:313
  11.8 1.3 collective-permute-start.4
  13.1 1.3 collective-permute-start.5
  14.4 1.3 collective-permute-start.6
  15.7 17.3 %collective-permute-done.4 = f32[256,128]{1,0:T(8,128)} collective-permute-done((f32[256,128]{1,0:T(8,128)}, f32[256,128]{1,0:T(8,128)}, u32[]{:S(2)}, u32[]{:S(2)}) %collective-permute-start.4) | collective-permute-done | bytes 131104 | tf_op jit(solution)/shard_map/ppermute | solution.py:346
  33.0 3.2 %collective-permute-start.11 = (f32[128,1280]{1,0:T(8,128)S(1)}, f32[128,1280]{1,0:T(8,128)S(1)}, u32[]{:S(2)}, u32[]{:S(2)}) collective-permute-start(f32[128,1280]{1,0:T(8,128)S(1)} %get-tuple-element.32), channel_id=1, source_target_pairs={{0,16},{8,24},{1,17},{9,25},{2,18},{10,26},{3,19},{11,27},{4,20},{... | collective-permute-start | bytes 1966088 | tf_op jit(solution)/shard_map/ppermute | solution.py:313
  37.2 5.2 %collective-permute-start.7 = (f32[256,128]{1,0:T(8,128)S(1)}, f32[256,128]{1,0:T(8,128)S(1)}, u32[]{:S(2)}, u32[]{:S(2)}) collective-permute-start(f32[256,128]{1,0:T(8,128)S(1)} %select_select_fusion.5), channel_id=1, source_target_pairs={{0,1},{1,0},{2,3},{3,2},{4,5},{5,4},{6,7},{7,6},{8,9},{9,8},{10,11... | collective-permute-start | bytes 393224 | tf_op jit(solution)/shard_map/ppermute | solution.py:348
  42.4 1.1 slice_select_fusion.1
  43.6 1.3 collective-permute-start.12
  44.9 1.3 collective-permute-start.10
  46.7 13.3 %collective-permute-done.10 = f32[1024,128]{1,0:T(8,128)S(1)} collective-permute-done((f32[1024,128]{1,0:T(8,128)S(1)}, f32[1024,128]{1,0:T(8,128)S(1)}, u32[]{:S(2)}, u32[]{:S(2)}) %collective-permute-start.10) | collective-permute-done | bytes 524320 | tf_op jit(solution)/shard_map/ppermute | solution.py:380
  60.0 1.1 slice_select_fusion.2
  61.1 1.3 collective-permute-start.14
  62.6 1.2 collective-permute-start.15
  63.8 9.8 %shard_map.17 = (f32[256,256]{1,0:T(8,128)S(1)}, bf16[256,768]{1,0:T(8,128)(2,1)S(1)}, bf16[768,256]{1,0:T(8,128)(2,1)S(1)}) custom-call(f32[256,256]{1,0:T(8,128)S(1)} %pad_maximum_fusion.corner_ref), custom_call_target="tpu_custom_call" | custom-call | flops 40000000 | bytes 1048576 | tf_op jit(solution)/shard_map/pallas_call | solution.py:132
  73.6 1.6 %collective-permute-done.14 = f32[1024,128]{1,0:T(8,128)S(1)} collective-permute-done((f32[1024,128]{1,0:T(8,128)S(1)}, f32[1024,128]{1,0:T(8,128)S(1)}, u32[]{:S(2)}, u32[]{:S(2)}) %collective-permute-start.14) | collective-permute-done | bytes 524320 | tf_op jit(solution)/shard_map/ppermute | solution.py:380
  75.3 1.1 slice_select_fusion
  76.4 1.3 collective-permute-start.16
  77.8 1.9 %shard_map.18.right_ref = bf16[768,2560]{1,0:T(8,128)(2,1)S(1)} custom-call(s32[4]{0:T(128)S(1)} %pad_add_fusion.info_ref, bf16[256,768]{1,0:T(8,128)(2,1)S(1)} %get-tuple-element.36.inv_ref, f32[128,1280]{1,0:T(8,128)S(1)} %broadcast_select_fusion.1.refs_0_, f32[128,1280]{1,0:T(8,128)S(1)} %collective-permute-done.12.refs_1_, ...), custom_call_target="tpu_custom_call" | custom-call | flops 1006632960 | bytes 5242880 | tf_op jit(solution)/shard_map/pallas_call | solution.py:163
  79.8 2.1 %collective-permute-start.20 = (f32[1024,128]{1,0:T(8,128)S(1)}, f32[1024,128]{1,0:T(8,128)S(1)}, u32[]{:S(2)}, u32[]{:S(2)}) collective-permute-start(f32[1024,128]{1,0:T(8,128)S(1)} %select_select_fusion.3.mine_ref), channel_id=1, source_target_pairs={{0,1},{1,0},{2,3},{3,2},{4,5},{5,4},{6,7},{7,6},{8,9},{9,8},{10,11... | collective-permute-start | bytes 1572872 | tf_op jit(solution)/shard_map/ppermute | solution.py:387
  82.0 7.7 %collective-permute-done.16 = f32[1024,128]{1,0:T(8,128)S(1)} collective-permute-done((f32[1024,128]{1,0:T(8,128)S(1)}, f32[1024,128]{1,0:T(8,128)S(1)}, u32[]{:S(2)}, u32[]{:S(2)}) %collective-permute-start.16) | collective-permute-done | bytes 524320 | tf_op jit(solution)/shard_map/ppermute | solution.py:380
  89.6 1.5 collective-permute-start.17
  91.2 3.0 %collective-permute-start.19 = (f32[1024,128]{1,0:T(8,128)S(1)}, f32[1024,128]{1,0:T(8,128)S(1)}, u32[]{:S(2)}, u32[]{:S(2)}) collective-permute-start(f32[1024,128]{1,0:T(8,128)S(1)} %select_select_fusion.2.mine_ref), channel_id=1, source_target_pairs={{0,1},{1,0},{2,3},{3,2},{4,5},{5,4},{6,7},{7,6},{8,9},{9,8},{10,11... | collective-permute-start | bytes 1572872 | tf_op jit(solution)/shard_map/ppermute | solution.py:387
  94.2 10.6 %shard_map.19.refs_0_ = f32[5120,2560]{1,0:T(8,128)} custom-call(s32[4]{0:T(128)S(1)} %pad_add_fusion.info_ref, f32[5120,2560]{1,0:T(8,128)} %mat_ref.9, bf16[768,2560]{1,0:T(8,128)(2,1)S(1)} %shard_map.18.right_ref, f32[256,256]{1,0:T(8,128)S(1)} %get-tuple-element.37.lower_ref, bf16[768,256]{1,0:T(8,128)(2,1)S(1)} %get-tuple-element.38.inv_t_ref, ...), custom_call_target="tpu_custom_call" | custom-call | flops 4026531840 | bytes 20971520 | tf_op jit(solution)/shard_map/pallas_call | solution.py:282
  104.9 1.3 collective-permute-start.18
  106.3 1.8 %collective-permute-start.22 = (f32[1024,128]{1,0:T(8,128)S(1)}, f32[1024,128]{1,0:T(8,128)S(1)}, u32[]{:S(2)}, u32[]{:S(2)}) collective-permute-start(f32[1024,128]{1,0:T(8,128)S(1)} %select_select_fusion.1.mine_ref), channel_id=1, source_target_pairs={{0,1},{1,0},{2,3},{3,2},{4,5},{5,4},{6,7},{7,6},{8,9},{9,8},{10,11... | collective-permute-start | bytes 1572872 | tf_op jit(solution)/shard_map/ppermute | solution.py:387
  108.1 10.5 %shard_map.20.refs_0_ = f32[5120,2560]{1,0:T(8,128)} custom-call(s32[4]{0:T(128)S(1)} %pad_add_fusion.info_ref, f32[5120,2560]{1,0:T(8,128)} %mat_ref.9, bf16[768,2560]{1,0:T(8,128)(2,1)S(1)} %shard_map.18.right_ref, f32[256,256]{1,0:T(8,128)S(1)} %get-tuple-element.37.lower_ref, ...), custom_call_target="tpu_custom_call", output_to_operand_aliasing={{}: (7, {})} | custom-call | flops 4026531840 | bytes 20971520 | tf_op jit(solution)/shard_map/pallas_call | solution.py:282
  118.7 10.5 %shard_map.21.refs_0_ = f32[5120,2560]{1,0:T(8,128)} custom-call(s32[4]{0:T(128)S(1)} %pad_add_fusion.info_ref, f32[5120,2560]{1,0:T(8,128)} %mat_ref.9, bf16[768,2560]{1,0:T(8,128)(2,1)S(1)} %shard_map.18.right_ref, f32[256,256]{1,0:T(8,128)S(1)} %get-tuple-element.37.lower_ref, ...), custom_call_target="tpu_custom_call", output_to_operand_aliasing={{}: (7, {})} | custom-call | flops 4026531840 | bytes 20971520 | tf_op jit(solution)/shard_map/pallas_call | solution.py:282
  129.4 10.5 %shard_map.22.refs_0_ = f32[5120,2560]{1,0:T(8,128)} custom-call(s32[4]{0:T(128)S(1)} %pad_add_fusion.info_ref, f32[5120,2560]{1,0:T(8,128)} %mat_ref.9, bf16[768,2560]{1,0:T(8,128)(2,1)S(1)} %shard_map.18.right_ref, f32[256,256]{1,0:T(8,128)S(1)} %get-tuple-element.37.lower_ref, ...), custom_call_target="tpu_custom_call", output_to_operand_aliasing={{}: (7, {})} | custom-call | flops 4026531840 | bytes 20971520 | tf_op jit(solution)/shard_map/pallas_call | solution.py:282
  139.9 10.5 %shard_map.23 = f32[5120,2560]{1,0:T(8,128)} custom-call(s32[4]{0:T(128)S(1)} %pad_add_fusion.info_ref, f32[5120,2560]{1,0:T(8,128)} %mat_ref.9, bf16[768,2560]{1,0:T(8,128)(2,1)S(1)} %shard_map.18.right_ref, f32[256,256]{1,0:T(8,128)S(1)} %get-tuple-element.37.lower_ref, ...), custom_call_target="tpu_custom_call", output_to_operand_aliasing={{}: (7, {})} | custom-call | flops 4026531840 | bytes 20971520 | tf_op jit(solution)/shard_map/pallas_call | solution.py:282
  (41 shorter events, 8.5 us)
Async XLA Ops:
  1.1 4.3 %collective-permute-start.3 = (f32[1024,128]{1,0:T(8,128)S(1)}, f32[1024,128]{1,0:T(8,128)S(1)}, u32[]{:S(2)}, u32[]{:S(2)}) collective-permute-start(f32[1024,128]{1,0:T(8,128)S(1)} %slice.25), channel_id=1, source_target_pairs={{0,2},{1,3},{8,10},{9,11},{16,18},{17,19},{24,26},{25,27}} | collective-permute-start | bytes 1572872 | tf_op jit(solution)/shard_map/ppermute | solution.py:380
  2.6 2.1 %collective-permute-start = (f32[128,128]{1,0:T(8,128)S(1)}, f32[128,128]{1,0:T(8,128)S(1)}, u32[]{:S(2)}, u32[]{:S(2)}) collective-permute-start(f32[128,128]{1,0:T(8,128)S(1)} %slice.24), channel_id=1, source_target_pairs={{0,24},{1,25},{8,0},{9,1}} | collective-permute-start | bytes 196616 | tf_op jit(solution)/shard_map/ppermute | solution.py:338
  3.3 1.4 collective-permute-start.1
  4.0 0.7 collective-permute-start.2
  6.5 35.9 %collective-permute-start.8 = (f32[1024,128]{1,0:T(8,128)S(1)}, f32[1024,128]{1,0:T(8,128)S(1)}, u32[]{:S(2)}, u32[]{:S(2)}) collective-permute-start(f32[1024,128]{1,0:T(8,128)S(1)} %slice_select_fusion.3), channel_id=1, source_target_pairs={{0,2},{1,3},{2,4},{3,5},{8,10},{9,11},{10,12},{11,13},{16,18},{17,... | collective-permute-start | bytes 1572872 | tf_op jit(solution)/shard_map/ppermute | solution.py:380
  8.6 34.9 %collective-permute-start.9 = (f32[128,1280]{1,0:T(8,128)S(1)}, f32[128,1280]{1,0:T(8,128)S(1)}, u32[]{:S(2)}, u32[]{:S(2)}) collective-permute-start(f32[128,1280]{1,0:T(8,128)S(1)} %get-tuple-element.31), channel_id=1, source_target_pairs={{0,16},{8,24},{1,17},{9,25},{2,18},{10,26},{3,19},{11,27},{4,20},{... | collective-permute-start | bytes 1966088 | tf_op jit(solution)/shard_map/ppermute | solution.py:313
  11.8 21.2 %collective-permute-start.4 = (f32[256,128]{1,0:T(8,128)}, f32[256,128]{1,0:T(8,128)}, u32[]{:S(2)}, u32[]{:S(2)}) collective-permute-start(f32[256,128]{1,0:T(8,128)} %pad_maximum_fusion.1), channel_id=1, source_target_pairs={{0,6},{1,7},{8,14},{9,15},{16,22},{17,23},{24,30},{25,31}} | collective-permute-start | bytes 393224 | tf_op jit(solution)/shard_map/ppermute | solution.py:346
  13.1 23.1 %collective-permute-start.5 = (f32[256,128]{1,0:T(8,128)}, f32[256,128]{1,0:T(8,128)}, u32[]{:S(2)}, u32[]{:S(2)}) collective-permute-start(f32[256,128]{1,0:T(8,128)} %pad_maximum_fusion.1), channel_id=1, source_target_pairs={{0,4},{1,5},{8,12},{9,13},{16,20},{17,21},{24,28},{25,29}} | collective-permute-start | bytes 393224 | tf_op jit(solution)/shard_map/ppermute | solution.py:346
  14.4 21.8 %collective-permute-start.6 = (f32[256,128]{1,0:T(8,128)}, f32[256,128]{1,0:T(8,128)}, u32[]{:S(2)}, u32[]{:S(2)}) collective-permute-start(f32[256,128]{1,0:T(8,128)} %pad_maximum_fusion.1), channel_id=1, source_target_pairs={{0,2},{1,3},{8,10},{9,11},{16,18},{17,19},{24,26},{25,27}} | collective-permute-start | bytes 393224 | tf_op jit(solution)/shard_map/ppermute | solution.py:346
  33.0 13.2 %collective-permute-start.11 = (f32[128,1280]{1,0:T(8,128)S(1)}, f32[128,1280]{1,0:T(8,128)S(1)}, u32[]{:S(2)}, u32[]{:S(2)}) collective-permute-start(f32[128,1280]{1,0:T(8,128)S(1)} %get-tuple-element.32), channel_id=1, source_target_pairs={{0,16},{8,24},{1,17},{9,25},{2,18},{10,26},{3,19},{11,27},{4,20},{... | collective-permute-start | bytes 1966088 | tf_op jit(solution)/shard_map/ppermute | solution.py:313
  37.2 26.5 %collective-permute-start.7 = (f32[256,128]{1,0:T(8,128)S(1)}, f32[256,128]{1,0:T(8,128)S(1)}, u32[]{:S(2)}, u32[]{:S(2)}) collective-permute-start(f32[256,128]{1,0:T(8,128)S(1)} %select_select_fusion.5), channel_id=1, source_target_pairs={{0,1},{1,0},{2,3},{3,2},{4,5},{5,4},{6,7},{7,6},{8,9},{9,8},{10,11... | collective-permute-start | bytes 393224 | tf_op jit(solution)/shard_map/ppermute | solution.py:348
  43.6 32.8 %collective-permute-start.12 = (f32[128,1280]{1,0:T(8,128)S(1)}, f32[128,1280]{1,0:T(8,128)S(1)}, u32[]{:S(2)}, u32[]{:S(2)}) collective-permute-start(f32[128,1280]{1,0:T(8,128)S(1)} %broadcast_select_fusion.1.refs_0_), channel_id=1, source_target_pairs={{0,8},{8,0},{16,24},{24,16},{1,9},{9,1},{17,25},{25,17},{2,10},{10... | collective-permute-start | bytes 1966088 | tf_op jit(solution)/shard_map/ppermute | solution.py:320
  44.9 15.1 %collective-permute-start.10 = (f32[1024,128]{1,0:T(8,128)S(1)}, f32[1024,128]{1,0:T(8,128)S(1)}, u32[]{:S(2)}, u32[]{:S(2)}) collective-permute-start(f32[1024,128]{1,0:T(8,128)S(1)} %slice_select_fusion.1), channel_id=1, source_target_pairs={{0,2},{1,3},{2,4},{3,5},{4,6},{5,7},{8,10},{9,11},{10,12},{11,13},... | collective-permute-start | bytes 1572872 | tf_op jit(solution)/shard_map/ppermute | solution.py:380
  46.3 31.5 %collective-permute-start.13 = (f32[128,1280]{1,0:T(8,128)S(1)}, f32[128,1280]{1,0:T(8,128)S(1)}, u32[]{:S(2)}, u32[]{:S(2)}) collective-permute-start(f32[128,1280]{1,0:T(8,128)S(1)} %broadcast_select_fusion.refs_2_), channel_id=1, source_target_pairs={{0,8},{8,0},{16,24},{24,16},{1,9},{9,1},{17,25},{25,17},{2,10},{10... | collective-permute-start | bytes 1966088 | tf_op jit(solution)/shard_map/ppermute | solution.py:320
  61.1 14.2 %collective-permute-start.14 = (f32[1024,128]{1,0:T(8,128)S(1)}, f32[1024,128]{1,0:T(8,128)S(1)}, u32[]{:S(2)}, u32[]{:S(2)}) collective-permute-start(f32[1024,128]{1,0:T(8,128)S(1)} %slice_select_fusion.2), channel_id=1, source_target_pairs={{0,2},{1,3},{2,4},{3,5},{4,6},{5,7},{8,10},{9,11},{10,12},{11,13},... | collective-permute-start | bytes 1572872 | tf_op jit(solution)/shard_map/ppermute | solution.py:380
  62.6 13.8 %collective-permute-start.15 = (f32[1024,128]{1,0:T(8,128)S(1)}, f32[1024,128]{1,0:T(8,128)S(1)}, u32[]{:S(2)}, u32[]{:S(2)}) collective-permute-start(f32[1024,128]{1,0:T(8,128)S(1)} %select_select_fusion.4.mine_ref), channel_id=1, source_target_pairs={{0,1},{1,0},{2,3},{3,2},{4,5},{5,4},{6,7},{7,6},{8,9},{9,8},{10,11... | collective-permute-start | bytes 1572872 | tf_op jit(solution)/shard_map/ppermute | solution.py:387
  76.4 13.3 %collective-permute-start.16 = (f32[1024,128]{1,0:T(8,128)S(1)}, f32[1024,128]{1,0:T(8,128)S(1)}, u32[]{:S(2)}, u32[]{:S(2)}) collective-permute-start(f32[1024,128]{1,0:T(8,128)S(1)} %slice_select_fusion), channel_id=1, source_target_pairs={{0,2},{1,3},{2,4},{3,5},{4,6},{5,7},{8,10},{9,11},{10,12},{11,13},... | collective-permute-start | bytes 1572872 | tf_op jit(solution)/shard_map/ppermute | solution.py:380
  79.8 28.3 %collective-permute-start.20 = (f32[1024,128]{1,0:T(8,128)S(1)}, f32[1024,128]{1,0:T(8,128)S(1)}, u32[]{:S(2)}, u32[]{:S(2)}) collective-permute-start(f32[1024,128]{1,0:T(8,128)S(1)} %select_select_fusion.3.mine_ref), channel_id=1, source_target_pairs={{0,1},{1,0},{2,3},{3,2},{4,5},{5,4},{6,7},{7,6},{8,9},{9,8},{10,11... | collective-permute-start | bytes 1572872 | tf_op jit(solution)/shard_map/ppermute | solution.py:387
  89.6 15.2 %collective-permute-start.17 = (f32[1024,128]{1,0:T(8,128)S(1)}, f32[1024,128]{1,0:T(8,128)S(1)}, u32[]{:S(2)}, u32[]{:S(2)}) collective-permute-start(f32[1024,128]{1,0:T(8,128)S(1)} %collective-permute-done.16), channel_id=1, source_target_pairs={{2,4},{3,5},{4,6},{5,7},{10,12},{11,13},{12,14},{13,15},{18,20},{1... | collective-permute-start | bytes 1572872 | tf_op jit(solution)/shard_map/ppermute | solution.py:380
  91.2 27.4 %collective-permute-start.19 = (f32[1024,128]{1,0:T(8,128)S(1)}, f32[1024,128]{1,0:T(8,128)S(1)}, u32[]{:S(2)}, u32[]{:S(2)}) collective-permute-start(f32[1024,128]{1,0:T(8,128)S(1)} %select_select_fusion.2.mine_ref), channel_id=1, source_target_pairs={{0,1},{1,0},{2,3},{3,2},{4,5},{5,4},{6,7},{7,6},{8,9},{9,8},{10,11... | collective-permute-start | bytes 1572872 | tf_op jit(solution)/shard_map/ppermute | solution.py:387
  104.9 24.3 %collective-permute-start.18 = (f32[1024,128]{1,0:T(8,128)S(1)}, f32[1024,128]{1,0:T(8,128)S(1)}, u32[]{:S(2)}, u32[]{:S(2)}) collective-permute-start(f32[1024,128]{1,0:T(8,128)S(1)} %collective-permute-done.17), channel_id=1, source_target_pairs={{4,6},{5,7},{12,14},{13,15},{20,22},{21,23},{28,30},{29,31}} | collective-permute-start | bytes 1572872 | tf_op jit(solution)/shard_map/ppermute | solution.py:380
  106.3 23.1 %collective-permute-start.22 = (f32[1024,128]{1,0:T(8,128)S(1)}, f32[1024,128]{1,0:T(8,128)S(1)}, u32[]{:S(2)}, u32[]{:S(2)}) collective-permute-start(f32[1024,128]{1,0:T(8,128)S(1)} %select_select_fusion.1.mine_ref), channel_id=1, source_target_pairs={{0,1},{1,0},{2,3},{3,2},{4,5},{5,4},{6,7},{7,6},{8,9},{9,8},{10,11... | collective-permute-start | bytes 1572872 | tf_op jit(solution)/shard_map/ppermute | solution.py:387
  129.3 10.6 %collective-permute-start.21 = (f32[1024,128]{1,0:T(8,128)S(1)}, f32[1024,128]{1,0:T(8,128)S(1)}, u32[]{:S(2)}, u32[]{:S(2)}) collective-permute-start(f32[1024,128]{1,0:T(8,128)S(1)} %select_select_fusion.mine_ref), channel_id=1, source_target_pairs={{0,1},{1,0},{2,3},{3,2},{4,5},{5,4},{6,7},{7,6},{8,9},{9,8},{10,11... | collective-permute-start | bytes 1572872 | tf_op jit(solution)/shard_map/ppermute | solution.py:387

commit v7 on v6

--- a/solution.py
+++ b/solution.py
@@ -13,8 +13,8 @@
 CORES = 2
 VMEM_LIMIT = 40 * 1024 * 1024
 GROUP = 8
-IN_SLOTS = 5
-OUT_SLOTS = 3
+IN_SLOTS = 3
+OUT_SLOTS = 2
 PIECES = 4
 
 
@@ -269,7 +269,7 @@
 
 def update_rows(start, info, matrix, right, lower, inv_t, mine, other, out):
     rows, columns = mine.shape[0], matrix.shape[1]
-    block = 2 * TILE if columns % (2 * TILE) == 0 else TILE
+    block = next(b for b in (512, 640, 256, TILE) if columns % b == 0)
     any_spec = pl.BlockSpec(memory_space=pl.ANY)
     vmem = pl.BlockSpec(memory_space=pltpu.VMEM)
     in_specs = [pl.BlockSpec(memory_space=pltpu.SMEM), any_spec] + [vmem] * 5
@@ -306,11 +306,11 @@
     return lax.optimization_barrier((value, *earlier))[0]
 
 
-def double_rows(block, row, row_count):
+def double_rows(block, row, row_count, *earlier):
     stride = PANELS
     while stride < row_count:
         pairs = [(i, i + stride) for i in range(min(stride, row_count - stride))]
-        got = lax.ppermute(block, "row", pairs)
+        got = after(lax.ppermute(block, "row", pairs), *earlier)
         block = jnp.where(jnp.logical_and(row >= stride, row < 2 * stride), got, block)
         stride *= 2
     return block
@@ -339,15 +339,15 @@
     return jnp.concatenate([pick(got, (row - p) % row_count) for p in range(PANELS)], axis=0)
 
 
-def share_corner(column, place, core, col_count):
+def share_corner(column, earlier, place, core, col_count):
     got = [column]
     for shift in range(1, col_count // CORES):
         pairs = [(c, c + CORES * shift) for c in range(CORES)]
         got.append(lax.ppermute(column, "col", pairs))
-    column = pick(got, place)
+    column = after(pick(got, place), earlier)
     beside = lax.ppermute(column, "col", [(c, c ^ 1) for c in range(col_count)])
     halves = [jnp.where(core == 0, column, beside), jnp.where(core == 0, beside, column)]
-    return column, jnp.concatenate(halves, axis=1)
+    return jnp.concatenate(halves, axis=1)
 
 
 def per_device(matrix):
@@ -393,29 +393,25 @@
     got = fill(column)
     bands = [after(matrix[:TILE, :half], held[1]), after(matrix[:TILE, half:], held[1])]
     column = after(column, *bands)
-    bands = [double_rows(band, row, row_count) for band in bands]
-    column, corner = share_corner(column, place, core, col_count)
-    got = fill(column, bands[0])
+    bands[0] = double_rows(bands[0], row, row_count)
+    corner = share_corner(column, bands[0], place, core, col_count)
+    got = fill()
     while len(held) < depth:
-        got = fill()
+        got = fill(corner)
+    bands[1] = double_rows(bands[1], row, row_count, corner)
+    besides = [swap_rows(band, row_count) for band in bands]
     mark = exchange()
-    besides = [swap_rows(band, row_count) for band in bands]
     lower, inverse, inv_t = factor_corner(after(corner, held[-1], mark, bands[1]))
-    got = fill(inverse, ready[0][1], besides[0])
+    got = fill(inverse, besides[0])
     mark = exchange()
-    right = solve_columns(info, inverse, list(zip(bands, besides)))
+    right = solve_columns(info, after(inverse, held[-1]), list(zip(bands, besides)))
     out = None
     for chunk in range(chunks):
-        earlier = (mark,) if out is None else (mark, out)
-        closing = len(held) == last
-        if len(held) < last:
-            got = fill(*earlier)
-            mark = exchange(*earlier)
         mine, other = ready[chunk]
         other = after(other, held[-1], mark)
         out = update_rows(chunk * rows, info, matrix, right, lower, inv_t, mine, other, out)
-        if closing:
-            fill(out)
+        if len(held) <= last:
+            got = fill(mark, out)
             mark = exchange(out)
     return out
 

time: 154 us -> 142 us (0.922); the launches traced: 151 us -> 140 us
  waiting for transfers between devices: 39.9 us -> 33.9 us
  starting transfers between devices: 35.4 us -> 32.8 us
  Pallas kernels: 64.4 us -> 62.6 us
    ppermute x7, waiting for transfers between devices: 22.6 us -> 11.7 us  [fill(): return lax.ppermute(held[-1], 'col', hops) if slot < last else None]
    ppermute x3, waiting for transfers between devices: 17.3 us -> 21.7 us  [share_corner(): got.append(lax.ppermute(column, 'col', pairs))]
    ppermute x1, starting transfers between devices: 5.18 us -> 2.83 us  [share_corner(): beside = lax.ppermute(column, 'col', [(c, c ^ 1) for c in range(col_count)])]
    pallas_call x5, Pallas kernels: 52.7 us -> 50.8 us  [update_rows(): pl.pallas_call(functools.partial(update_kernel, start, block), in_specs=i...]
  transfers between devices with their start and end apart: 23 -> 23, of which waited for: 4 -> 6; matrix products, arithmetic and copies ran while one was open for 5% -> 6% of each run, Pallas kernels for 36% -> 37%
where the time goes in v7:
time: 142 us; the launch traced here: 140 us
  Pallas kernels  62.6 us (44%)
  waiting for transfers between devices  33.9 us (24%)
  starting transfers between devices  32.8 us (23%)
  other arithmetic  7.14 us (5%)
  local copies, waits for them, and re-layouts  3.3 us (2%)
    pallas_call x5, Pallas kernels, update_rows(): pl.pallas_call(functools.partial(update_kernel, start, block), in_specs=i...  50.8 us
    ppermute x3, waiting for transfers between devices, share_corner(): got.append(lax.ppermute(column, 'col', pairs))  21.7 us
    ppermute x7, waiting for transfers between devices, fill(): return lax.ppermute(held[-1], 'col', hops) if slot < last else None  11.7 us
    pallas_call x1, Pallas kernels, factor_corner(): pl.pallas_call(corner_kernel, out_shape=(jax.ShapeDtypeStruct((WIDE, WIDE...  9.83 us
    ppermute x5, starting transfers between devices, exchange(): ready.append((mine, lax.ppermute(mine, 'col', swap)))  8.72 us
    ppermute x7, starting transfers between devices, fill(): return lax.ppermute(held[-1], 'col', hops) if slot < last else None  8.01 us
    ppermute x2, starting transfers between devices, double_rows(): got = after(lax.ppermute(block, 'row', pairs), *earlier)  6.18 us
    select_n x4, other arithmetic, fill(): block = own if got is None else jnp.where(place == 0, own, got)  4.56 us
  transfers between devices with their start and end apart: 23, of which 6 were waited for; matrix products, arithmetic and copies ran while one was open for 6% of the time, Pallas kernels for 37%

profile of v7, /device:TPU:25, one launch (start us, length us, event | category | flops | bytes accessed | tf_op | source)
XLA Modules:
  0.0 140.3 jit_solution(10068579506352581149)
XLA Ops:
  0.0 1.1 slice.25
  4.8 1.1 slice_select_fusion.3
  6.6 1.4 fusion
  8.0 4.0 %collective-permute-start.7 = (f32[128,1280]{1,0:T(8,128)S(1)}, f32[128,1280]{1,0:T(8,128)}, u32[]{:S(2)}, u32[]{:S(2)}) collective-permute-start(f32[128,1280]{1,0:T(8,128)S(1)} %get-tuple-element.34), channel_id=1, source_target_pairs={{0,16},{8,24},{1,17},{9,25},{2,18},{10,26},{3,19},{11,27},{4,20},{... | collective-permute-start | bytes 1966088 | tf_op jit(solution)/shard_map/ppermute | solution.py:313
  13.3 1.3 collective-permute-start.4
  14.7 2.2 %collective-permute-start.11 = (f32[128,1280]{1,0:T(8,128)S(1)}, f32[128,1280]{1,0:T(8,128)}, u32[]{:S(2)}, u32[]{:S(2)}) collective-permute-start(f32[128,1280]{1,0:T(8,128)S(1)} %get-tuple-element.35), channel_id=1, source_target_pairs={{0,16},{8,24},{1,17},{9,25},{2,18},{10,26},{3,19},{11,27},{4,20},{... | collective-permute-start | bytes 1966088 | tf_op jit(solution)/shard_map/ppermute | solution.py:313
  16.8 21.7 %collective-permute-done.4 = f32[256,128]{1,0:T(8,128)S(1)} collective-permute-done((f32[256,128]{1,0:T(8,128)S(1)}, f32[256,128]{1,0:T(8,128)S(1)}, u32[]{:S(2)}, u32[]{:S(2)}) %collective-permute-start.4) | collective-permute-done | bytes 131104 | tf_op jit(solution)/shard_map/ppermute | solution.py:346
  39.2 1.1 slice_select_fusion.1
  40.3 1.3 collective-permute-start.10
  41.7 2.8 %collective-permute-start.8 = (f32[256,128]{1,0:T(8,128)}, f32[256,128]{1,0:T(8,128)S(1)}, u32[]{:S(2)}, u32[]{:S(2)}) collective-permute-start(f32[256,128]{1,0:T(8,128)} %select_select_fusion.5), channel_id=1, source_target_pairs={{0,1},{1,0},{2,3},{3,2},{4,5},{5,4},{6,7},{7,6},{8,9},{9,8},{10,11... | collective-permute-start | bytes 393224 | tf_op jit(solution)/shard_map/ppermute | solution.py:348
  44.6 1.2 collective-permute-start.13
  45.8 0.9 broadcast_select_fusion.3
  46.8 6.2 %collective-permute-done.10 = f32[1024,128]{1,0:T(8,128)} collective-permute-done((f32[1024,128]{1,0:T(8,128)S(1)}, f32[1024,128]{1,0:T(8,128)}, u32[]{:S(2)}, u32[]{:S(2)}) %collective-permute-start.10) | collective-permute-done | bytes 524320 | tf_op jit(solution)/shard_map/ppermute | solution.py:380
  53.0 1.3 slice_select_fusion.2
  54.2 1.3 collective-permute-start.12
  55.6 1.3 collective-permute-start.14
  57.1 4.0 %collective-permute-start.16 = (f32[1024,128]{1,0:T(8,128)S(1)}, f32[1024,128]{1,0:T(8,128)S(1)}, u32[]{:S(2)}, u32[]{:S(2)}) collective-permute-start(f32[1024,128]{1,0:T(8,128)S(1)} %select_select_fusion.4.mine_ref), channel_id=1, source_target_pairs={{0,1},{1,0},{2,3},{3,2},{4,5},{5,4},{6,7},{7,6},{8,9},{9,8},{10,11... | collective-permute-start | bytes 1572872 | tf_op jit(solution)/shard_map/ppermute | solution.py:387
  61.1 9.8 %shard_map.17 = (f32[256,256]{1,0:T(8,128)S(1)}, bf16[256,768]{1,0:T(8,128)(2,1)S(1)}, bf16[768,256]{1,0:T(8,128)(2,1)S(1)}) custom-call(f32[256,256]{1,0:T(8,128)S(1)} %pad_maximum_fusion.corner_ref), custom_call_target="tpu_custom_call" | custom-call | flops 40000000 | bytes 1048576 | tf_op jit(solution)/shard_map/pallas_call | solution.py:132
  70.9 1.1 slice_select_fusion
  72.0 1.5 %collective-permute-start.15 = (f32[1024,128]{1,0:T(8,128)S(1)}, f32[1024,128]{1,0:T(8,128)S(1)}, u32[]{:S(2)}, u32[]{:S(2)}) collective-permute-start(f32[1024,128]{1,0:T(8,128)S(1)} %slice_select_fusion), channel_id=1, source_target_pairs={{0,2},{1,3},{2,4},{3,5},{4,6},{5,7},{8,10},{9,11},{10,12},{11,13},... | collective-permute-start | bytes 1572872 | tf_op jit(solution)/shard_map/ppermute | solution.py:380
  74.2 1.9 %shard_map.18.right_ref = bf16[768,2560]{1,0:T(8,128)(2,1)S(1)} custom-call(s32[4]{0:T(128)S(1)} %pad_add_fusion.info_ref, bf16[256,768]{1,0:T(8,128)(2,1)S(1)} %get-tuple-element.43.inv_ref, f32[128,1280]{1,0:T(8,128)S(1)} %broadcast_select_fusion.1.refs_0_, f32[128,1280]{1,0:T(8,128)S(1)} %collective-permute-done.13.refs_1_, ...), custom_call_target="tpu_custom_call" | custom-call | flops 1006632960 | bytes 5242880 | tf_op jit(solution)/shard_map/pallas_call | solution.py:163
  76.1 10.2 %shard_map.19.refs_0_ = f32[5120,2560]{1,0:T(8,128)} custom-call(s32[4]{0:T(128)S(1)} %pad_add_fusion.info_ref, f32[5120,2560]{1,0:T(8,128)} %mat_ref.9, bf16[768,2560]{1,0:T(8,128)(2,1)S(1)} %shard_map.18.right_ref, f32[256,256]{1,0:T(8,128)S(1)} %get-tuple-element.44.lower_ref, bf16[768,256]{1,0:T(8,128)(2,1)S(1)} %get-tuple-element.45.inv_t_ref, ...), custom_call_target="tpu_custom_call" | custom-call | flops 4026531840 | bytes 20971520 | tf_op jit(solution)/shard_map/pallas_call | solution.py:282
  86.3 2.3 %collective-permute-done.15 = f32[1024,128]{1,0:T(8,128)S(1)} collective-permute-done((f32[1024,128]{1,0:T(8,128)S(1)}, f32[1024,128]{1,0:T(8,128)S(1)}, u32[]{:S(2)}, u32[]{:S(2)}) %collective-permute-start.15) | collective-permute-done | bytes 524320 | tf_op jit(solution)/shard_map/ppermute | solution.py:380
  88.6 1.3 collective-permute-start.17
  90.7 10.2 %shard_map.20.refs_0_ = f32[5120,2560]{1,0:T(8,128)} custom-call(s32[4]{0:T(128)S(1)} %pad_add_fusion.info_ref, f32[5120,2560]{1,0:T(8,128)} %mat_ref.9, bf16[768,2560]{1,0:T(8,128)(2,1)S(1)} %shard_map.18.right_ref, f32[256,256]{1,0:T(8,128)S(1)} %get-tuple-element.44.lower_ref, ...), custom_call_target="tpu_custom_call", output_to_operand_aliasing={{}: (7, {})} | custom-call | flops 4026531840 | bytes 20971520 | tf_op jit(solution)/shard_map/pallas_call | solution.py:282
  100.9 2.5 %collective-permute-done.17 = f32[1024,128]{1,0:T(8,128)S(1)} collective-permute-done((f32[1024,128]{1,0:T(8,128)S(1)}, f32[1024,128]{1,0:T(8,128)S(1)}, u32[]{:S(2)}, u32[]{:S(2)}) %collective-permute-start.17) | collective-permute-done | bytes 524320 | tf_op jit(solution)/shard_map/ppermute | solution.py:380
  103.4 1.3 collective-permute-start.19
  104.8 1.5 %collective-permute-start.22 = (f32[1024,128]{1,0:T(8,128)S(1)}, f32[1024,128]{1,0:T(8,128)S(1)}, u32[]{:S(2)}, u32[]{:S(2)}) collective-permute-start(f32[1024,128]{1,0:T(8,128)S(1)} %select_select_fusion.1.mine_ref), channel_id=1, source_target_pairs={{0,1},{1,0},{2,3},{3,2},{4,5},{5,4},{6,7},{7,6},{8,9},{9,8},{10,11... | collective-permute-start | bytes 1572872 | tf_op jit(solution)/shard_map/ppermute | solution.py:387
  106.3 10.2 %shard_map.21.refs_0_ = f32[5120,2560]{1,0:T(8,128)} custom-call(s32[4]{0:T(128)S(1)} %pad_add_fusion.info_ref, f32[5120,2560]{1,0:T(8,128)} %mat_ref.9, bf16[768,2560]{1,0:T(8,128)(2,1)S(1)} %shard_map.18.right_ref, f32[256,256]{1,0:T(8,128)S(1)} %get-tuple-element.44.lower_ref, ...), custom_call_target="tpu_custom_call", output_to_operand_aliasing={{}: (7, {})} | custom-call | flops 4026531840 | bytes 20971520 | tf_op jit(solution)/shard_map/pallas_call | solution.py:282
  117.3 2.4 %collective-permute-start.21 = (f32[1024,128]{1,0:T(8,128)S(1)}, f32[1024,128]{1,0:T(8,128)S(1)}, u32[]{:S(2)}, u32[]{:S(2)}) collective-permute-start(f32[1024,128]{1,0:T(8,128)S(1)} %select_select_fusion.mine_ref), channel_id=1, source_target_pairs={{0,1},{1,0},{2,3},{3,2},{4,5},{5,4},{6,7},{7,6},{8,9},{9,8},{10,11... | collective-permute-start | bytes 1572872 | tf_op jit(solution)/shard_map/ppermute | solution.py:387
  119.8 10.2 %shard_map.22.refs_0_ = f32[5120,2560]{1,0:T(8,128)} custom-call(s32[4]{0:T(128)S(1)} %pad_add_fusion.info_ref, f32[5120,2560]{1,0:T(8,128)} %mat_ref.9, bf16[768,2560]{1,0:T(8,128)(2,1)S(1)} %shard_map.18.right_ref, f32[256,256]{1,0:T(8,128)S(1)} %get-tuple-element.44.lower_ref, ...), custom_call_target="tpu_custom_call", output_to_operand_aliasing={{}: (7, {})} | custom-call | flops 4026531840 | bytes 20971520 | tf_op jit(solution)/shard_map/pallas_call | solution.py:282
  129.9 10.2 %shard_map.23 = f32[5120,2560]{1,0:T(8,128)} custom-call(s32[4]{0:T(128)S(1)} %pad_add_fusion.info_ref, f32[5120,2560]{1,0:T(8,128)} %mat_ref.9, bf16[768,2560]{1,0:T(8,128)(2,1)S(1)} %shard_map.18.right_ref, f32[256,256]{1,0:T(8,128)S(1)} %get-tuple-element.44.lower_ref, ...), custom_call_target="tpu_custom_call", output_to_operand_aliasing={{}: (7, {})} | custom-call | flops 4026531840 | bytes 20971520 | tf_op jit(solution)/shard_map/pallas_call | solution.py:282
  (41 shorter events, 9.1 us)
Async XLA Ops:
  1.1 3.7 %collective-permute-start.3 = (f32[1024,128]{1,0:T(8,128)S(1)}, f32[1024,128]{1,0:T(8,128)S(1)}, u32[]{:S(2)}, u32[]{:S(2)}) collective-permute-start(f32[1024,128]{1,0:T(8,128)S(1)} %slice.25), channel_id=1, source_target_pairs={{0,2},{1,3},{8,10},{9,11},{16,18},{17,19},{24,26},{25,27}} | collective-permute-start | bytes 1572872 | tf_op jit(solution)/shard_map/ppermute | solution.py:380
  2.6 2.1 %collective-permute-start.2 = (f32[128,128]{1,0:T(8,128)S(1)}, f32[128,128]{1,0:T(8,128)S(1)}, u32[]{:S(2)}, u32[]{:S(2)}) collective-permute-start(f32[128,128]{1,0:T(8,128)S(1)} %slice.24), channel_id=1, source_target_pairs={{0,8},{1,9},{8,16},{9,17}} | collective-permute-start | bytes 196616 | tf_op jit(solution)/shard_map/ppermute | solution.py:338
  3.3 1.4 %collective-permute-start.1 = (f32[128,128]{1,0:T(8,128)S(1)}, f32[128,128]{1,0:T(8,128)S(1)}, u32[]{:S(2)}, u32[]{:S(2)}) collective-permute-start(f32[128,128]{1,0:T(8,128)S(1)} %slice.24), channel_id=1, source_target_pairs={{0,16},{1,17},{8,24},{9,25}} | collective-permute-start | bytes 196616 | tf_op jit(solution)/shard_map/ppermute | solution.py:338
  4.0 0.8 collective-permute-start
  5.9 33.3 %collective-permute-start.9 = (f32[1024,128]{1,0:T(8,128)S(1)}, f32[1024,128]{1,0:T(8,128)S(1)}, u32[]{:S(2)}, u32[]{:S(2)}) collective-permute-start(f32[1024,128]{1,0:T(8,128)S(1)} %slice_select_fusion.3), channel_id=1, source_target_pairs={{0,2},{1,3},{2,4},{3,5},{8,10},{9,11},{10,12},{11,13},{16,18},{17,... | collective-permute-start | bytes 1572872 | tf_op jit(solution)/shard_map/ppermute | solution.py:380
  8.0 33.7 %collective-permute-start.7 = (f32[128,1280]{1,0:T(8,128)S(1)}, f32[128,1280]{1,0:T(8,128)}, u32[]{:S(2)}, u32[]{:S(2)}) collective-permute-start(f32[128,1280]{1,0:T(8,128)S(1)} %get-tuple-element.34), channel_id=1, source_target_pairs={{0,16},{8,24},{1,17},{9,25},{2,18},{10,26},{3,19},{11,27},{4,20},{... | collective-permute-start | bytes 1966088 | tf_op jit(solution)/shard_map/ppermute | solution.py:313
  12.0 2.7 %collective-permute-start.6 = (f32[256,128]{1,0:T(8,128)S(1)}, f32[256,128]{1,0:T(8,128)S(1)}, u32[]{:S(2)}, u32[]{:S(2)}) collective-permute-start(f32[256,128]{1,0:T(8,128)S(1)} %pad_maximum_fusion.1), channel_id=1, source_target_pairs={{0,2},{1,3},{8,10},{9,11},{16,18},{17,19},{24,26},{25,27}} | collective-permute-start | bytes 393224 | tf_op jit(solution)/shard_map/ppermute | solution.py:346
  12.7 4.2 %collective-permute-start.5 = (f32[256,128]{1,0:T(8,128)S(1)}, f32[256,128]{1,0:T(8,128)S(1)}, u32[]{:S(2)}, u32[]{:S(2)}) collective-permute-start(f32[256,128]{1,0:T(8,128)S(1)} %pad_maximum_fusion.1), channel_id=1, source_target_pairs={{0,4},{1,5},{8,12},{9,13},{16,20},{17,21},{24,28},{25,29}} | collective-permute-start | bytes 393224 | tf_op jit(solution)/shard_map/ppermute | solution.py:346
  13.3 25.2 %collective-permute-start.4 = (f32[256,128]{1,0:T(8,128)S(1)}, f32[256,128]{1,0:T(8,128)S(1)}, u32[]{:S(2)}, u32[]{:S(2)}) collective-permute-start(f32[256,128]{1,0:T(8,128)S(1)} %pad_maximum_fusion.1), channel_id=1, source_target_pairs={{0,6},{1,7},{8,14},{9,15},{16,22},{17,23},{24,30},{25,31}} | collective-permute-start | bytes 393224 | tf_op jit(solution)/shard_map/ppermute | solution.py:346
  14.7 32.1 %collective-permute-start.11 = (f32[128,1280]{1,0:T(8,128)S(1)}, f32[128,1280]{1,0:T(8,128)}, u32[]{:S(2)}, u32[]{:S(2)}) collective-permute-start(f32[128,1280]{1,0:T(8,128)S(1)} %get-tuple-element.35), channel_id=1, source_target_pairs={{0,16},{8,24},{1,17},{9,25},{2,18},{10,26},{3,19},{11,27},{4,20},{... | collective-permute-start | bytes 1966088 | tf_op jit(solution)/shard_map/ppermute | solution.py:313
  40.3 12.7 %collective-permute-start.10 = (f32[1024,128]{1,0:T(8,128)S(1)}, f32[1024,128]{1,0:T(8,128)}, u32[]{:S(2)}, u32[]{:S(2)}) collective-permute-start(f32[1024,128]{1,0:T(8,128)S(1)} %slice_select_fusion.1), channel_id=1, source_target_pairs={{0,2},{1,3},{2,4},{3,5},{4,6},{5,7},{8,10},{9,11},{10,12},{11,13},... | collective-permute-start | bytes 1572872 | tf_op jit(solution)/shard_map/ppermute | solution.py:380
  41.7 4.1 %collective-permute-start.8 = (f32[256,128]{1,0:T(8,128)}, f32[256,128]{1,0:T(8,128)S(1)}, u32[]{:S(2)}, u32[]{:S(2)}) collective-permute-start(f32[256,128]{1,0:T(8,128)} %select_select_fusion.5), channel_id=1, source_target_pairs={{0,1},{1,0},{2,3},{3,2},{4,5},{5,4},{6,7},{7,6},{8,9},{9,8},{10,11... | collective-permute-start | bytes 393224 | tf_op jit(solution)/shard_map/ppermute | solution.py:348
  44.6 27.4 %collective-permute-start.13 = (f32[128,1280]{1,0:T(8,128)S(1)}, f32[128,1280]{1,0:T(8,128)S(1)}, u32[]{:S(2)}, u32[]{:S(2)}) collective-permute-start(f32[128,1280]{1,0:T(8,128)S(1)} %broadcast_select_fusion.1.refs_0_), channel_id=1, source_target_pairs={{0,8},{8,0},{16,24},{24,16},{1,9},{9,1},{17,25},{25,17},{2,10},{10... | collective-permute-start | bytes 1966088 | tf_op jit(solution)/shard_map/ppermute | solution.py:320
  54.2 16.7 %collective-permute-start.12 = (f32[1024,128]{1,0:T(8,128)S(1)}, f32[1024,128]{1,0:T(8,128)S(1)}, u32[]{:S(2)}, u32[]{:S(2)}) collective-permute-start(f32[1024,128]{1,0:T(8,128)S(1)} %slice_select_fusion.2), channel_id=1, source_target_pairs={{0,2},{1,3},{2,4},{3,5},{4,6},{5,7},{8,10},{9,11},{10,12},{11,13},... | collective-permute-start | bytes 1572872 | tf_op jit(solution)/shard_map/ppermute | solution.py:380
  55.6 18.6 %collective-permute-start.14 = (f32[128,1280]{1,0:T(8,128)S(1)}, f32[128,1280]{1,0:T(8,128)S(1)}, u32[]{:S(2)}, u32[]{:S(2)}) collective-permute-start(f32[128,1280]{1,0:T(8,128)S(1)} %broadcast_select_fusion.refs_2_), channel_id=1, source_target_pairs={{0,8},{8,0},{16,24},{24,16},{1,9},{9,1},{17,25},{25,17},{2,10},{10... | collective-permute-start | bytes 1966088 | tf_op jit(solution)/shard_map/ppermute | solution.py:320
  57.1 16.7 %collective-permute-start.16 = (f32[1024,128]{1,0:T(8,128)S(1)}, f32[1024,128]{1,0:T(8,128)S(1)}, u32[]{:S(2)}, u32[]{:S(2)}) collective-permute-start(f32[1024,128]{1,0:T(8,128)S(1)} %select_select_fusion.4.mine_ref), channel_id=1, source_target_pairs={{0,1},{1,0},{2,3},{3,2},{4,5},{5,4},{6,7},{7,6},{8,9},{9,8},{10,11... | collective-permute-start | bytes 1572872 | tf_op jit(solution)/shard_map/ppermute | solution.py:387
  72.0 16.6 %collective-permute-start.15 = (f32[1024,128]{1,0:T(8,128)S(1)}, f32[1024,128]{1,0:T(8,128)S(1)}, u32[]{:S(2)}, u32[]{:S(2)}) collective-permute-start(f32[1024,128]{1,0:T(8,128)S(1)} %slice_select_fusion), channel_id=1, source_target_pairs={{0,2},{1,3},{2,4},{3,5},{4,6},{5,7},{8,10},{9,11},{10,12},{11,13},... | collective-permute-start | bytes 1572872 | tf_op jit(solution)/shard_map/ppermute | solution.py:380
  73.7 17.0 %collective-permute-start.18 = (f32[1024,128]{1,0:T(8,128)S(1)}, f32[1024,128]{1,0:T(8,128)S(1)}, u32[]{:S(2)}, u32[]{:S(2)}) collective-permute-start(f32[1024,128]{1,0:T(8,128)S(1)} %select_select_fusion.3.mine_ref), channel_id=1, source_target_pairs={{0,1},{1,0},{2,3},{3,2},{4,5},{5,4},{6,7},{7,6},{8,9},{9,8},{10,11... | collective-permute-start | bytes 1572872 | tf_op jit(solution)/shard_map/ppermute | solution.py:387
  88.6 14.8 %collective-permute-start.17 = (f32[1024,128]{1,0:T(8,128)S(1)}, f32[1024,128]{1,0:T(8,128)S(1)}, u32[]{:S(2)}, u32[]{:S(2)}) collective-permute-start(f32[1024,128]{1,0:T(8,128)S(1)} %collective-permute-done.15), channel_id=1, source_target_pairs={{2,4},{3,5},{4,6},{5,7},{10,12},{11,13},{12,14},{13,15},{18,20},{1... | collective-permute-start | bytes 1572872 | tf_op jit(solution)/shard_map/ppermute | solution.py:380
  90.0 16.2 %collective-permute-start.20 = (f32[1024,128]{1,0:T(8,128)S(1)}, f32[1024,128]{1,0:T(8,128)S(1)}, u32[]{:S(2)}, u32[]{:S(2)}) collective-permute-start(f32[1024,128]{1,0:T(8,128)S(1)} %select_select_fusion.2.mine_ref), channel_id=1, source_target_pairs={{0,1},{1,0},{2,3},{3,2},{4,5},{5,4},{6,7},{7,6},{8,9},{9,8},{10,11... | collective-permute-start | bytes 1572872 | tf_op jit(solution)/shard_map/ppermute | solution.py:387
  103.4 13.8 %collective-permute-start.19 = (f32[1024,128]{1,0:T(8,128)S(1)}, f32[1024,128]{1,0:T(8,128)S(1)}, u32[]{:S(2)}, u32[]{:S(2)}) collective-permute-start(f32[1024,128]{1,0:T(8,128)S(1)} %collective-permute-done.17), channel_id=1, source_target_pairs={{4,6},{5,7},{12,14},{13,15},{20,22},{21,23},{28,30},{29,31}} | collective-permute-start | bytes 1572872 | tf_op jit(solution)/shard_map/ppermute | solution.py:380
  104.8 15.0 %collective-permute-start.22 = (f32[1024,128]{1,0:T(8,128)S(1)}, f32[1024,128]{1,0:T(8,128)S(1)}, u32[]{:S(2)}, u32[]{:S(2)}) collective-permute-start(f32[1024,128]{1,0:T(8,128)S(1)} %select_select_fusion.1.mine_ref), channel_id=1, source_target_pairs={{0,1},{1,0},{2,3},{3,2},{4,5},{5,4},{6,7},{7,6},{8,9},{9,8},{10,11... | collective-permute-start | bytes 1572872 | tf_op jit(solution)/shard_map/ppermute | solution.py:387
  117.3 12.6 %collective-permute-start.21 = (f32[1024,128]{1,0:T(8,128)S(1)}, f32[1024,128]{1,0:T(8,128)S(1)}, u32[]{:S(2)}, u32[]{:S(2)}) collective-permute-start(f32[1024,128]{1,0:T(8,128)S(1)} %select_select_fusion.mine_ref), channel_id=1, source_target_pairs={{0,1},{1,0},{2,3},{3,2},{4,5},{5,4},{6,7},{7,6},{8,9},{9,8},{10,11... | collective-permute-start | bytes 1572872 | tf_op jit(solution)/shard_map/ppermute | solution.py:387

commit v8 on v7

--- a/solution.py
+++ b/solution.py
@@ -109,14 +109,21 @@
     return jnp.concatenate(upper, axis=0), jnp.concatenate(inverse, axis=0)
 
 
-def corner_kernel(corner_ref, low_ref, inv_ref, inv_t_ref):
+def first_kernel(corner_ref, upper_ref, inv_ref, low_ref, square_ref):
+    upper, inverse = factor_tile(corner_ref[:TILE, :TILE])
+    low = dot_full(corner_ref[TILE:, :TILE], inverse, ((1,), (1,)))
+    upper_ref[...] = upper
+    inv_ref[...] = inverse
+    low_ref[...] = low
+    square_ref[...] = corner_ref[TILE:, TILE:] - dot_full(low, low, ((1,), (1,)))
+
+
+def second_kernel(upper_ref, inv_0_ref, low_10_ref, square_ref, low_ref, inv_ref, inv_t_ref):
     zero = jnp.zeros((TILE, TILE), jnp.float32)
-    upper_0, inv_0 = factor_tile(corner_ref[:TILE, :TILE])
-    low_10 = dot_full(corner_ref[TILE:, :TILE], inv_0, ((1,), (1,)))
-    square = corner_ref[TILE:, TILE:] - dot_full(low_10, low_10, ((1,), (1,)))
-    upper_1, inv_1 = factor_tile(square)
+    inv_0, low_10 = inv_0_ref[...], low_10_ref[...]
+    upper_1, inv_1 = factor_tile(square_ref[...])
     inv_10 = -dot_full(inv_1, dot_full(low_10, inv_0))
-    low_ref[:TILE, :TILE] = upper_0.T
+    low_ref[:TILE, :TILE] = upper_ref[...].T
     low_ref[:TILE, TILE:] = zero
     low_ref[TILE:, :TILE] = low_10
     low_ref[TILE:, TILE:] = upper_1.T
@@ -128,17 +135,27 @@
     stack_halves(inv_t_ref, jnp.concatenate([first, second], axis=0))
 
 
-def factor_corner(corner):
+def factor_first(corner):
+    tile = jax.ShapeDtypeStruct((TILE, TILE), jnp.float32)
     return pl.pallas_call(
-        corner_kernel,
+        first_kernel,
+        out_shape=(tile,) * 4,
+        compiler_params=pltpu.CompilerParams(vmem_limit_bytes=VMEM_LIMIT),
+        cost_estimate=pl.CostEstimate(flops=20_000_000, bytes_accessed=1 << 19, transcendentals=0),
+    )(corner)
+
+
+def factor_second(*parts):
+    return pl.pallas_call(
+        second_kernel,
         out_shape=(
             jax.ShapeDtypeStruct((WIDE, WIDE), jnp.float32),
             jax.ShapeDtypeStruct((WIDE, 3 * WIDE), jnp.bfloat16),
             jax.ShapeDtypeStruct((3 * WIDE, WIDE), jnp.bfloat16),
         ),
         compiler_params=pltpu.CompilerParams(vmem_limit_bytes=VMEM_LIMIT),
-        cost_estimate=pl.CostEstimate(flops=40_000_000, bytes_accessed=1 << 20, transcendentals=0),
-    )(corner)
+        cost_estimate=pl.CostEstimate(flops=20_000_000, bytes_accessed=1 << 20, transcendentals=0),
+    )(*parts)
 
 
 def columns_kernel(info_ref, inv_ref, *refs):
@@ -396,12 +413,14 @@
     bands[0] = double_rows(bands[0], row, row_count)
     corner = share_corner(column, bands[0], place, core, col_count)
     got = fill()
+    parts = factor_first(after(corner, held[2]))
     while len(held) < depth:
-        got = fill(corner)
-    bands[1] = double_rows(bands[1], row, row_count, corner)
+        got = fill(parts[3])
+    bands[1] = double_rows(bands[1], row, row_count, parts[3])
     besides = [swap_rows(band, row_count) for band in bands]
     mark = exchange()
-    lower, inverse, inv_t = factor_corner(after(corner, held[-1], mark, bands[1]))
+    square = after(parts[3], held[-1], mark, bands[1])
+    lower, inverse, inv_t = factor_second(*parts[:3], square)
     got = fill(inverse, besides[0])
     mark = exchange()
     right = solve_columns(info, after(inverse, held[-1]), list(zip(bands, besides)))

time: 142 us -> 140 us (0.986)
  waiting for transfers between devices: 33.9 us -> 25.3 us
  starting transfers between devices: 32.8 us -> 39.1 us
    ppermute x7, waiting for transfers between devices: 11.7 us -> 2.75 us  [fill(): return lax.ppermute(held[-1], 'col', hops) if slot < last else None]
    ppermute x5, starting transfers between devices: 8.72 us -> 15 us  [exchange(): ready.append((mine, lax.ppermute(mine, 'col', swap)))]
    pallas_call x1 -> x2, Pallas kernels: 9.83 us -> 9.98 us  [the longest x1 5.34 us: factor_first(): pl.pallas_call(first_kernel, out_shape=(tile,) * 4, compiler_params=pltpu...]
  transfers between devices with their start and end apart: 23 -> 23, of which waited for: 6 -> 5; matrix products, arithmetic and copies ran while one was open for 6% -> 6% of each run, Pallas kernels for 37% -> 38%
where the time goes in v8:
time: 140 us; the launch traced here: 138 us
  Pallas kernels  62.7 us (45%)
  starting transfers between devices  39.1 us (28%)
  waiting for transfers between devices  25.3 us (18%)
  other arithmetic  7.14 us (5%)
  local copies, waits for them, and re-layouts  3.3 us (2%)
    pallas_call x5, Pallas kernels, update_rows(): pl.pallas_call(functools.partial(update_kernel, start, block), in_specs=i...  50.8 us
    ppermute x3, waiting for transfers between devices, share_corner(): got.append(lax.ppermute(column, 'col', pairs))  21.7 us
    ppermute x5, starting transfers between devices, exchange(): ready.append((mine, lax.ppermute(mine, 'col', swap)))  15 us
    ppermute x7, starting transfers between devices, fill(): return lax.ppermute(held[-1], 'col', hops) if slot < last else None  8.02 us
    ppermute x2, starting transfers between devices, double_rows(): got = after(lax.ppermute(block, 'row', pairs), *earlier)  6.17 us
    pallas_call x1, Pallas kernels, factor_first(): pl.pallas_call(first_kernel, out_shape=(tile,) * 4, compiler_params=pltpu...  5.34 us
    pallas_call x1, Pallas kernels, factor_second(): pl.pallas_call(second_kernel, out_shape=(jax.ShapeDtypeStruct((WIDE, WIDE...  4.63 us
    select_n x4, other arithmetic, fill(): block = own if got is None else jnp.where(place == 0, own, got)  4.56 us
  transfers between devices with their start and end apart: 23, of which 5 were waited for; matrix products, arithmetic and copies ran while one was open for 6% of the time, Pallas kernels for 38%

profile of v8, /device:TPU:25, one launch (start us, length us, event | category | flops | bytes accessed | tf_op | source)
XLA Modules:
  0.0 138.1 jit_solution(12940868859737608950)
XLA Ops:
  0.0 1.1 slice.25
  4.8 1.1 slice_select_fusion.3
  6.6 1.4 fusion
  8.0 4.0 %collective-permute-start.7 = (f32[128,1280]{1,0:T(8,128)S(1)}, f32[128,1280]{1,0:T(8,128)}, u32[]{:S(2)}, u32[]{:S(2)}) collective-permute-start(f32[128,1280]{1,0:T(8,128)S(1)} %get-tuple-element.39), channel_id=1, source_target_pairs={{0,16},{8,24},{1,17},{9,25},{2,18},{10,26},{3,19},{11,27},{4,20},{... | collective-permute-start | bytes 1966088 | tf_op jit(solution)/shard_map/ppermute | solution.py:330
  13.3 1.3 collective-permute-start.4
  14.7 2.1 %collective-permute-start.11 = (f32[128,1280]{1,0:T(8,128)S(1)}, f32[128,1280]{1,0:T(8,128)}, u32[]{:S(2)}, u32[]{:S(2)}) collective-permute-start(f32[128,1280]{1,0:T(8,128)S(1)} %get-tuple-element.40), channel_id=1, source_target_pairs={{0,16},{8,24},{1,17},{9,25},{2,18},{10,26},{3,19},{11,27},{4,20},{... | collective-permute-start | bytes 1966088 | tf_op jit(solution)/shard_map/ppermute | solution.py:330
  16.8 21.7 %collective-permute-done.4 = f32[256,128]{1,0:T(8,128)S(1)} collective-permute-done((f32[256,128]{1,0:T(8,128)S(1)}, f32[256,128]{1,0:T(8,128)S(1)}, u32[]{:S(2)}, u32[]{:S(2)}) %collective-permute-start.4) | collective-permute-done | bytes 131104 | tf_op jit(solution)/shard_map/ppermute | solution.py:363
  39.2 1.1 slice_select_fusion.2
  40.3 1.3 collective-permute-start.10
  41.7 2.8 %collective-permute-start.8 = (f32[256,128]{1,0:T(8,128)}, f32[256,128]{1,0:T(8,128)S(1)}, u32[]{:S(2)}, u32[]{:S(2)}) collective-permute-start(f32[256,128]{1,0:T(8,128)} %select_select_fusion.5), channel_id=1, source_target_pairs={{0,1},{1,0},{2,3},{3,2},{4,5},{5,4},{6,7},{7,6},{8,9},{9,8},{10,11... | collective-permute-start | bytes 393224 | tf_op jit(solution)/shard_map/ppermute | solution.py:365
  44.6 1.2 collective-permute-start.13
  46.8 5.3 %shard_map.17 = (f32[128,128]{1,0:T(8,128)S(1)}, f32[128,128]{1,0:T(8,128)S(1)}, f32[128,128]{1,0:T(8,128)S(1)}, f32[128,128]{1,0:T(8,128)S(1)}) custom-call(f32[256,256]{1,0:T(8,128)S(1)} %pad_maximum_fusion.corner_ref), custom_call_target="tpu_custom_call" | custom-call | flops 20000000 | bytes 524288 | tf_op jit(solution)/shard_map/pallas_call | solution.py:140
  53.0 1.3 slice_select_fusion.1
  54.2 1.3 collective-permute-start.12
  55.6 1.3 collective-permute-start.14
  57.1 4.0 %collective-permute-start.16 = (f32[1024,128]{1,0:T(8,128)S(1)}, f32[1024,128]{1,0:T(8,128)S(1)}, u32[]{:S(2)}, u32[]{:S(2)}) collective-permute-start(f32[1024,128]{1,0:T(8,128)S(1)} %select_select_fusion.4.mine_ref), channel_id=1, source_target_pairs={{0,1},{1,0},{2,3},{3,2},{4,5},{5,4},{6,7},{7,6},{8,9},{9,8},{10,11... | collective-permute-start | bytes 1572872 | tf_op jit(solution)/shard_map/ppermute | solution.py:404
  61.1 4.6 %shard_map.18 = (f32[256,256]{1,0:T(8,128)S(1)}, bf16[256,768]{1,0:T(8,128)(2,1)S(1)}, bf16[768,256]{1,0:T(8,128)(2,1)S(1)}) custom-call(f32[128,128]{1,0:T(8,128)S(1)} %get-tuple-element.44.upper_ref, f32[128,128]{1,0:T(8,128)S(1)} %get-tuple-element.45.inv_0_ref, f32[128,128]{1,0:T(8,128)S(1)} %get-tuple-element.46.low_10_ref, ...), custom_call_target="tpu_custom_call" | custom-call | flops 20000000 | bytes 1048576 | tf_op jit(solution)/shard_map/pallas_call | solution.py:149
  66.1 1.1 slice_select_fusion
  67.2 1.5 %collective-permute-start.15 = (f32[1024,128]{1,0:T(8,128)S(1)}, f32[1024,128]{1,0:T(8,128)S(1)}, u32[]{:S(2)}, u32[]{:S(2)}) collective-permute-start(f32[1024,128]{1,0:T(8,128)S(1)} %slice_select_fusion), channel_id=1, source_target_pairs={{0,2},{1,3},{2,4},{3,5},{4,6},{5,7},{8,10},{9,11},{10,12},{11,13},... | collective-permute-start | bytes 1572872 | tf_op jit(solution)/shard_map/ppermute | solution.py:397
  68.9 4.6 %collective-permute-start.18 = (f32[1024,128]{1,0:T(8,128)S(1)}, f32[1024,128]{1,0:T(8,128)S(1)}, u32[]{:S(2)}, u32[]{:S(2)}) collective-permute-start(f32[1024,128]{1,0:T(8,128)S(1)} %select_select_fusion.3.mine_ref), channel_id=1, source_target_pairs={{0,1},{1,0},{2,3},{3,2},{4,5},{5,4},{6,7},{7,6},{8,9},{9,8},{10,11... | collective-permute-start | bytes 1572872 | tf_op jit(solution)/shard_map/ppermute | solution.py:404
  74.2 1.9 %shard_map.19.right_ref = bf16[768,2560]{1,0:T(8,128)(2,1)S(1)} custom-call(s32[4]{0:T(128)S(1)} %pad_add_fusion.info_ref, bf16[256,768]{1,0:T(8,128)(2,1)S(1)} %get-tuple-element.53.inv_ref, f32[128,1280]{1,0:T(8,128)S(1)} %broadcast_select_fusion.1.refs_0_, f32[128,1280]{1,0:T(8,128)S(1)} %collective-permute-done.13.refs_1_, ...), custom_call_target="tpu_custom_call" | custom-call | flops 1006632960 | bytes 5242880 | tf_op jit(solution)/shard_map/pallas_call | solution.py:180
  76.1 10.2 %shard_map.20.refs_0_ = f32[5120,2560]{1,0:T(8,128)} custom-call(s32[4]{0:T(128)S(1)} %pad_add_fusion.info_ref, f32[5120,2560]{1,0:T(8,128)} %mat_ref.9, bf16[768,2560]{1,0:T(8,128)(2,1)S(1)} %shard_map.19.right_ref, f32[256,256]{1,0:T(8,128)S(1)} %get-tuple-element.54.lower_ref, bf16[768,256]{1,0:T(8,128)(2,1)S(1)} %get-tuple-element.55.inv_t_ref, ...), custom_call_target="tpu_custom_call" | custom-call | flops 4026531840 | bytes 20971520 | tf_op jit(solution)/shard_map/pallas_call | solution.py:299
  86.3 1.3 collective-permute-start.17
  87.8 1.7 %collective-permute-start.20 = (f32[1024,128]{1,0:T(8,128)S(1)}, f32[1024,128]{1,0:T(8,128)S(1)}, u32[]{:S(2)}, u32[]{:S(2)}) collective-permute-start(f32[1024,128]{1,0:T(8,128)S(1)} %select_select_fusion.2.mine_ref), channel_id=1, source_target_pairs={{0,1},{1,0},{2,3},{3,2},{4,5},{5,4},{6,7},{7,6},{8,9},{9,8},{10,11... | collective-permute-start | bytes 1572872 | tf_op jit(solution)/shard_map/ppermute | solution.py:404
  89.5 10.2 %shard_map.21.refs_0_ = f32[5120,2560]{1,0:T(8,128)} custom-call(s32[4]{0:T(128)S(1)} %pad_add_fusion.info_ref, f32[5120,2560]{1,0:T(8,128)} %mat_ref.9, bf16[768,2560]{1,0:T(8,128)(2,1)S(1)} %shard_map.19.right_ref, f32[256,256]{1,0:T(8,128)S(1)} %get-tuple-element.54.lower_ref, ...), custom_call_target="tpu_custom_call", output_to_operand_aliasing={{}: (7, {})} | custom-call | flops 4026531840 | bytes 20971520 | tf_op jit(solution)/shard_map/pallas_call | solution.py:299
  99.7 1.6 %collective-permute-done.17 = f32[1024,128]{1,0:T(8,128)S(1)} collective-permute-done((f32[1024,128]{1,0:T(8,128)S(1)}, f32[1024,128]{1,0:T(8,128)S(1)}, u32[]{:S(2)}, u32[]{:S(2)}) %collective-permute-start.17) | collective-permute-done | bytes 524320 | tf_op jit(solution)/shard_map/ppermute | solution.py:397
  101.2 1.3 collective-permute-start.19
  102.6 2.3 %collective-permute-start.22 = (f32[1024,128]{1,0:T(8,128)S(1)}, f32[1024,128]{1,0:T(8,128)S(1)}, u32[]{:S(2)}, u32[]{:S(2)}) collective-permute-start(f32[1024,128]{1,0:T(8,128)S(1)} %select_select_fusion.1.mine_ref), channel_id=1, source_target_pairs={{0,1},{1,0},{2,3},{3,2},{4,5},{5,4},{6,7},{7,6},{8,9},{9,8},{10,11... | collective-permute-start | bytes 1572872 | tf_op jit(solution)/shard_map/ppermute | solution.py:404
  105.0 10.2 %shard_map.22.refs_0_ = f32[5120,2560]{1,0:T(8,128)} custom-call(s32[4]{0:T(128)S(1)} %pad_add_fusion.info_ref, f32[5120,2560]{1,0:T(8,128)} %mat_ref.9, bf16[768,2560]{1,0:T(8,128)(2,1)S(1)} %shard_map.19.right_ref, f32[256,256]{1,0:T(8,128)S(1)} %get-tuple-element.54.lower_ref, ...), custom_call_target="tpu_custom_call", output_to_operand_aliasing={{}: (7, {})} | custom-call | flops 4026531840 | bytes 20971520 | tf_op jit(solution)/shard_map/pallas_call | solution.py:299
  115.2 2.4 %collective-permute-start.21 = (f32[1024,128]{1,0:T(8,128)S(1)}, f32[1024,128]{1,0:T(8,128)S(1)}, u32[]{:S(2)}, u32[]{:S(2)}) collective-permute-start(f32[1024,128]{1,0:T(8,128)S(1)} %select_select_fusion.mine_ref), channel_id=1, source_target_pairs={{0,1},{1,0},{2,3},{3,2},{4,5},{5,4},{6,7},{7,6},{8,9},{9,8},{10,11... | collective-permute-start | bytes 1572872 | tf_op jit(solution)/shard_map/ppermute | solution.py:404
  117.6 10.2 %shard_map.23.refs_0_ = f32[5120,2560]{1,0:T(8,128)} custom-call(s32[4]{0:T(128)S(1)} %pad_add_fusion.info_ref, f32[5120,2560]{1,0:T(8,128)} %mat_ref.9, bf16[768,2560]{1,0:T(8,128)(2,1)S(1)} %shard_map.19.right_ref, f32[256,256]{1,0:T(8,128)S(1)} %get-tuple-element.54.lower_ref, ...), custom_call_target="tpu_custom_call", output_to_operand_aliasing={{}: (7, {})} | custom-call | flops 4026531840 | bytes 20971520 | tf_op jit(solution)/shard_map/pallas_call | solution.py:299
  127.8 10.2 %shard_map.24 = f32[5120,2560]{1,0:T(8,128)} custom-call(s32[4]{0:T(128)S(1)} %pad_add_fusion.info_ref, f32[5120,2560]{1,0:T(8,128)} %mat_ref.9, bf16[768,2560]{1,0:T(8,128)(2,1)S(1)} %shard_map.19.right_ref, f32[256,256]{1,0:T(8,128)S(1)} %get-tuple-element.54.lower_ref, ...), custom_call_target="tpu_custom_call", output_to_operand_aliasing={{}: (7, {})} | custom-call | flops 4026531840 | bytes 20971520 | tf_op jit(solution)/shard_map/pallas_call | solution.py:299
  (42 shorter events, 10.1 us)
Async XLA Ops:
  1.1 3.7 %collective-permute-start.3 = (f32[1024,128]{1,0:T(8,128)S(1)}, f32[1024,128]{1,0:T(8,128)S(1)}, u32[]{:S(2)}, u32[]{:S(2)}) collective-permute-start(f32[1024,128]{1,0:T(8,128)S(1)} %slice.25), channel_id=1, source_target_pairs={{0,2},{1,3},{8,10},{9,11},{16,18},{17,19},{24,26},{25,27}} | collective-permute-start | bytes 1572872 | tf_op jit(solution)/shard_map/ppermute | solution.py:397
  2.6 2.1 %collective-permute-start.2 = (f32[128,128]{1,0:T(8,128)S(1)}, f32[128,128]{1,0:T(8,128)S(1)}, u32[]{:S(2)}, u32[]{:S(2)}) collective-permute-start(f32[128,128]{1,0:T(8,128)S(1)} %slice.24), channel_id=1, source_target_pairs={{0,8},{1,9},{8,16},{9,17}} | collective-permute-start | bytes 196616 | tf_op jit(solution)/shard_map/ppermute | solution.py:355
  3.3 1.4 %collective-permute-start.1 = (f32[128,128]{1,0:T(8,128)S(1)}, f32[128,128]{1,0:T(8,128)S(1)}, u32[]{:S(2)}, u32[]{:S(2)}) collective-permute-start(f32[128,128]{1,0:T(8,128)S(1)} %slice.24), channel_id=1, source_target_pairs={{0,16},{1,17},{8,24},{9,25}} | collective-permute-start | bytes 196616 | tf_op jit(solution)/shard_map/ppermute | solution.py:355
  4.0 0.8 collective-permute-start
  5.9 33.3 %collective-permute-start.9 = (f32[1024,128]{1,0:T(8,128)S(1)}, f32[1024,128]{1,0:T(8,128)S(1)}, u32[]{:S(2)}, u32[]{:S(2)}) collective-permute-start(f32[1024,128]{1,0:T(8,128)S(1)} %slice_select_fusion.3), channel_id=1, source_target_pairs={{0,2},{1,3},{2,4},{3,5},{8,10},{9,11},{10,12},{11,13},{16,18},{17,... | collective-permute-start | bytes 1572872 | tf_op jit(solution)/shard_map/ppermute | solution.py:397
  8.0 33.7 %collective-permute-start.7 = (f32[128,1280]{1,0:T(8,128)S(1)}, f32[128,1280]{1,0:T(8,128)}, u32[]{:S(2)}, u32[]{:S(2)}) collective-permute-start(f32[128,1280]{1,0:T(8,128)S(1)} %get-tuple-element.39), channel_id=1, source_target_pairs={{0,16},{8,24},{1,17},{9,25},{2,18},{10,26},{3,19},{11,27},{4,20},{... | collective-permute-start | bytes 1966088 | tf_op jit(solution)/shard_map/ppermute | solution.py:330
  12.0 2.7 %collective-permute-start.6 = (f32[256,128]{1,0:T(8,128)S(1)}, f32[256,128]{1,0:T(8,128)S(1)}, u32[]{:S(2)}, u32[]{:S(2)}) collective-permute-start(f32[256,128]{1,0:T(8,128)S(1)} %pad_maximum_fusion.1), channel_id=1, source_target_pairs={{0,2},{1,3},{8,10},{9,11},{16,18},{17,19},{24,26},{25,27}} | collective-permute-start | bytes 393224 | tf_op jit(solution)/shard_map/ppermute | solution.py:363
  12.7 4.2 %collective-permute-start.5 = (f32[256,128]{1,0:T(8,128)S(1)}, f32[256,128]{1,0:T(8,128)S(1)}, u32[]{:S(2)}, u32[]{:S(2)}) collective-permute-start(f32[256,128]{1,0:T(8,128)S(1)} %pad_maximum_fusion.1), channel_id=1, source_target_pairs={{0,4},{1,5},{8,12},{9,13},{16,20},{17,21},{24,28},{25,29}} | collective-permute-start | bytes 393224 | tf_op jit(solution)/shard_map/ppermute | solution.py:363
  13.3 25.2 %collective-permute-start.4 = (f32[256,128]{1,0:T(8,128)S(1)}, f32[256,128]{1,0:T(8,128)S(1)}, u32[]{:S(2)}, u32[]{:S(2)}) collective-permute-start(f32[256,128]{1,0:T(8,128)S(1)} %pad_maximum_fusion.1), channel_id=1, source_target_pairs={{0,6},{1,7},{8,14},{9,15},{16,22},{17,23},{24,30},{25,31}} | collective-permute-start | bytes 393224 | tf_op jit(solution)/shard_map/ppermute | solution.py:363
  14.7 37.5 %collective-permute-start.11 = (f32[128,1280]{1,0:T(8,128)S(1)}, f32[128,1280]{1,0:T(8,128)}, u32[]{:S(2)}, u32[]{:S(2)}) collective-permute-start(f32[128,1280]{1,0:T(8,128)S(1)} %get-tuple-element.40), channel_id=1, source_target_pairs={{0,16},{8,24},{1,17},{9,25},{2,18},{10,26},{3,19},{11,27},{4,20},{... | collective-permute-start | bytes 1966088 | tf_op jit(solution)/shard_map/ppermute | solution.py:330
  40.3 12.7 %collective-permute-start.10 = (f32[1024,128]{1,0:T(8,128)S(1)}, f32[1024,128]{1,0:T(8,128)}, u32[]{:S(2)}, u32[]{:S(2)}) collective-permute-start(f32[1024,128]{1,0:T(8,128)S(1)} %slice_select_fusion.2), channel_id=1, source_target_pairs={{0,2},{1,3},{2,4},{3,5},{4,6},{5,7},{8,10},{9,11},{10,12},{11,13},... | collective-permute-start | bytes 1572872 | tf_op jit(solution)/shard_map/ppermute | solution.py:397
  41.7 4.1 %collective-permute-start.8 = (f32[256,128]{1,0:T(8,128)}, f32[256,128]{1,0:T(8,128)S(1)}, u32[]{:S(2)}, u32[]{:S(2)}) collective-permute-start(f32[256,128]{1,0:T(8,128)} %select_select_fusion.5), channel_id=1, source_target_pairs={{0,1},{1,0},{2,3},{3,2},{4,5},{5,4},{6,7},{7,6},{8,9},{9,8},{10,11... | collective-permute-start | bytes 393224 | tf_op jit(solution)/shard_map/ppermute | solution.py:365
  44.6 22.6 %collective-permute-start.13 = (f32[128,1280]{1,0:T(8,128)S(1)}, f32[128,1280]{1,0:T(8,128)S(1)}, u32[]{:S(2)}, u32[]{:S(2)}) collective-permute-start(f32[128,1280]{1,0:T(8,128)S(1)} %broadcast_select_fusion.1.refs_0_), channel_id=1, source_target_pairs={{0,8},{8,0},{16,24},{24,16},{1,9},{9,1},{17,25},{25,17},{2,10},{10... | collective-permute-start | bytes 1966088 | tf_op jit(solution)/shard_map/ppermute | solution.py:337
  54.2 11.9 %collective-permute-start.12 = (f32[1024,128]{1,0:T(8,128)S(1)}, f32[1024,128]{1,0:T(8,128)S(1)}, u32[]{:S(2)}, u32[]{:S(2)}) collective-permute-start(f32[1024,128]{1,0:T(8,128)S(1)} %slice_select_fusion.1), channel_id=1, source_target_pairs={{0,2},{1,3},{2,4},{3,5},{4,6},{5,7},{8,10},{9,11},{10,12},{11,13},... | collective-permute-start | bytes 1572872 | tf_op jit(solution)/shard_map/ppermute | solution.py:397
  55.6 18.6 %collective-permute-start.14 = (f32[128,1280]{1,0:T(8,128)S(1)}, f32[128,1280]{1,0:T(8,128)S(1)}, u32[]{:S(2)}, u32[]{:S(2)}) collective-permute-start(f32[128,1280]{1,0:T(8,128)S(1)} %broadcast_select_fusion.refs_2_), channel_id=1, source_target_pairs={{0,8},{8,0},{16,24},{24,16},{1,9},{9,1},{17,25},{25,17},{2,10},{10... | collective-permute-start | bytes 1966088 | tf_op jit(solution)/shard_map/ppermute | solution.py:337
  57.1 16.4 %collective-permute-start.16 = (f32[1024,128]{1,0:T(8,128)S(1)}, f32[1024,128]{1,0:T(8,128)S(1)}, u32[]{:S(2)}, u32[]{:S(2)}) collective-permute-start(f32[1024,128]{1,0:T(8,128)S(1)} %select_select_fusion.4.mine_ref), channel_id=1, source_target_pairs={{0,1},{1,0},{2,3},{3,2},{4,5},{5,4},{6,7},{7,6},{8,9},{9,8},{10,11... | collective-permute-start | bytes 1572872 | tf_op jit(solution)/shard_map/ppermute | solution.py:404
  67.2 19.1 %collective-permute-start.15 = (f32[1024,128]{1,0:T(8,128)S(1)}, f32[1024,128]{1,0:T(8,128)S(1)}, u32[]{:S(2)}, u32[]{:S(2)}) collective-permute-start(f32[1024,128]{1,0:T(8,128)S(1)} %slice_select_fusion), channel_id=1, source_target_pairs={{0,2},{1,3},{2,4},{3,5},{4,6},{5,7},{8,10},{9,11},{10,12},{11,13},... | collective-permute-start | bytes 1572872 | tf_op jit(solution)/shard_map/ppermute | solution.py:397
  68.9 20.6 %collective-permute-start.18 = (f32[1024,128]{1,0:T(8,128)S(1)}, f32[1024,128]{1,0:T(8,128)S(1)}, u32[]{:S(2)}, u32[]{:S(2)}) collective-permute-start(f32[1024,128]{1,0:T(8,128)S(1)} %select_select_fusion.3.mine_ref), channel_id=1, source_target_pairs={{0,1},{1,0},{2,3},{3,2},{4,5},{5,4},{6,7},{7,6},{8,9},{9,8},{10,11... | collective-permute-start | bytes 1572872 | tf_op jit(solution)/shard_map/ppermute | solution.py:404
  86.3 14.9 %collective-permute-start.17 = (f32[1024,128]{1,0:T(8,128)S(1)}, f32[1024,128]{1,0:T(8,128)S(1)}, u32[]{:S(2)}, u32[]{:S(2)}) collective-permute-start(f32[1024,128]{1,0:T(8,128)S(1)} %collective-permute-done.15), channel_id=1, source_target_pairs={{2,4},{3,5},{4,6},{5,7},{10,12},{11,13},{12,14},{13,15},{18,20},{1... | collective-permute-start | bytes 1572872 | tf_op jit(solution)/shard_map/ppermute | solution.py:397
  87.8 17.2 %collective-permute-start.20 = (f32[1024,128]{1,0:T(8,128)S(1)}, f32[1024,128]{1,0:T(8,128)S(1)}, u32[]{:S(2)}, u32[]{:S(2)}) collective-permute-start(f32[1024,128]{1,0:T(8,128)S(1)} %select_select_fusion.2.mine_ref), channel_id=1, source_target_pairs={{0,1},{1,0},{2,3},{3,2},{4,5},{5,4},{6,7},{7,6},{8,9},{9,8},{10,11... | collective-permute-start | bytes 1572872 | tf_op jit(solution)/shard_map/ppermute | solution.py:404
  101.2 13.9 %collective-permute-start.19 = (f32[1024,128]{1,0:T(8,128)S(1)}, f32[1024,128]{1,0:T(8,128)S(1)}, u32[]{:S(2)}, u32[]{:S(2)}) collective-permute-start(f32[1024,128]{1,0:T(8,128)S(1)} %collective-permute-done.17), channel_id=1, source_target_pairs={{4,6},{5,7},{12,14},{13,15},{20,22},{21,23},{28,30},{29,31}} | collective-permute-start | bytes 1572872 | tf_op jit(solution)/shard_map/ppermute | solution.py:397
  102.6 15.0 %collective-permute-start.22 = (f32[1024,128]{1,0:T(8,128)S(1)}, f32[1024,128]{1,0:T(8,128)S(1)}, u32[]{:S(2)}, u32[]{:S(2)}) collective-permute-start(f32[1024,128]{1,0:T(8,128)S(1)} %select_select_fusion.1.mine_ref), channel_id=1, source_target_pairs={{0,1},{1,0},{2,3},{3,2},{4,5},{5,4},{6,7},{7,6},{8,9},{9,8},{10,11... | collective-permute-start | bytes 1572872 | tf_op jit(solution)/shard_map/ppermute | solution.py:404
  115.2 12.6 %collective-permute-start.21 = (f32[1024,128]{1,0:T(8,128)S(1)}, f32[1024,128]{1,0:T(8,128)S(1)}, u32[]{:S(2)}, u32[]{:S(2)}) collective-permute-start(f32[1024,128]{1,0:T(8,128)S(1)} %select_select_fusion.mine_ref), channel_id=1, source_target_pairs={{0,1},{1,0},{2,3},{3,2},{4,5},{5,4},{6,7},{7,6},{8,9},{9,8},{10,11... | collective-permute-start | bytes 1572872 | tf_op jit(solution)/shard_map/ppermute | solution.py:404

commit v9 on v8

--- a/solution.py
+++ b/solution.py
@@ -13,8 +13,8 @@
 CORES = 2
 VMEM_LIMIT = 40 * 1024 * 1024
 GROUP = 8
-IN_SLOTS = 3
-OUT_SLOTS = 2
+IN_SLOTS = 4
+OUT_SLOTS = 3
 PIECES = 4
 
 

time: 140 us -> 137 us (0.979)
  Pallas kernels: 62.7 us -> 58.2 us
    pallas_call x5, Pallas kernels: 50.8 us -> 46.3 us  [update_rows(): pl.pallas_call(functools.partial(update_kernel, start, block), in_specs=i...]
  transfers between devices with their start and end apart: 23 -> 23, of which waited for: 5 -> 6; matrix products, arithmetic and copies ran while one was open for 6% -> 6% of each run, Pallas kernels for 38% -> 36%
where the time goes in v9:
time: 137 us; the launch traced here: 135 us
  Pallas kernels  58.2 us (42%)
  starting transfers between devices  40 us (29%)
  waiting for transfers between devices  26.3 us (19%)
  other arithmetic  7.14 us (5%)
  local copies, waits for them, and re-layouts  3.3 us (2%)
    pallas_call x5, Pallas kernels, update_rows(): pl.pallas_call(functools.partial(update_kernel, start, block), in_specs=i...  46.3 us
    ppermute x3, waiting for transfers between devices, share_corner(): got.append(lax.ppermute(column, 'col', pairs))  21.7 us
    ppermute x5, starting transfers between devices, exchange(): ready.append((mine, lax.ppermute(mine, 'col', swap)))  15.9 us
    ppermute x7, starting transfers between devices, fill(): return lax.ppermute(held[-1], 'col', hops) if slot < last else None  8.02 us
    ppermute x2, starting transfers between devices, double_rows(): got = after(lax.ppermute(block, 'row', pairs), *earlier)  6.17 us
    pallas_call x1, Pallas kernels, factor_first(): pl.pallas_call(first_kernel, out_shape=(tile,) * 4, compiler_params=pltpu...  5.34 us
    pallas_call x1, Pallas kernels, factor_second(): pl.pallas_call(second_kernel, out_shape=(jax.ShapeDtypeStruct((WIDE, WIDE...  4.63 us
    select_n x4, other arithmetic, fill(): block = own if got is None else jnp.where(place == 0, own, got)  4.56 us
  transfers between devices with their start and end apart: 23, of which 6 were waited for; matrix products, arithmetic and copies ran while one was open for 6% of the time, Pallas kernels for 36%

profile of v9, /device:TPU:25, one launch (start us, length us, event | category | flops | bytes accessed | tf_op | source)
XLA Modules:
  0.0 135.4 jit_solution(4038008083045315799)
XLA Ops:
  0.0 1.1 slice.25
  4.8 1.1 slice_select_fusion.3
  6.6 1.4 %fusion = (f32[128,1280]{1,0:T(8,128)S(1)}, f32[128,1280]{1,0:T(8,128)S(1)}) fusion(f32[5120,2560]{1,0:T(8,128)} %mat_ref.9), kind=kLoop, calls=%fused_computation.19 | loop fusion | bytes 2621440 | tf_op jit(solution)/shard_map/slice | solution.py:411
  8.0 4.0 %collective-permute-start.7 = (f32[128,1280]{1,0:T(8,128)S(1)}, f32[128,1280]{1,0:T(8,128)}, u32[]{:S(2)}, u32[]{:S(2)}) collective-permute-start(f32[128,1280]{1,0:T(8,128)S(1)} %get-tuple-element.39), channel_id=1, source_target_pairs={{0,16},{8,24},{1,17},{9,25},{2,18},{10,26},{3,19},{11,27},{4,20},{... | collective-permute-start | bytes 1966088 | tf_op jit(solution)/shard_map/ppermute | solution.py:330
  13.3 1.3 collective-permute-start.4
  14.7 2.1 %collective-permute-start.11 = (f32[128,1280]{1,0:T(8,128)S(1)}, f32[128,1280]{1,0:T(8,128)}, u32[]{:S(2)}, u32[]{:S(2)}) collective-permute-start(f32[128,1280]{1,0:T(8,128)S(1)} %get-tuple-element.40), channel_id=1, source_target_pairs={{0,16},{8,24},{1,17},{9,25},{2,18},{10,26},{3,19},{11,27},{4,20},{... | collective-permute-start | bytes 1966088 | tf_op jit(solution)/shard_map/ppermute | solution.py:330
  16.8 21.7 %collective-permute-done.4 = f32[256,128]{1,0:T(8,128)S(1)} collective-permute-done((f32[256,128]{1,0:T(8,128)S(1)}, f32[256,128]{1,0:T(8,128)S(1)}, u32[]{:S(2)}, u32[]{:S(2)}) %collective-permute-start.4) | collective-permute-done | bytes 131104 | tf_op jit(solution)/shard_map/ppermute | solution.py:363
  39.2 1.1 slice_select_fusion.2
  40.3 1.3 collective-permute-start.10
  41.7 2.8 %collective-permute-start.8 = (f32[256,128]{1,0:T(8,128)}, f32[256,128]{1,0:T(8,128)S(1)}, u32[]{:S(2)}, u32[]{:S(2)}) collective-permute-start(f32[256,128]{1,0:T(8,128)} %select_select_fusion.5), channel_id=1, source_target_pairs={{0,1},{1,0},{2,3},{3,2},{4,5},{5,4},{6,7},{7,6},{8,9},{9,8},{10,11... | collective-permute-start | bytes 393224 | tf_op jit(solution)/shard_map/ppermute | solution.py:365
  44.6 1.2 collective-permute-start.13
  46.8 5.3 %shard_map.17 = (f32[128,128]{1,0:T(8,128)S(1)}, f32[128,128]{1,0:T(8,128)S(1)}, f32[128,128]{1,0:T(8,128)S(1)}, f32[128,128]{1,0:T(8,128)S(1)}) custom-call(f32[256,256]{1,0:T(8,128)S(1)} %pad_maximum_fusion.corner_ref), custom_call_target="tpu_custom_call" | custom-call | flops 20000000 | bytes 524288 | tf_op jit(solution)/shard_map/pallas_call | solution.py:140
  53.0 1.3 slice_select_fusion.1
  54.2 1.3 collective-permute-start.12
  55.6 1.3 collective-permute-start.14
  57.1 4.0 %collective-permute-start.16 = (f32[1024,128]{1,0:T(8,128)S(1)}, f32[1024,128]{1,0:T(8,128)S(1)}, u32[]{:S(2)}, u32[]{:S(2)}) collective-permute-start(f32[1024,128]{1,0:T(8,128)S(1)} %select_select_fusion.4.mine_ref), channel_id=1, source_target_pairs={{0,1},{1,0},{2,3},{3,2},{4,5},{5,4},{6,7},{7,6},{8,9},{9,8},{10,11... | collective-permute-start | bytes 1572872 | tf_op jit(solution)/shard_map/ppermute | solution.py:404
  61.1 4.6 %shard_map.18 = (f32[256,256]{1,0:T(8,128)S(1)}, bf16[256,768]{1,0:T(8,128)(2,1)S(1)}, bf16[768,256]{1,0:T(8,128)(2,1)S(1)}) custom-call(f32[128,128]{1,0:T(8,128)S(1)} %get-tuple-element.44.upper_ref, f32[128,128]{1,0:T(8,128)S(1)} %get-tuple-element.45.inv_0_ref, f32[128,128]{1,0:T(8,128)S(1)} %get-tuple-element.46.low_10_ref, ...), custom_call_target="tpu_custom_call" | custom-call | flops 20000000 | bytes 1048576 | tf_op jit(solution)/shard_map/pallas_call | solution.py:149
  66.1 1.1 slice_select_fusion
  67.2 1.5 %collective-permute-start.15 = (f32[1024,128]{1,0:T(8,128)S(1)}, f32[1024,128]{1,0:T(8,128)S(1)}, u32[]{:S(2)}, u32[]{:S(2)}) collective-permute-start(f32[1024,128]{1,0:T(8,128)S(1)} %slice_select_fusion), channel_id=1, source_target_pairs={{0,2},{1,3},{2,4},{3,5},{4,6},{5,7},{8,10},{9,11},{10,12},{11,13},... | collective-permute-start | bytes 1572872 | tf_op jit(solution)/shard_map/ppermute | solution.py:397
  68.9 4.6 %collective-permute-start.18 = (f32[1024,128]{1,0:T(8,128)S(1)}, f32[1024,128]{1,0:T(8,128)S(1)}, u32[]{:S(2)}, u32[]{:S(2)}) collective-permute-start(f32[1024,128]{1,0:T(8,128)S(1)} %select_select_fusion.3.mine_ref), channel_id=1, source_target_pairs={{0,1},{1,0},{2,3},{3,2},{4,5},{5,4},{6,7},{7,6},{8,9},{9,8},{10,11... | collective-permute-start | bytes 1572872 | tf_op jit(solution)/shard_map/ppermute | solution.py:404
  74.2 1.9 %shard_map.19.right_ref = bf16[768,2560]{1,0:T(8,128)(2,1)S(1)} custom-call(s32[4]{0:T(128)S(1)} %pad_add_fusion.info_ref, bf16[256,768]{1,0:T(8,128)(2,1)S(1)} %get-tuple-element.53.inv_ref, f32[128,1280]{1,0:T(8,128)S(1)} %broadcast_select_fusion.1.refs_0_, f32[128,1280]{1,0:T(8,128)S(1)} %collective-permute-done.13.refs_1_, ...), custom_call_target="tpu_custom_call" | custom-call | flops 1006632960 | bytes 5242880 | tf_op jit(solution)/shard_map/pallas_call | solution.py:180
  76.1 9.3 %shard_map.20.refs_0_ = f32[5120,2560]{1,0:T(8,128)} custom-call(s32[4]{0:T(128)S(1)} %pad_add_fusion.info_ref, f32[5120,2560]{1,0:T(8,128)} %mat_ref.9, bf16[768,2560]{1,0:T(8,128)(2,1)S(1)} %shard_map.19.right_ref, f32[256,256]{1,0:T(8,128)S(1)} %get-tuple-element.54.lower_ref, bf16[768,256]{1,0:T(8,128)(2,1)S(1)} %get-tuple-element.55.inv_t_ref, ...), custom_call_target="tpu_custom_call" | custom-call | flops 4026531840 | bytes 20971520 | tf_op jit(solution)/shard_map/pallas_call | solution.py:299
  85.5 1.3 collective-permute-start.17
  86.9 1.7 %collective-permute-start.20 = (f32[1024,128]{1,0:T(8,128)S(1)}, f32[1024,128]{1,0:T(8,128)S(1)}, u32[]{:S(2)}, u32[]{:S(2)}) collective-permute-start(f32[1024,128]{1,0:T(8,128)S(1)} %select_select_fusion.2.mine_ref), channel_id=1, source_target_pairs={{0,1},{1,0},{2,3},{3,2},{4,5},{5,4},{6,7},{7,6},{8,9},{9,8},{10,11... | collective-permute-start | bytes 1572872 | tf_op jit(solution)/shard_map/ppermute | solution.py:404
  88.6 9.2 %shard_map.21.refs_0_ = f32[5120,2560]{1,0:T(8,128)} custom-call(s32[4]{0:T(128)S(1)} %pad_add_fusion.info_ref, f32[5120,2560]{1,0:T(8,128)} %mat_ref.9, bf16[768,2560]{1,0:T(8,128)(2,1)S(1)} %shard_map.19.right_ref, f32[256,256]{1,0:T(8,128)S(1)} %get-tuple-element.54.lower_ref, ...), custom_call_target="tpu_custom_call", output_to_operand_aliasing={{}: (7, {})} | custom-call | flops 4026531840 | bytes 20971520 | tf_op jit(solution)/shard_map/pallas_call | solution.py:299
  97.9 2.5 %collective-permute-done.17 = f32[1024,128]{1,0:T(8,128)S(1)} collective-permute-done((f32[1024,128]{1,0:T(8,128)S(1)}, f32[1024,128]{1,0:T(8,128)S(1)}, u32[]{:S(2)}, u32[]{:S(2)}) %collective-permute-start.17) | collective-permute-done | bytes 524320 | tf_op jit(solution)/shard_map/ppermute | solution.py:397
  100.4 1.3 collective-permute-start.19
  101.8 2.3 %collective-permute-start.22 = (f32[1024,128]{1,0:T(8,128)S(1)}, f32[1024,128]{1,0:T(8,128)S(1)}, u32[]{:S(2)}, u32[]{:S(2)}) collective-permute-start(f32[1024,128]{1,0:T(8,128)S(1)} %select_select_fusion.1.mine_ref), channel_id=1, source_target_pairs={{0,1},{1,0},{2,3},{3,2},{4,5},{5,4},{6,7},{7,6},{8,9},{9,8},{10,11... | collective-permute-start | bytes 1572872 | tf_op jit(solution)/shard_map/ppermute | solution.py:404
  104.1 9.2 %shard_map.22.refs_0_ = f32[5120,2560]{1,0:T(8,128)} custom-call(s32[4]{0:T(128)S(1)} %pad_add_fusion.info_ref, f32[5120,2560]{1,0:T(8,128)} %mat_ref.9, bf16[768,2560]{1,0:T(8,128)(2,1)S(1)} %shard_map.19.right_ref, f32[256,256]{1,0:T(8,128)S(1)} %get-tuple-element.54.lower_ref, ...), custom_call_target="tpu_custom_call", output_to_operand_aliasing={{}: (7, {})} | custom-call | flops 4026531840 | bytes 20971520 | tf_op jit(solution)/shard_map/pallas_call | solution.py:299
  113.5 3.3 %collective-permute-start.21 = (f32[1024,128]{1,0:T(8,128)S(1)}, f32[1024,128]{1,0:T(8,128)S(1)}, u32[]{:S(2)}, u32[]{:S(2)}) collective-permute-start(f32[1024,128]{1,0:T(8,128)S(1)} %select_select_fusion.mine_ref), channel_id=1, source_target_pairs={{0,1},{1,0},{2,3},{3,2},{4,5},{5,4},{6,7},{7,6},{8,9},{9,8},{10,11... | collective-permute-start | bytes 1572872 | tf_op jit(solution)/shard_map/ppermute | solution.py:404
  116.7 9.2 %shard_map.23.refs_0_ = f32[5120,2560]{1,0:T(8,128)} custom-call(s32[4]{0:T(128)S(1)} %pad_add_fusion.info_ref, f32[5120,2560]{1,0:T(8,128)} %mat_ref.9, bf16[768,2560]{1,0:T(8,128)(2,1)S(1)} %shard_map.19.right_ref, f32[256,256]{1,0:T(8,128)S(1)} %get-tuple-element.54.lower_ref, ...), custom_call_target="tpu_custom_call", output_to_operand_aliasing={{}: (7, {})} | custom-call | flops 4026531840 | bytes 20971520 | tf_op jit(solution)/shard_map/pallas_call | solution.py:299
  126.0 9.2 %shard_map.24 = f32[5120,2560]{1,0:T(8,128)} custom-call(s32[4]{0:T(128)S(1)} %pad_add_fusion.info_ref, f32[5120,2560]{1,0:T(8,128)} %mat_ref.9, bf16[768,2560]{1,0:T(8,128)(2,1)S(1)} %shard_map.19.right_ref, f32[256,256]{1,0:T(8,128)S(1)} %get-tuple-element.54.lower_ref, ...), custom_call_target="tpu_custom_call", output_to_operand_aliasing={{}: (7, {})} | custom-call | flops 4026531840 | bytes 20971520 | tf_op jit(solution)/shard_map/pallas_call | solution.py:299
  (42 shorter events, 10.2 us)
Async XLA Ops:
  1.1 3.7 %collective-permute-start.3 = (f32[1024,128]{1,0:T(8,128)S(1)}, f32[1024,128]{1,0:T(8,128)S(1)}, u32[]{:S(2)}, u32[]{:S(2)}) collective-permute-start(f32[1024,128]{1,0:T(8,128)S(1)} %slice.25), channel_id=1, source_target_pairs={{0,2},{1,3},{8,10},{9,11},{16,18},{17,19},{24,26},{25,27}} | collective-permute-start | bytes 1572872 | tf_op jit(solution)/shard_map/ppermute | solution.py:397
  2.6 2.1 %collective-permute-start.2 = (f32[128,128]{1,0:T(8,128)S(1)}, f32[128,128]{1,0:T(8,128)S(1)}, u32[]{:S(2)}, u32[]{:S(2)}) collective-permute-start(f32[128,128]{1,0:T(8,128)S(1)} %slice.24), channel_id=1, source_target_pairs={{0,8},{1,9},{8,16},{9,17}} | collective-permute-start | bytes 196616 | tf_op jit(solution)/shard_map/ppermute | solution.py:355
  3.3 1.4 %collective-permute-start.1 = (f32[128,128]{1,0:T(8,128)S(1)}, f32[128,128]{1,0:T(8,128)S(1)}, u32[]{:S(2)}, u32[]{:S(2)}) collective-permute-start(f32[128,128]{1,0:T(8,128)S(1)} %slice.24), channel_id=1, source_target_pairs={{0,16},{1,17},{8,24},{9,25}} | collective-permute-start | bytes 196616 | tf_op jit(solution)/shard_map/ppermute | solution.py:355
  4.0 0.8 collective-permute-start
  5.9 33.3 %collective-permute-start.9 = (f32[1024,128]{1,0:T(8,128)S(1)}, f32[1024,128]{1,0:T(8,128)S(1)}, u32[]{:S(2)}, u32[]{:S(2)}) collective-permute-start(f32[1024,128]{1,0:T(8,128)S(1)} %slice_select_fusion.3), channel_id=1, source_target_pairs={{0,2},{1,3},{2,4},{3,5},{8,10},{9,11},{10,12},{11,13},{16,18},{17,... | collective-permute-start | bytes 1572872 | tf_op jit(solution)/shard_map/ppermute | solution.py:397
  8.0 33.7 %collective-permute-start.7 = (f32[128,1280]{1,0:T(8,128)S(1)}, f32[128,1280]{1,0:T(8,128)}, u32[]{:S(2)}, u32[]{:S(2)}) collective-permute-start(f32[128,1280]{1,0:T(8,128)S(1)} %get-tuple-element.39), channel_id=1, source_target_pairs={{0,16},{8,24},{1,17},{9,25},{2,18},{10,26},{3,19},{11,27},{4,20},{... | collective-permute-start | bytes 1966088 | tf_op jit(solution)/shard_map/ppermute | solution.py:330
  12.0 2.7 %collective-permute-start.6 = (f32[256,128]{1,0:T(8,128)S(1)}, f32[256,128]{1,0:T(8,128)S(1)}, u32[]{:S(2)}, u32[]{:S(2)}) collective-permute-start(f32[256,128]{1,0:T(8,128)S(1)} %pad_maximum_fusion.1), channel_id=1, source_target_pairs={{0,2},{1,3},{8,10},{9,11},{16,18},{17,19},{24,26},{25,27}} | collective-permute-start | bytes 393224 | tf_op jit(solution)/shard_map/ppermute | solution.py:363
  12.7 4.2 %collective-permute-start.5 = (f32[256,128]{1,0:T(8,128)S(1)}, f32[256,128]{1,0:T(8,128)S(1)}, u32[]{:S(2)}, u32[]{:S(2)}) collective-permute-start(f32[256,128]{1,0:T(8,128)S(1)} %pad_maximum_fusion.1), channel_id=1, source_target_pairs={{0,4},{1,5},{8,12},{9,13},{16,20},{17,21},{24,28},{25,29}} | collective-permute-start | bytes 393224 | tf_op jit(solution)/shard_map/ppermute | solution.py:363
  13.3 25.2 %collective-permute-start.4 = (f32[256,128]{1,0:T(8,128)S(1)}, f32[256,128]{1,0:T(8,128)S(1)}, u32[]{:S(2)}, u32[]{:S(2)}) collective-permute-start(f32[256,128]{1,0:T(8,128)S(1)} %pad_maximum_fusion.1), channel_id=1, source_target_pairs={{0,6},{1,7},{8,14},{9,15},{16,22},{17,23},{24,30},{25,31}} | collective-permute-start | bytes 393224 | tf_op jit(solution)/shard_map/ppermute | solution.py:363
  14.7 37.5 %collective-permute-start.11 = (f32[128,1280]{1,0:T(8,128)S(1)}, f32[128,1280]{1,0:T(8,128)}, u32[]{:S(2)}, u32[]{:S(2)}) collective-permute-start(f32[128,1280]{1,0:T(8,128)S(1)} %get-tuple-element.40), channel_id=1, source_target_pairs={{0,16},{8,24},{1,17},{9,25},{2,18},{10,26},{3,19},{11,27},{4,20},{... | collective-permute-start | bytes 1966088 | tf_op jit(solution)/shard_map/ppermute | solution.py:330
  40.3 12.7 %collective-permute-start.10 = (f32[1024,128]{1,0:T(8,128)S(1)}, f32[1024,128]{1,0:T(8,128)}, u32[]{:S(2)}, u32[]{:S(2)}) collective-permute-start(f32[1024,128]{1,0:T(8,128)S(1)} %slice_select_fusion.2), channel_id=1, source_target_pairs={{0,2},{1,3},{2,4},{3,5},{4,6},{5,7},{8,10},{9,11},{10,12},{11,13},... | collective-permute-start | bytes 1572872 | tf_op jit(solution)/shard_map/ppermute | solution.py:397
  41.7 4.1 %collective-permute-start.8 = (f32[256,128]{1,0:T(8,128)}, f32[256,128]{1,0:T(8,128)S(1)}, u32[]{:S(2)}, u32[]{:S(2)}) collective-permute-start(f32[256,128]{1,0:T(8,128)} %select_select_fusion.5), channel_id=1, source_target_pairs={{0,1},{1,0},{2,3},{3,2},{4,5},{5,4},{6,7},{7,6},{8,9},{9,8},{10,11... | collective-permute-start | bytes 393224 | tf_op jit(solution)/shard_map/ppermute | solution.py:365
  44.6 22.6 %collective-permute-start.13 = (f32[128,1280]{1,0:T(8,128)S(1)}, f32[128,1280]{1,0:T(8,128)S(1)}, u32[]{:S(2)}, u32[]{:S(2)}) collective-permute-start(f32[128,1280]{1,0:T(8,128)S(1)} %broadcast_select_fusion.1.refs_0_), channel_id=1, source_target_pairs={{0,8},{8,0},{16,24},{24,16},{1,9},{9,1},{17,25},{25,17},{2,10},{10... | collective-permute-start | bytes 1966088 | tf_op jit(solution)/shard_map/ppermute | solution.py:337
  54.2 11.9 %collective-permute-start.12 = (f32[1024,128]{1,0:T(8,128)S(1)}, f32[1024,128]{1,0:T(8,128)S(1)}, u32[]{:S(2)}, u32[]{:S(2)}) collective-permute-start(f32[1024,128]{1,0:T(8,128)S(1)} %slice_select_fusion.1), channel_id=1, source_target_pairs={{0,2},{1,3},{2,4},{3,5},{4,6},{5,7},{8,10},{9,11},{10,12},{11,13},... | collective-permute-start | bytes 1572872 | tf_op jit(solution)/shard_map/ppermute | solution.py:397
  55.6 18.6 %collective-permute-start.14 = (f32[128,1280]{1,0:T(8,128)S(1)}, f32[128,1280]{1,0:T(8,128)S(1)}, u32[]{:S(2)}, u32[]{:S(2)}) collective-permute-start(f32[128,1280]{1,0:T(8,128)S(1)} %broadcast_select_fusion.refs_2_), channel_id=1, source_target_pairs={{0,8},{8,0},{16,24},{24,16},{1,9},{9,1},{17,25},{25,17},{2,10},{10... | collective-permute-start | bytes 1966088 | tf_op jit(solution)/shard_map/ppermute | solution.py:337
  57.1 16.4 %collective-permute-start.16 = (f32[1024,128]{1,0:T(8,128)S(1)}, f32[1024,128]{1,0:T(8,128)S(1)}, u32[]{:S(2)}, u32[]{:S(2)}) collective-permute-start(f32[1024,128]{1,0:T(8,128)S(1)} %select_select_fusion.4.mine_ref), channel_id=1, source_target_pairs={{0,1},{1,0},{2,3},{3,2},{4,5},{5,4},{6,7},{7,6},{8,9},{9,8},{10,11... | collective-permute-start | bytes 1572872 | tf_op jit(solution)/shard_map/ppermute | solution.py:404
  67.2 18.3 %collective-permute-start.15 = (f32[1024,128]{1,0:T(8,128)S(1)}, f32[1024,128]{1,0:T(8,128)S(1)}, u32[]{:S(2)}, u32[]{:S(2)}) collective-permute-start(f32[1024,128]{1,0:T(8,128)S(1)} %slice_select_fusion), channel_id=1, source_target_pairs={{0,2},{1,3},{2,4},{3,5},{4,6},{5,7},{8,10},{9,11},{10,12},{11,13},... | collective-permute-start | bytes 1572872 | tf_op jit(solution)/shard_map/ppermute | solution.py:397
  68.9 19.8 %collective-permute-start.18 = (f32[1024,128]{1,0:T(8,128)S(1)}, f32[1024,128]{1,0:T(8,128)S(1)}, u32[]{:S(2)}, u32[]{:S(2)}) collective-permute-start(f32[1024,128]{1,0:T(8,128)S(1)} %select_select_fusion.3.mine_ref), channel_id=1, source_target_pairs={{0,1},{1,0},{2,3},{3,2},{4,5},{5,4},{6,7},{7,6},{8,9},{9,8},{10,11... | collective-permute-start | bytes 1572872 | tf_op jit(solution)/shard_map/ppermute | solution.py:404
  85.5 14.9 %collective-permute-start.17 = (f32[1024,128]{1,0:T(8,128)S(1)}, f32[1024,128]{1,0:T(8,128)S(1)}, u32[]{:S(2)}, u32[]{:S(2)}) collective-permute-start(f32[1024,128]{1,0:T(8,128)S(1)} %collective-permute-done.15), channel_id=1, source_target_pairs={{2,4},{3,5},{4,6},{5,7},{10,12},{11,13},{12,14},{13,15},{18,20},{1... | collective-permute-start | bytes 1572872 | tf_op jit(solution)/shard_map/ppermute | solution.py:397
  86.9 17.2 %collective-permute-start.20 = (f32[1024,128]{1,0:T(8,128)S(1)}, f32[1024,128]{1,0:T(8,128)S(1)}, u32[]{:S(2)}, u32[]{:S(2)}) collective-permute-start(f32[1024,128]{1,0:T(8,128)S(1)} %select_select_fusion.2.mine_ref), channel_id=1, source_target_pairs={{0,1},{1,0},{2,3},{3,2},{4,5},{5,4},{6,7},{7,6},{8,9},{9,8},{10,11... | collective-permute-start | bytes 1572872 | tf_op jit(solution)/shard_map/ppermute | solution.py:404
  100.4 13.0 %collective-permute-start.19 = (f32[1024,128]{1,0:T(8,128)S(1)}, f32[1024,128]{1,0:T(8,128)S(1)}, u32[]{:S(2)}, u32[]{:S(2)}) collective-permute-start(f32[1024,128]{1,0:T(8,128)S(1)} %collective-permute-done.17), channel_id=1, source_target_pairs={{4,6},{5,7},{12,14},{13,15},{20,22},{21,23},{28,30},{29,31}} | collective-permute-start | bytes 1572872 | tf_op jit(solution)/shard_map/ppermute | solution.py:397
  101.8 15.0 %collective-permute-start.22 = (f32[1024,128]{1,0:T(8,128)S(1)}, f32[1024,128]{1,0:T(8,128)S(1)}, u32[]{:S(2)}, u32[]{:S(2)}) collective-permute-start(f32[1024,128]{1,0:T(8,128)S(1)} %select_select_fusion.1.mine_ref), channel_id=1, source_target_pairs={{0,1},{1,0},{2,3},{3,2},{4,5},{5,4},{6,7},{7,6},{8,9},{9,8},{10,11... | collective-permute-start | bytes 1572872 | tf_op jit(solution)/shard_map/ppermute | solution.py:404
  113.5 12.5 %collective-permute-start.21 = (f32[1024,128]{1,0:T(8,128)S(1)}, f32[1024,128]{1,0:T(8,128)S(1)}, u32[]{:S(2)}, u32[]{:S(2)}) collective-permute-start(f32[1024,128]{1,0:T(8,128)S(1)} %select_select_fusion.mine_ref), channel_id=1, source_target_pairs={{0,1},{1,0},{2,3},{3,2},{4,5},{5,4},{6,7},{7,6},{8,9},{9,8},{10,11... | collective-permute-start | bytes 1572872 | tf_op jit(solution)/shard_map/ppermute | solution.py:404
